TPU v7x, 512 devices: a whole 4x8x8 slice. The times are simulated.
512 devices in a mesh: gz: 16 (over z, core), ga: 32 (over y, x).
Axes of the slice: x: 4, y: 8, z: 8, core: 2. Of those that a mesh axis runs over, the one named last changes fastest.
Arguments:
- right_sides: float32 [16, 32, 32, 512], P('gz', 'ga'), may hold values from -6 to 6
- diag_inverse: float32 [16, 32, 512, 512], P('gz', 'ga'), as said below
- chain_block: float32 [16, 32, 512, 512], P('gz', 'ga')
- top_block: float32 [16, 32, 256, 512], P('gz', 'ga'), may hold values from -0.0234375 to 0.0234375
- top_rows: int32 [16, 32, 256], P('gz', 'ga'), may hold values from 0 to 1023, as said below
- live_cols: int32 [16, 32], P('gz', 'ga'), may hold values from 128 to 512, as said below
- top_right: float32 [32, 1024], replicated, may hold values from -6 to 6
- top_inverse: float32 [1024, 1024], P('ga'), as said below
Outputs:
- solution: float32 [16, 32, 32, 512], P('gz', 'ga')
- top_solution: float32 [32, 1024], replicated
Inputs may be any that keep to these rules, and one draw needn't show every extreme that they name: diag_inverse[g,k] and top_inverse are lower triangular. top_inverse is lower triangular. `top_rows`: the 256 entries of one chain supernode are distinct. `live_cols`: every entry is a multiple of 128; the last supernode of every chain (position 15) has all 512 columns live.
All inputs are finite; a program needn't handle non-finite values.
Results may differ from a plain program's by a relative error of at most 0.0003.
Values sent between devices are 32-bit elements; how exact they have to be, the bound alone decides.
No kernel may reach another device: no remote copies, remote signals or barrier semaphores. Data moves between devices by JAX's collectives and lax.ppermute only.
A program may use at most 128 MiB of HBM per device.

v0:
```python
import jax
import jax.numpy as jnp
from jax import lax
from jax.sharding import PartitionSpec as P

BRANCHES = 2


PRECISE = lax.Precision.HIGHEST


def shifted(block, axis, distance):
    devices = range(lax.axis_size(axis))
    route = [(i - distance, i) for i in devices if i - distance in devices]
    return lax.ppermute(block, axis, route)


def product(left, right_part):
    return jnp.dot(left, right_part, precision=PRECISE, preferred_element_type=jnp.float32)


def times_transposed(left, right_part):
    return lax.dot_general(
        left,
        right_part,
        (((1,), (1,)), ((), ())),
        precision=PRECISE,
        preferred_element_type=jnp.float32,
    )


def shards(
    right_sides, diag_inverse, chain_block, top_block, top_rows, live_cols, top_right, top_inverse
):
    chain_len = lax.axis_size("ga") // BRANCHES
    position = lax.axis_index("ga") % chain_len
    has_child = (position > 0).astype(jnp.float32)
    right_side = right_sides[0, 0]
    inverse = diag_inverse[0, 0]
    coupling = chain_block[0, 0]
    across = top_block[0, 0]
    rows_here = top_rows[0, 0]
    width_cols = right_side.shape[1]
    keep_mask = (lax.broadcasted_iota(jnp.int32, (1, width_cols), 1) < live_cols[0, 0]).astype(
        jnp.float32
    )
    own_term = keep_mask * times_transposed(right_side, inverse)

    def descend(step_index, current):
        prior_rows = shifted(current, "ga", 1)
        pushed = has_child * times_transposed(prior_rows, coupling)
        return keep_mask * times_transposed(right_side - pushed, inverse)

    solved = lax.fori_loop(0, chain_len - 1, descend, own_term)
    onehot = (
        rows_here[:, None] == lax.broadcasted_iota(jnp.int32, (1, top_right.shape[1]), 1)
    ).astype(jnp.float32)
    partial_value = product(times_transposed(solved, across), onehot)
    residual_top = top_right - lax.psum(partial_value, ("gz", "ga"))
    local_part = product(times_transposed(residual_top, top_inverse), top_inverse)
    column_share = lax.psum_scatter(local_part, "ga", scatter_dimension=1, tiled=True)
    top_solution = lax.all_gather(column_share, "ga", axis=1, tiled=True)
    lifted = times_transposed(top_solution, onehot)
    reduced = solved - product(lifted, across)
    start_value = product(keep_mask * reduced, inverse)

    def ascend(step_index, current):
        sent_term = has_child * product(current, coupling)
        above_term = shifted(sent_term, "ga", -1)
        return product(keep_mask * (reduced - above_term), inverse)

    result = lax.fori_loop(0, chain_len - 1, ascend, start_value)
    return (result[None, None], top_solution)


def solution(mesh):
    placed = (
        P("gz", "ga", None, None),
        P("gz", "ga", None, None),
        P("gz", "ga", None, None),
        P("gz", "ga", None, None),
        P("gz", "ga", None),
        P("gz", "ga"),
        P(),
        P("ga", None),
    )
    return jax.shard_map(
        shards,
        mesh=mesh,
        in_specs=placed,
        out_specs=(P("gz", "ga", None, None), P()),
        check_vma=False,
    )
```

profile of v0, /device:TPU:30, one launch (start us, length us, event | category | flops | bytes accessed | tf_op | source)
XLA Modules:
  0.0 907.5 jit_solution(8091915293969979457)
XLA Ops:
  10.4 189.8 %while.22 = (s32[]{:T(128)}, f32[32,512]{1,0:T(8,128)S(1)}, f32[]{:T(128)}, f32[512,512]{1,0:T(8,128)}, f32[32,512]{1,0:T(8,128)S(1)}, /*index=5*/f32[512,512]{1,0:T(8,128)S(1)}, s32[]{:T(128)}, s32[]{:T(128)}) while((s32[]{:T(128)}, f32[32,512]{1,0:T(8,128)S(1)}, f32[]{:T(128)}, f32[512,512]{1,0:T(8,128)}, ...), condition=%wide.region_1.2_spmd.clone, body=%wide.region_0.1_spmd.clone.sunk | while | flops 201376768 | bytes 2691205 | solution.py:54
  20.2 7.6 collective-permute-start
  33.1 7.6 collective-permute-start
  45.9 7.6 collective-permute-start
  58.7 7.6 collective-permute-start
  71.5 7.6 collective-permute-start
  84.3 7.6 collective-permute-start
  97.2 7.6 collective-permute-start
  110.0 7.6 collective-permute-start
  122.8 7.6 collective-permute-start
  136.0 7.7 collective-permute-start
  149.0 7.6 collective-permute-start
  161.8 7.6 collective-permute-start
  174.6 7.6 collective-permute-start
  187.4 7.6 collective-permute-start
  202.8 265.5 %all-reduce.2.cloned.1.call-done = f32[32,1024]{1,0:T(8,128)} async-done(((f32[32,1024]{1,0:T(8,128)}), f32[32,1024]{1,0:T(8,128)}) %all-reduce.2.cloned.1.call-update) | async-done | bytes 131088 | tf_op jit(solution)/shard_map/psum | solution.py:59
  471.3 214.4 %reduce-scatter.4.cloned.1.call-done = f32[32,32]{1,0:T(8,128)} async-done(((f32[1024,32]{1,0:T(8,128)}), f32[32,32]{1,0:T(8,128)}) %reduce-scatter.4.cloned.1.call-update) | async-done | bytes 4112
  685.6 47.1 %all_gather.3 = f32[32,1024]{0,1:T(8,128)S(1)} all-gather(f32[32,32]{0,1:T(8,128)} %bitcast.62), channel_id=1, replica_groups=mesh['gz'=16,'ga'=32] {'ga'}, dimensions={1}, use_global_device_ids=true | all-gather | bytes 135168 | tf_op jit(solution)/shard_map/all_gather | solution.py:62
  735.4 164.6 %while.23 = (s32[]{:T(128)}, f32[32,512]{1,0:T(8,128)S(1)}, f32[]{:T(128)}, f32[512,512]{1,0:T(8,128)S(1)}, f32[32,512]{1,0:T(8,128)S(1)}, /*index=5*/f32[512,512]{1,0:T(8,128)S(1)}, s32[]{:T(128)}, s32[]{:T(128)}) while((s32[]{:T(128)}, f32[32,512]{1,0:T(8,128)S(1)}, f32[]{:T(128)}, f32[512,512]{1,0:T(8,128)S(1)}, ...), condition=%wide.region_5.6_spmd.clone, body=%wide.region_4.5_spmd.clone.sunk | while | flops 201376768 | bytes 2691205 | solution.py:72
  749.7 7.2 collective-permute-done.1
  760.9 6.9 collective-permute-done.1
  793.7 6.9 collective-permute-done.1
  804.6 6.9 collective-permute-done.1
  848.3 7.3 collective-permute-done.1
  (161 shorter events, 222.6 us)
Async XLA Ops:
  7.2 461.1 %all-reduce.2.cloned.1.call-start = ((), (), s32[]{:S(2)}) async-start(), calls=%async_computation.1 | async-start | bytes 262144 | tf_op jit(solution)/shard_map/psum | solution.py:59
  20.2 9.5 %collective-permute-start = (f32[32,512]{1,0:T(8,128)S(1)}, f32[32,512]{1,0:T(8,128)S(1)}, u32[]{:S(2)}, u32[]{:S(2)}) collective-permute-start(f32[32,512]{1,0:T(8,128)S(1)} %get-tuple-element.237), channel_id=1, source_target_pairs={{0,1},{1,2},{2,3},{3,4},{4,5},{5,6},{6,7},{7,8},{8,9},{9,10},{10,1... | collective-permute-start | bytes 196616 | tf_op jit(solution)/shard_map/while/body/eval_jaxpr/ppermute | solution.py:15
  45.9 9.5 %collective-permute-start = (f32[32,512]{1,0:T(8,128)S(1)}, f32[32,512]{1,0:T(8,128)S(1)}, u32[]{:S(2)}, u32[]{:S(2)}) collective-permute-start(f32[32,512]{1,0:T(8,128)S(1)} %get-tuple-element.237), channel_id=1, source_target_pairs={{0,1},{1,2},{2,3},{3,4},{4,5},{5,6},{6,7},{7,8},{8,9},{9,10},{10,1... | collective-permute-start | bytes 196616 | tf_op jit(solution)/shard_map/while/body/eval_jaxpr/ppermute | solution.py:15
  71.5 9.5 %collective-permute-start = (f32[32,512]{1,0:T(8,128)S(1)}, f32[32,512]{1,0:T(8,128)S(1)}, u32[]{:S(2)}, u32[]{:S(2)}) collective-permute-start(f32[32,512]{1,0:T(8,128)S(1)} %get-tuple-element.237), channel_id=1, source_target_pairs={{0,1},{1,2},{2,3},{3,4},{4,5},{5,6},{6,7},{7,8},{8,9},{9,10},{10,1... | collective-permute-start | bytes 196616 | tf_op jit(solution)/shard_map/while/body/eval_jaxpr/ppermute | solution.py:15
  84.3 9.5 %collective-permute-start = (f32[32,512]{1,0:T(8,128)S(1)}, f32[32,512]{1,0:T(8,128)S(1)}, u32[]{:S(2)}, u32[]{:S(2)}) collective-permute-start(f32[32,512]{1,0:T(8,128)S(1)} %get-tuple-element.237), channel_id=1, source_target_pairs={{0,1},{1,2},{2,3},{3,4},{4,5},{5,6},{6,7},{7,8},{8,9},{9,10},{10,1... | collective-permute-start | bytes 196616 | tf_op jit(solution)/shard_map/while/body/eval_jaxpr/ppermute | solution.py:15
  97.2 9.5 %collective-permute-start = (f32[32,512]{1,0:T(8,128)S(1)}, f32[32,512]{1,0:T(8,128)S(1)}, u32[]{:S(2)}, u32[]{:S(2)}) collective-permute-start(f32[32,512]{1,0:T(8,128)S(1)} %get-tuple-element.237), channel_id=1, source_target_pairs={{0,1},{1,2},{2,3},{3,4},{4,5},{5,6},{6,7},{7,8},{8,9},{9,10},{10,1... | collective-permute-start | bytes 196616 | tf_op jit(solution)/shard_map/while/body/eval_jaxpr/ppermute | solution.py:15
  110.0 9.5 %collective-permute-start = (f32[32,512]{1,0:T(8,128)S(1)}, f32[32,512]{1,0:T(8,128)S(1)}, u32[]{:S(2)}, u32[]{:S(2)}) collective-permute-start(f32[32,512]{1,0:T(8,128)S(1)} %get-tuple-element.237), channel_id=1, source_target_pairs={{0,1},{1,2},{2,3},{3,4},{4,5},{5,6},{6,7},{7,8},{8,9},{9,10},{10,1... | collective-permute-start | bytes 196616 | tf_op jit(solution)/shard_map/while/body/eval_jaxpr/ppermute | solution.py:15
  122.8 9.9 %collective-permute-start = (f32[32,512]{1,0:T(8,128)S(1)}, f32[32,512]{1,0:T(8,128)S(1)}, u32[]{:S(2)}, u32[]{:S(2)}) collective-permute-start(f32[32,512]{1,0:T(8,128)S(1)} %get-tuple-element.237), channel_id=1, source_target_pairs={{0,1},{1,2},{2,3},{3,4},{4,5},{5,6},{6,7},{7,8},{8,9},{9,10},{10,1... | collective-permute-start | bytes 196616 | tf_op jit(solution)/shard_map/while/body/eval_jaxpr/ppermute | solution.py:15
  136.0 9.6 %collective-permute-start = (f32[32,512]{1,0:T(8,128)S(1)}, f32[32,512]{1,0:T(8,128)S(1)}, u32[]{:S(2)}, u32[]{:S(2)}) collective-permute-start(f32[32,512]{1,0:T(8,128)S(1)} %get-tuple-element.237), channel_id=1, source_target_pairs={{0,1},{1,2},{2,3},{3,4},{4,5},{5,6},{6,7},{7,8},{8,9},{9,10},{10,1... | collective-permute-start | bytes 196616 | tf_op jit(solution)/shard_map/while/body/eval_jaxpr/ppermute | solution.py:15
  161.8 9.5 %collective-permute-start = (f32[32,512]{1,0:T(8,128)S(1)}, f32[32,512]{1,0:T(8,128)S(1)}, u32[]{:S(2)}, u32[]{:S(2)}) collective-permute-start(f32[32,512]{1,0:T(8,128)S(1)} %get-tuple-element.237), channel_id=1, source_target_pairs={{0,1},{1,2},{2,3},{3,4},{4,5},{5,6},{6,7},{7,8},{8,9},{9,10},{10,1... | collective-permute-start | bytes 196616 | tf_op jit(solution)/shard_map/while/body/eval_jaxpr/ppermute | solution.py:15
  187.4 9.5 %collective-permute-start = (f32[32,512]{1,0:T(8,128)S(1)}, f32[32,512]{1,0:T(8,128)S(1)}, u32[]{:S(2)}, u32[]{:S(2)}) collective-permute-start(f32[32,512]{1,0:T(8,128)S(1)} %get-tuple-element.237), channel_id=1, source_target_pairs={{0,1},{1,2},{2,3},{3,4},{4,5},{5,6},{6,7},{7,8},{8,9},{9,10},{10,1... | collective-permute-start | bytes 196616 | tf_op jit(solution)/shard_map/while/body/eval_jaxpr/ppermute | solution.py:15
  202.7 482.9 %reduce-scatter.4.cloned.1.call-start = ((), (), s32[]{:S(2)}) async-start(), calls=%async_computation.2 | async-start | bytes 540672
  736.2 9.5 %collective-permute-start.1 = (f32[32,512]{1,0:T(8,128)S(1)}, f32[32,512]{1,0:T(8,128)S(1)}, u32[]{:S(2)}, u32[]{:S(2)}) collective-permute-start(f32[32,512]{1,0:T(8,128)S(1)} %convolution_multiply_fusion.7), channel_id=1, source_target_pairs={{1,0},{2,1},{3,2},{4,3},{5,4},{6,5},{7,6},{8,7},{9,8},{10,9},{11,1... | collective-permute-start | bytes 196616 | tf_op jit(solution)/shard_map/while/body/eval_jaxpr/ppermute | solution.py:15
  747.1 9.8 %collective-permute-start.1 = (f32[32,512]{1,0:T(8,128)S(1)}, f32[32,512]{1,0:T(8,128)S(1)}, u32[]{:S(2)}, u32[]{:S(2)}) collective-permute-start(f32[32,512]{1,0:T(8,128)S(1)} %convolution_multiply_fusion.7), channel_id=1, source_target_pairs={{1,0},{2,1},{3,2},{4,3},{5,4},{6,5},{7,6},{8,7},{9,8},{10,9},{11,1... | collective-permute-start | bytes 196616 | tf_op jit(solution)/shard_map/while/body/eval_jaxpr/ppermute | solution.py:15
  758.3 9.5 %collective-permute-start.1 = (f32[32,512]{1,0:T(8,128)S(1)}, f32[32,512]{1,0:T(8,128)S(1)}, u32[]{:S(2)}, u32[]{:S(2)}) collective-permute-start(f32[32,512]{1,0:T(8,128)S(1)} %convolution_multiply_fusion.7), channel_id=1, source_target_pairs={{1,0},{2,1},{3,2},{4,3},{5,4},{6,5},{7,6},{8,7},{9,8},{10,9},{11,1... | collective-permute-start | bytes 196616 | tf_op jit(solution)/shard_map/while/body/eval_jaxpr/ppermute | solution.py:15
  769.3 9.5 %collective-permute-start.1 = (f32[32,512]{1,0:T(8,128)S(1)}, f32[32,512]{1,0:T(8,128)S(1)}, u32[]{:S(2)}, u32[]{:S(2)}) collective-permute-start(f32[32,512]{1,0:T(8,128)S(1)} %convolution_multiply_fusion.7), channel_id=1, source_target_pairs={{1,0},{2,1},{3,2},{4,3},{5,4},{6,5},{7,6},{8,7},{9,8},{10,9},{11,1... | collective-permute-start | bytes 196616 | tf_op jit(solution)/shard_map/while/body/eval_jaxpr/ppermute | solution.py:15
  780.2 9.5 %collective-permute-start.1 = (f32[32,512]{1,0:T(8,128)S(1)}, f32[32,512]{1,0:T(8,128)S(1)}, u32[]{:S(2)}, u32[]{:S(2)}) collective-permute-start(f32[32,512]{1,0:T(8,128)S(1)} %convolution_multiply_fusion.7), channel_id=1, source_target_pairs={{1,0},{2,1},{3,2},{4,3},{5,4},{6,5},{7,6},{8,7},{9,8},{10,9},{11,1... | collective-permute-start | bytes 196616 | tf_op jit(solution)/shard_map/while/body/eval_jaxpr/ppermute | solution.py:15
  791.1 9.5 %collective-permute-start.1 = (f32[32,512]{1,0:T(8,128)S(1)}, f32[32,512]{1,0:T(8,128)S(1)}, u32[]{:S(2)}, u32[]{:S(2)}) collective-permute-start(f32[32,512]{1,0:T(8,128)S(1)} %convolution_multiply_fusion.7), channel_id=1, source_target_pairs={{1,0},{2,1},{3,2},{4,3},{5,4},{6,5},{7,6},{8,7},{9,8},{10,9},{11,1... | collective-permute-start | bytes 196616 | tf_op jit(solution)/shard_map/while/body/eval_jaxpr/ppermute | solution.py:15
  802.0 9.5 %collective-permute-start.1 = (f32[32,512]{1,0:T(8,128)S(1)}, f32[32,512]{1,0:T(8,128)S(1)}, u32[]{:S(2)}, u32[]{:S(2)}) collective-permute-start(f32[32,512]{1,0:T(8,128)S(1)} %convolution_multiply_fusion.7), channel_id=1, source_target_pairs={{1,0},{2,1},{3,2},{4,3},{5,4},{6,5},{7,6},{8,7},{9,8},{10,9},{11,1... | collective-permute-start | bytes 196616 | tf_op jit(solution)/shard_map/while/body/eval_jaxpr/ppermute | solution.py:15
  834.8 9.5 %collective-permute-start.1 = (f32[32,512]{1,0:T(8,128)S(1)}, f32[32,512]{1,0:T(8,128)S(1)}, u32[]{:S(2)}, u32[]{:S(2)}) collective-permute-start(f32[32,512]{1,0:T(8,128)S(1)} %convolution_multiply_fusion.7), channel_id=1, source_target_pairs={{1,0},{2,1},{3,2},{4,3},{5,4},{6,5},{7,6},{8,7},{9,8},{10,9},{11,1... | collective-permute-start | bytes 196616 | tf_op jit(solution)/shard_map/while/body/eval_jaxpr/ppermute | solution.py:15
  845.7 9.9 %collective-permute-start.1 = (f32[32,512]{1,0:T(8,128)S(1)}, f32[32,512]{1,0:T(8,128)S(1)}, u32[]{:S(2)}, u32[]{:S(2)}) collective-permute-start(f32[32,512]{1,0:T(8,128)S(1)} %convolution_multiply_fusion.7), channel_id=1, source_target_pairs={{1,0},{2,1},{3,2},{4,3},{5,4},{6,5},{7,6},{8,7},{9,8},{10,9},{11,1... | collective-permute-start | bytes 196616 | tf_op jit(solution)/shard_map/while/body/eval_jaxpr/ppermute | solution.py:15
  857.1 9.5 %collective-permute-start.1 = (f32[32,512]{1,0:T(8,128)S(1)}, f32[32,512]{1,0:T(8,128)S(1)}, u32[]{:S(2)}, u32[]{:S(2)}) collective-permute-start(f32[32,512]{1,0:T(8,128)S(1)} %convolution_multiply_fusion.7), channel_id=1, source_target_pairs={{1,0},{2,1},{3,2},{4,3},{5,4},{6,5},{7,6},{8,7},{9,8},{10,9},{11,1... | collective-permute-start | bytes 196616 | tf_op jit(solution)/shard_map/while/body/eval_jaxpr/ppermute | solution.py:15
  878.9 9.5 %collective-permute-start.1 = (f32[32,512]{1,0:T(8,128)S(1)}, f32[32,512]{1,0:T(8,128)S(1)}, u32[]{:S(2)}, u32[]{:S(2)}) collective-permute-start(f32[32,512]{1,0:T(8,128)S(1)} %convolution_multiply_fusion.7), channel_id=1, source_target_pairs={{1,0},{2,1},{3,2},{4,3},{5,4},{6,5},{7,6},{8,7},{9,8},{10,9},{11,1... | collective-permute-start | bytes 196616 | tf_op jit(solution)/shard_map/while/body/eval_jaxpr/ppermute | solution.py:15
  889.9 9.5 %collective-permute-start.1 = (f32[32,512]{1,0:T(8,128)S(1)}, f32[32,512]{1,0:T(8,128)S(1)}, u32[]{:S(2)}, u32[]{:S(2)}) collective-permute-start(f32[32,512]{1,0:T(8,128)S(1)} %convolution_multiply_fusion.7), channel_id=1, source_target_pairs={{1,0},{2,1},{3,2},{4,3},{5,4},{6,5},{7,6},{8,7},{9,8},{10,9},{11,1... | collective-permute-start | bytes 196616 | tf_op jit(solution)/shard_map/while/body/eval_jaxpr/ppermute | solution.py:15
  (16 other events, 806.4 us)
Sparse Core Ops, SparseCore 0:
  202.8 265.4 all-reduce.1
  473.3 212.3 reduce-scatter.3
where the time goes:
time: 909 us; the launch traced here: 908 us
  waiting for transfers between devices  602 us (66%)
  starting transfers between devices  141 us (16%)
  matrix products  79.6 us (9%)
  blocking collectives  47.1 us (5%)
  other arithmetic  19.6 us (2%)
  between operations  14.9 us (2%)
    psum x1, waiting for transfers between devices, shards(): residual_top = top_right - lax.psum(partial_value, ('gz', 'ga'))  266 us
    unnamed x3, waiting for transfers between devices  214 us
    ppermute x30, starting transfers between devices, shifted(): return lax.ppermute(block, axis, route)  141 us
    ppermute x30, waiting for transfers between devices, shifted(): return lax.ppermute(block, axis, route)  122 us
    dot_general x34, matrix products, times_transposed(): lax.dot_general(left, right_part, (((1,), (1,)), ((), ())), precision=PRE...  54.3 us
    all_gather x1, blocking collectives, shards(): top_solution = lax.all_gather(column_share, 'ga', axis=1, tiled=True)  47.1 us
    dot_general x33, matrix products, product(): jnp.dot(left, right_part, precision=PRECISE, preferred_element_type=jnp.f...  23.5 us
    convert_element_type x31, other arithmetic, shards(): (lax.broadcasted_iota(jnp.int32, (1, width_cols), 1) < live_cols[0, 0]).a...  19.6 us
  transfers between devices with their start and end apart: 32, of which 32 were waited for; matrix products, arithmetic and copies ran while one was open for 2% of the time, Pallas kernels for 0%

commit v1 on v0

v1 whole, which is shorter than its diff:
```python
import jax
import jax.numpy as jnp
from jax import lax
from jax.experimental import pallas as pl
from jax.experimental.pallas import tpu as pltpu
from jax.sharding import PartitionSpec as P

BRANCHES = 2
ROW = 4
NN = (((1,), (0,)), ((), ()))
NT = (((1,), (1,)), ((), ()))
VMEM = pl.BlockSpec(memory_space=pltpu.VMEM)
SMEM = pl.BlockSpec(memory_space=pltpu.SMEM)
F32 = jnp.float32
BF16 = jnp.bfloat16


def split(value):
    high = value.astype(BF16)
    return high, (value - high.astype(F32)).astype(BF16)


def bdot(left, right, dims):
    return lax.dot_general(left, right, dims, preferred_element_type=F32)


def dot3(left, right, dims):
    rows = left[0].shape[0]
    both = bdot(jnp.concatenate(left, 0), right[0], dims)
    return both[:rows] + both[rows:] + bdot(left[0], right[1], dims)


def kernel_call(body, outs, ins, scratch=(), flops=0, nbytes=0, limit=40):
    return pl.pallas_call(
        body,
        out_shape=outs,
        in_specs=ins,
        out_specs=jax.tree.map(lambda _: VMEM, outs),
        scratch_shapes=list(scratch),
        compiler_params=pltpu.CompilerParams(vmem_limit_bytes=limit * 2**20),
        cost_estimate=pl.CostEstimate(flops=flops, bytes_accessed=nbytes, transcendentals=0),
    )


def shape(*dims, kind=F32):
    return jax.ShapeDtypeStruct(dims, kind)


def prepare(live, right, inverse, coupling, upper, lower):
    width = inverse.shape[0]
    half = width // 2
    rhs = right.shape[0]
    count = live[0, 0]
    dh, dl = split(inverse[...])
    ch, cl = split(coupling[...])
    row = lax.broadcasted_iota(jnp.int32, (half, width), 0)
    top = dot3((dh[:half, :half], dl[:half, :half]), (ch[:half], cl[:half]), NN)
    upper[:half] = jnp.where(row < count, -top, 0.0)
    bottom = dot3((dh[half:], dl[half:]), (ch, cl), NN)
    lower[:half] = jnp.where(row + half < count, -bottom, 0.0)
    own = dot3(split(right[...]), (dh, dl), NT)
    col = lax.broadcasted_iota(jnp.int32, (rhs, width), 1)
    own = jnp.where(col < count, own, 0.0)
    upper[half:] = own[: rhs // 2]
    lower[half:] = own[rhs // 2 :]


def assemble(place, a0, b0, a1, b1, a2, b2, a3, b3, nh, nl, group, last):
    half = nh.shape[1] // 2
    rhs = group.shape[1]
    here = place[0]
    for offset, (a, b) in enumerate(((a0, b0), (a1, b1), (a2, b2), (a3, b3))):
        slot = lax.rem(here + offset, ROW)
        high, low = split(a[:half])
        nh[slot, :half] = high
        nl[slot, :half] = low
        high, low = split(b[:half])
        nh[slot, half:] = high
        nl[slot, half:] = low
        group[slot, : rhs // 2] = a[half:]
        group[slot, rhs // 2 :] = b[half:]
    value = group[0]
    for j in range(1, ROW):
        value = group[j] + dot3(split(value), (nh[j], nl[j]), NT)
        group[j] = value
    last[...] = value


def multiply_up(place, nh, nl, qh, ql, ph, plow):
    here = place[0]
    high, low = nh[0], nl[0]

    @pl.when(here == 0)
    def _():
        qh[...] = high
        ql[...] = low

    for j in range(1, ROW):
        high, low = split(dot3((nh[j], nl[j]), (high, low), NN))

        @pl.when(here == j)
        def _():
            qh[...] = high
            ql[...] = low

    ph[...] = high
    plow[...] = low


def hop_forward(base, coming, ph, plow, out):
    out[...] = base[...] + dot3(split(coming[...]), (ph[...], plow[...]), NT)


def hop_backward(base, coming, ph, plow, out):
    out[...] = base[...] + dot3(split(coming[...]), (ph[...], plow[...]), NN)


def onehot_of(rows, top):
    return (lax.broadcasted_iota(jnp.int32, (top, rows.shape[1]), 0) == rows[...]).astype(F32).astype(BF16)


def contribute(place, group, coming, qh, ql, across, rows, solved, tiles):
    here = place[0]
    value = group[here] + dot3(split(coming[...]), (qh[...], ql[...]), NT)
    solved[...] = value
    pushed = dot3(split(value), split(across[...]), NT)
    count, top_rows_, lanes = tiles.shape
    col_blocks = count // (value.shape[0] // top_rows_)
    onehot = onehot_of(rows, col_blocks * lanes)
    high, low = split(pushed)
    both = bdot(jnp.concatenate((high, low), 0), onehot, NT)
    total = both[: value.shape[0]] + both[value.shape[0] :]
    for piece in range(count):
        r, c = piece // col_blocks, piece % col_blocks
        tiles[piece] = total[r * top_rows_ : (r + 1) * top_rows_, c * lanes : (c + 1) * lanes]


def total_of(tiles, out):
    value = tiles[0]
    for piece in range(1, tiles.shape[0]):
        value = value + tiles[piece]
    for piece in range(out.shape[0]):
        out[piece] = value


def solve_top(tiles, top_right, weights, rows, solved, across, top_out, reduced):
    count, tile_rows, lanes = tiles.shape
    rhs, top = top_right.shape
    col_blocks = top // lanes
    lines = []
    for r in range(rhs // tile_rows):
        lines.append(jnp.concatenate([tiles[r * col_blocks + c] for c in range(col_blocks)], 1))
    rest = top_right[...] - jnp.concatenate(lines, 0)
    blocks, _, block_cols = weights.shape
    pairs = [split(weights[j]) for j in range(blocks)]
    mid = jnp.zeros((rhs, top), F32)
    for j in range(blocks):
        mid = mid + dot3(split(rest[:, j * block_cols : (j + 1) * block_cols]), pairs[j], NT)
    mid = split(mid)
    answer = jnp.concatenate([dot3(mid, pairs[j], NN) for j in range(blocks)], 1)
    top_out[...] = answer
    onehot = onehot_of(rows, top)
    high, low = split(answer)
    both = bdot(jnp.concatenate((high, low), 0), onehot, NN)
    lifted = both[:rhs] + both[rhs:]
    value = solved[...] - dot3(split(lifted), split(across[...]), NN)
    for piece in range(reduced.shape[0]):
        reduced[piece] = value


def row_backward(place, reduced, nh, nl, own, sent):
    here = place[0]
    value = reduced[ROW - 1]
    for j in range(ROW - 1, -1, -1):
        if j < ROW - 1:
            value = reduced[j] + value

        @pl.when(here == j)
        def _():
            own[...] = value

        value = dot3(split(value), (nh[j], nl[j]), NN)
    sent[...] = value


def finish(place, live, own, coming, nh, nl, inverse, out, term):
    here = place[0]
    term[...] = coming[...]
    for j in range(ROW - 1, 0, -1):

        @pl.when(here < j)
        def _():
            term[...] = dot3(split(term[...]), (nh[j], nl[j]), NN)

    value = own[...] + term[...]
    col = lax.broadcasted_iota(jnp.int32, value.shape, 1)
    value = jnp.where(col < live[0, 0], value, 0.0)
    out[...] = dot3(split(value), split(inverse[...]), NN)


def shards(
    right_sides, diag_inverse, chain_block, top_block, top_rows, live_cols, top_right, top_inverse
):
    ga, gz = lax.axis_size("ga"), lax.axis_size("gz")
    chain_len = ga // BRANCHES
    chain_rows = chain_len // ROW
    index = lax.axis_index("ga")
    place = (index % ROW).astype(jnp.int32)[None]
    right, inverse = right_sides[0, 0], diag_inverse[0, 0]
    coupling, across = chain_block[0, 0], top_block[0, 0]
    rows = top_rows[0]
    rhs, width = right.shape
    top = top_right.shape[1]
    x_groups = [[r * ROW + c for c in range(ROW)] for r in range(ga // ROW)]
    y_groups = [[r * ROW + c for r in range(ga // ROW)] for c in range(ROW)]

    def ring(value, step):
        return lax.ppermute(
            value, "ga", [(i, i // ROW * ROW + (i + step) % ROW) for i in range(ga)]
        )

    def hop(value, step):
        route = [
            (i, i + step * ROW)
            for i in range(ga)
            if 0 <= i // ROW % chain_rows + step < chain_rows
        ]
        return lax.ppermute(value, "ga", route)

    def pair(*dims):
        return (shape(*dims, kind=BF16), shape(*dims, kind=BF16))

    level = lax.axis_index("gz")
    tile = 8
    wide = top // (gz // (top_inverse.shape[0] // tile))
    ways = top_inverse.shape[0] // tile
    piece = lax.dynamic_slice(
        top_inverse, (level % ways * tile, level // ways * wide), (tile, wide)
    )
    piece = lax.all_gather(piece, "ga", axis_index_groups=y_groups)
    piece = lax.all_gather(piece, "ga", axis_index_groups=x_groups)
    weights = lax.all_gather(piece, "gz").reshape(gz // ways, top, wide)

    half = width // 2 + rhs // 2
    a0, b0 = kernel_call(
        prepare,
        (shape(half, width), shape(half, width)),
        [SMEM, VMEM, VMEM, VMEM],
        flops=6 * width**3,
        nbytes=16 * width**2,
    )(live_cols, right, inverse, coupling)
    a3 = ring(a0, 1)
    b1 = ring(b0, -1)
    b3 = ring(b0, 1)
    a1 = ring(a0, -1)
    a2 = ring(a3, 1)
    b2 = ring(b1, -1)

    nh, nl, group, last = kernel_call(
        assemble,
        pair(ROW, width, width) + (shape(ROW, rhs, width), shape(rhs, width)),
        [SMEM] + [VMEM] * 8,
        flops=24 * rhs * width**2,
        nbytes=32 * width**2,
    )(place, a0, b0, a1, b1, a2, b2, a3, b3)
    coming = hop(last, 1)
    qh, ql, ph, plow = kernel_call(
        multiply_up,
        pair(width, width) * 2,
        [SMEM, VMEM, VMEM],
        flops=18 * width**3,
        nbytes=24 * width**2,
    )(place, nh, nl)
    for _ in range(chain_rows - 2):
        moved = kernel_call(
            hop_forward, shape(rhs, width), [VMEM] * 4, flops=6 * rhs * width**2
        )(last, coming, ph, plow)
        coming = hop(moved, 1)

    pieces = ga
    tiles = (pieces, rhs * top // pieces // 128, 128)
    solved, partial = kernel_call(
        contribute,
        (shape(rhs, width), shape(*tiles)),
        [SMEM] + [VMEM] * 6,
        flops=12 * rhs * width**2,
    )(place, group, coming, qh, ql, across, rows)
    partial = lax.all_to_all(partial, "ga", 0, 0)
    partial = kernel_call(total_of, shape(gz, *tiles[1:]), [VMEM])(partial)
    partial = lax.all_to_all(partial, "gz", 0, 0)
    partial = kernel_call(total_of, shape(*tiles), [VMEM])(partial)
    partial = lax.all_to_all(partial, "ga", 0, 0)
    top_solution, reduced = kernel_call(
        solve_top,
        (shape(rhs, top), shape(ROW, rhs, width)),
        [VMEM] * 6,
        flops=12 * rhs * top**2,
    )(partial, top_right, weights, rows, solved, across)

    reduced = lax.all_to_all(reduced, "ga", 0, 0, axis_index_groups=x_groups)
    own, sent = kernel_call(
        row_backward,
        (shape(rhs, width), shape(rhs, width)),
        [SMEM] + [VMEM] * 3,
        flops=24 * rhs * width**2,
    )(place, reduced, nh, nl)
    coming = hop(sent, -1)
    for _ in range(chain_rows - 2):
        moved = kernel_call(
            hop_backward, shape(rhs, width), [VMEM] * 4, flops=6 * rhs * width**2
        )(sent, coming, ph, plow)
        coming = hop(moved, -1)
    result = kernel_call(
        finish,
        shape(rhs, width),
        [SMEM, SMEM] + [VMEM] * 5,
        scratch=[pltpu.VMEM((rhs, width), F32)],
        flops=24 * rhs * width**2,
    )(place, live_cols, own, coming, nh, nl, inverse)
    return (result[None, None], top_solution)


def solution(mesh):
    placed = (
        P("gz", "ga", None, None),
        P("gz", "ga", None, None),
        P("gz", "ga", None, None),
        P("gz", "ga", None, None),
        P("gz", "ga", None),
        P("gz", "ga"),
        P(),
        P("ga", None),
    )
    return jax.shard_map(
        shards,
        mesh=mesh,
        in_specs=placed,
        out_specs=(P("gz", "ga", None, None), P()),
        check_vma=False,
    )
```

time: 909 us -> 209 us (0.23)
  the two profiles are of different devices: /device:TPU:30 before, /device:TPU:8 now
where the time goes in v1:
time: 209 us; the launch traced here: 208 us
  blocking collectives  96.6 us (46%)
  starting transfers between devices  39.2 us (19%)
  waiting for transfers between devices  28.1 us (13%)
  Pallas kernels  16.1 us (8%)
  between operations  14.9 us (7%)
  local copies, waits for them, and re-layouts  12.9 us (6%)
    all_to_all x2, blocking collectives, shards(): partial = lax.all_to_all(partial, 'ga', 0, 0)  31.7 us
    all_gather x1, blocking collectives, shards(): piece = lax.all_gather(piece, 'ga', axis_index_groups=y_groups)  27.1 us
    ppermute x6, starting transfers between devices, ring(): lax.ppermute(value, 'ga', [(i, i // ROW * ROW + (i + step) % ROW) for i i...  19.9 us
    ppermute x6, starting transfers between devices, hop(): return lax.ppermute(value, 'ga', route)  19.2 us
    ppermute x6, waiting for transfers between devices, hop(): return lax.ppermute(value, 'ga', route)  16.2 us
    all_to_all x1, blocking collectives, shards(): partial = lax.all_to_all(partial, 'gz', 0, 0)  15.8 us
    all_gather x1, blocking collectives, shards(): piece = lax.all_gather(piece, 'ga', axis_index_groups=x_groups)  13 us
    unnamed x34, local copies, waits for them, and re-layouts  12.1 us
  transfers between devices with their start and end apart: 13, of which 8 were waited for; matrix products, arithmetic and copies ran while one was open for 0% of the time, Pallas kernels for 5%

profile of v1, /device:TPU:8, one launch (start us, length us, event | category | flops | bytes accessed | tf_op | source)
XLA Modules:
  0.0 207.7 jit_solution(14474175566730857648)
XLA Ops:
  7.9 27.1 %all-gather = f32[64,256]{1,0:T(8,128)S(1)} all-gather(f32[8,256]{1,0:T(8,128)S(1)} %dynamic_slice.3), channel_id=2, replica_groups={{0,4,8,12,16,20,24,28},{1,5,9,13,17,21,25,29},{2,6,10,14,18,22,26,30},{..., dimensions={0}, use_global_device_ids=true | all-gather | bytes 73728 | tf_op jit(solution)/shard_map/all_gather | solution.py:240
  35.1 13.0 %all-gather.1 = f32[32,8,256]{2,1,0:T(8,128)} all-gather(f32[8,8,256]{2,1,0:T(8,128)S(1)} %bitcast.20), channel_id=3, replica_groups={{0,1,2,3},{4,5,6,7},{8,9,10,11},{12,13,14,15},{16,17,18,19},{20,21,22,2..., dimensions={0}, use_global_device_ids=true | all-gather | bytes 327680 | tf_op jit(solution)/shard_map/all_gather | solution.py:241
  55.0 5.1 %collective-permute-start.1 = (f32[272,512]{1,0:T(8,128)S(1)}, f32[272,512]{1,0:T(8,128)S(1)}, u32[]{:S(2)}, u32[]{:S(2)}) collective-permute-start(f32[272,512]{1,0:T(8,128)S(1)} %get-tuple-element.19.b0), channel_id=1, source_target_pairs={{0,3},{1,0},{2,1},{3,2},{4,7},{5,4},{6,5},{7,6},{8,11},{9,8},{10,9... | collective-permute-start | bytes 1671176 | tf_op jit(solution)/shard_map/ppermute | solution.py:218
  62.1 3.9 %collective-permute-start.5 = (f32[272,512]{1,0:T(8,128)S(1)}, f32[272,512]{1,0:T(8,128)}, u32[]{:S(2)}, u32[]{:S(2)}) collective-permute-start(f32[272,512]{1,0:T(8,128)S(1)} %get-tuple-element.19.b0), channel_id=1, source_target_pairs={{0,1},{1,2},{2,3},{3,0},{4,5},{5,6},{6,7},{7,4},{8,9},{9,10},{10,1... | collective-permute-start | bytes 1671176 | tf_op jit(solution)/shard_map/ppermute | solution.py:218
  66.0 5.7 %collective-permute-done.2.a3 = f32[272,512]{1,0:T(8,128)S(1)} collective-permute-done((f32[272,512]{1,0:T(8,128)S(1)}, f32[272,512]{1,0:T(8,128)S(1)}, u32[]{:S(2)}, u32[]{:S(2)}) %collective-permute-start.2) | collective-permute-done | bytes 557088 | tf_op jit(solution)/shard_map/ppermute | solution.py:218
  74.5 5.1 %collective-permute-start.4 = (f32[272,512]{1,0:T(8,128)S(1)}, f32[272,512]{1,0:T(8,128)}, u32[]{:S(2)}, u32[]{:S(2)}) collective-permute-start(f32[272,512]{1,0:T(8,128)S(1)} %collective-permute-done.1.b1), channel_id=1, source_target_pairs={{0,3},{1,0},{2,1},{3,2},{4,7},{5,4},{6,5},{7,6},{8,11},{9,8},{10,9... | collective-permute-start | bytes 1671176 | tf_op jit(solution)/shard_map/ppermute | solution.py:218
  81.4 6.0 %collective-permute-done.3.a2 = f32[272,512]{1,0:T(8,128)} collective-permute-done((f32[272,512]{1,0:T(8,128)S(1)}, f32[272,512]{1,0:T(8,128)}, u32[]{:S(2)}, u32[]{:S(2)}) %collective-permute-start.3) | collective-permute-done | bytes 557088 | tf_op jit(solution)/shard_map/ppermute | solution.py:218
  90.5 3.4 %shard_map.96 = (bf16[4,512,512]{2,1,0:T(8,128)(2,1)S(1)}, bf16[4,512,512]{2,1,0:T(8,128)(2,1)S(1)}, f32[4,32,512]{2,1,0:T(8,128)S(1)}, f32[32,512]{1,0:T(8,128)S(1)}) custom-call(s32[1]{0:T(128)} %bitcast.place, f32[272,512]{1,0:T(8,128)S(1)} %get-tuple-element.18.a0, f32[272,512]{1,0:T(8,128)S(1)} %get-tuple-element.19.b0, f32[272,512]{1,0:T(8,128)S(1)} %copy-done.12, ...), custom_call_target="tpu_custom_call" | custom-call | flops 201326592 | bytes 8388608 | tf_op jit(solution)/shard_map/pallas_call | solution.py:259
  93.9 4.0 %collective-permute-start.6 = (f32[32,512]{1,0:T(8,128)S(1)}, f32[32,512]{1,0:T(8,128)S(1)}, u32[]{:S(2)}, u32[]{:S(2)}) collective-permute-start(f32[32,512]{1,0:T(8,128)S(1)} %get-tuple-element.21.base), channel_id=1, source_target_pairs={{0,4},{1,5},{2,6},{3,7},{4,8},{5,9},{6,10},{7,11},{8,12},{9,13},{1... | collective-permute-start | bytes 196616 | tf_op jit(solution)/shard_map/ppermute | solution.py:228
  97.9 3.2 %shard_map.97 = (bf16[512,512]{1,0:T(8,128)(2,1)S(1)}, bf16[512,512]{1,0:T(8,128)(2,1)S(1)}, bf16[512,512]{1,0:T(8,128)(2,1)S(1)}, bf16[512,512]{1,0:T(8,128)(2,1)S(1)}) custom-call(s32[1]{0:T(128)} %bitcast.place, bf16[4,512,512]{2,1,0:T(8,128)(2,1)S(1)} %get-tuple-element.22.nh, bf16[4,512,512]{2,1,0:T(8,128)(2,1)S(1)} %get-tuple-element.23.nl), custom_call_target="tpu_custom_call" | custom-call | flops 2415919104 | bytes 6291456 | tf_op jit(solution)/shard_map/pallas_call | solution.py:267
  101.6 3.0 %collective-permute-start.7 = (f32[32,512]{1,0:T(8,128)S(1)}, f32[32,512]{1,0:T(8,128)S(1)}, u32[]{:S(2)}, u32[]{:S(2)}) collective-permute-start(f32[32,512]{1,0:T(8,128)S(1)} %shard_map.98), channel_id=1, source_target_pairs={{0,4},{1,5},{2,6},{3,7},{4,8},{5,9},{6,10},{7,11},{8,12},{9,13},{1... | collective-permute-start | bytes 196616 | tf_op jit(solution)/shard_map/ppermute | solution.py:228
  104.6 3.3 %collective-permute-done.7.coming = f32[32,512]{1,0:T(8,128)S(1)} collective-permute-done((f32[32,512]{1,0:T(8,128)S(1)}, f32[32,512]{1,0:T(8,128)S(1)}, u32[]{:S(2)}, u32[]{:S(2)}) %collective-permute-start.7) | collective-permute-done | bytes 65568 | tf_op jit(solution)/shard_map/ppermute | solution.py:228
  111.2 3.6 %collective-permute-done.8.coming = f32[32,512]{1,0:T(8,128)S(1)} collective-permute-done((f32[32,512]{1,0:T(8,128)S(1)}, f32[32,512]{1,0:T(8,128)S(1)}, u32[]{:S(2)}, u32[]{:S(2)}) %collective-permute-start.8) | collective-permute-done | bytes 65568 | tf_op jit(solution)/shard_map/ppermute | solution.py:228
  115.9 17.3 %all_to_all.20.tiles = f32[32,8,128]{2,1,0:T(8,128)S(1)} all-to-all(f32[32,8,128]{2,1,0:T(8,128)S(1)} %get-tuple-element.28), channel_id=1, replica_groups=mesh['gz'=16,'ga'=32] {'ga'}, dimensions={0} | all-to-all | bytes 262144 | tf_op jit(solution)/shard_map/all_to_all | solution.py:288
  133.3 15.8 %all_to_all.21.tiles = f32[16,8,128]{2,1,0:T(8,128)S(1)} all-to-all(f32[16,8,128]{2,1,0:T(8,128)S(1)} %shard_map.101), channel_id=1, replica_groups=mesh['gz'=16,'ga'=32] {'gz'}, dimensions={0} | all-to-all | bytes 131072 | tf_op jit(solution)/shard_map/all_to_all | solution.py:290
  149.1 14.3 %all_to_all.22.tiles = f32[32,8,128]{2,1,0:T(8,128)S(1)} all-to-all(f32[32,8,128]{2,1,0:T(8,128)S(1)} %shard_map.102), channel_id=1, replica_groups=mesh['gz'=16,'ga'=32] {'ga'}, dimensions={0} | all-to-all | bytes 262144 | tf_op jit(solution)/shard_map/all_to_all | solution.py:292
  166.7 3.0 %shard_map.103 = (f32[32,1024]{1,0:T(8,128)}, f32[4,32,512]{2,1,0:T(8,128)S(1)}) custom-call(f32[32,8,128]{2,1,0:T(8,128)S(1)} %all_to_all.22.tiles, f32[32,1024]{1,0:T(8,128)S(1)} %copy-done.13, f32[4,1024,256]{2,1,0:T(8,128)S(1)} %bitcast.10, s32[1,256]{1,0:T(1,128)S(1)} %bitcast.16, f32[32,512]{1,0:T(8,128)S(1)} %get-tuple-element.29.solved, ...), custom_call_target="tpu_custom_call" | custom-call | flops 402653184 | tf_op jit(solution)/shard_map/pallas_call | solution.py:293
  169.7 9.1 %all_to_all.23.reduced = f32[4,32,512]{2,1,0:T(8,128)S(1)} all-to-all(f32[4,32,512]{2,1,0:T(8,128)S(1)} %get-tuple-element.30), channel_id=1, replica_groups={{0,1,2,3},{4,5,6,7},{8,9,10,11},{12,13,14,15},{16,17,18,19},{20,21,22,2..., dimensions={0} | all-to-all | bytes 524288 | tf_op jit(solution)/shard_map/all_to_all | solution.py:300
  179.9 3.2 %collective-permute-start.9 = (f32[32,512]{1,0:T(8,128)S(1)}, f32[32,512]{1,0:T(8,128)S(1)}, u32[]{:S(2)}, u32[]{:S(2)}) collective-permute-start(f32[32,512]{1,0:T(8,128)S(1)} %get-tuple-element.32.base), channel_id=1, source_target_pairs={{4,0},{5,1},{6,2},{7,3},{8,4},{9,5},{10,6},{11,7},{12,8},{13,9},{1... | collective-permute-start | bytes 196616 | tf_op jit(solution)/shard_map/ppermute | solution.py:228
  183.1 3.1 %collective-permute-done.9.coming = f32[32,512]{1,0:T(8,128)S(1)} collective-permute-done((f32[32,512]{1,0:T(8,128)S(1)}, f32[32,512]{1,0:T(8,128)S(1)}, u32[]{:S(2)}, u32[]{:S(2)}) %collective-permute-start.9) | collective-permute-done | bytes 65568 | tf_op jit(solution)/shard_map/ppermute | solution.py:228
  186.5 3.1 %collective-permute-start.10 = (f32[32,512]{1,0:T(8,128)S(1)}, f32[32,512]{1,0:T(8,128)S(1)}, u32[]{:S(2)}, u32[]{:S(2)}) collective-permute-start(f32[32,512]{1,0:T(8,128)S(1)} %shard_map.105), channel_id=1, source_target_pairs={{4,0},{5,1},{6,2},{7,3},{8,4},{9,5},{10,6},{11,7},{12,8},{13,9},{1... | collective-permute-start | bytes 196616 | tf_op jit(solution)/shard_map/ppermute | solution.py:228
  189.5 3.1 %collective-permute-done.10.coming = f32[32,512]{1,0:T(8,128)S(1)} collective-permute-done((f32[32,512]{1,0:T(8,128)S(1)}, f32[32,512]{1,0:T(8,128)S(1)}, u32[]{:S(2)}, u32[]{:S(2)}) %collective-permute-start.10) | collective-permute-done | bytes 65568 | tf_op jit(solution)/shard_map/ppermute | solution.py:228
  192.9 3.1 %collective-permute-start.11 = (f32[32,512]{1,0:T(8,128)S(1)}, f32[32,512]{1,0:T(8,128)S(1)}, u32[]{:S(2)}, u32[]{:S(2)}) collective-permute-start(f32[32,512]{1,0:T(8,128)S(1)} %shard_map.106), channel_id=1, source_target_pairs={{4,0},{5,1},{6,2},{7,3},{8,4},{9,5},{10,6},{11,7},{12,8},{13,9},{1... | collective-permute-start | bytes 196616 | tf_op jit(solution)/shard_map/ppermute | solution.py:228
  196.0 3.1 %collective-permute-done.11.coming = f32[32,512]{1,0:T(8,128)S(1)} collective-permute-done((f32[32,512]{1,0:T(8,128)S(1)}, f32[32,512]{1,0:T(8,128)S(1)}, u32[]{:S(2)}, u32[]{:S(2)}) %collective-permute-start.11) | collective-permute-done | bytes 65568 | tf_op jit(solution)/shard_map/ppermute | solution.py:228
  (57 shorter events, 28.2 us)
Async XLA Ops:
  7.2 156.3 %all-gather.5.cloned.1.call-start = ((), (), s32[]{:S(2)}) async-start(), calls=%async_computation.4 | async-start | bytes 4456448 | tf_op jit(solution)/shard_map/all_gather | solution.py:242
  48.7 1.2 copy-start.5
  50.0 1.2 copy-start.15
  53.1 18.7 %collective-permute-start.2 = (f32[272,512]{1,0:T(8,128)S(1)}, f32[272,512]{1,0:T(8,128)S(1)}, u32[]{:S(2)}, u32[]{:S(2)}) collective-permute-start(f32[272,512]{1,0:T(8,128)S(1)} %get-tuple-element.18.a0), channel_id=1, source_target_pairs={{0,1},{1,2},{2,3},{3,0},{4,5},{5,6},{6,7},{7,4},{8,9},{9,10},{10,1... | collective-permute-start | bytes 1671176 | tf_op jit(solution)/shard_map/ppermute | solution.py:218
  55.0 19.5 %collective-permute-start.1 = (f32[272,512]{1,0:T(8,128)S(1)}, f32[272,512]{1,0:T(8,128)S(1)}, u32[]{:S(2)}, u32[]{:S(2)}) collective-permute-start(f32[272,512]{1,0:T(8,128)S(1)} %get-tuple-element.19.b0), channel_id=1, source_target_pairs={{0,3},{1,0},{2,1},{3,2},{4,7},{5,4},{6,5},{7,6},{8,11},{9,8},{10,9... | collective-permute-start | bytes 1671176 | tf_op jit(solution)/shard_map/ppermute | solution.py:218
  60.1 20.3 %collective-permute-start = (f32[272,512]{1,0:T(8,128)S(1)}, f32[272,512]{1,0:T(8,128)S(1)}, u32[]{:S(2)}, u32[]{:S(2)}) collective-permute-start(f32[272,512]{1,0:T(8,128)S(1)} %get-tuple-element.18.a0), channel_id=1, source_target_pairs={{0,3},{1,0},{2,1},{3,2},{4,7},{5,4},{6,5},{7,6},{8,11},{9,8},{10,9... | collective-permute-start | bytes 1671176 | tf_op jit(solution)/shard_map/ppermute | solution.py:218
  62.1 19.3 %collective-permute-start.5 = (f32[272,512]{1,0:T(8,128)S(1)}, f32[272,512]{1,0:T(8,128)}, u32[]{:S(2)}, u32[]{:S(2)}) collective-permute-start(f32[272,512]{1,0:T(8,128)S(1)} %get-tuple-element.19.b0), channel_id=1, source_target_pairs={{0,1},{1,2},{2,3},{3,0},{4,5},{5,6},{6,7},{7,4},{8,9},{9,10},{10,1... | collective-permute-start | bytes 1671176 | tf_op jit(solution)/shard_map/ppermute | solution.py:218
  71.7 15.6 %collective-permute-start.3 = (f32[272,512]{1,0:T(8,128)S(1)}, f32[272,512]{1,0:T(8,128)}, u32[]{:S(2)}, u32[]{:S(2)}) collective-permute-start(f32[272,512]{1,0:T(8,128)S(1)} %collective-permute-done.2.a3), channel_id=1, source_target_pairs={{0,1},{1,2},{2,3},{3,0},{4,5},{5,6},{6,7},{7,4},{8,9},{9,10},{10,1... | collective-permute-start | bytes 1671176 | tf_op jit(solution)/shard_map/ppermute | solution.py:218
  74.5 12.9 %collective-permute-start.4 = (f32[272,512]{1,0:T(8,128)S(1)}, f32[272,512]{1,0:T(8,128)}, u32[]{:S(2)}, u32[]{:S(2)}) collective-permute-start(f32[272,512]{1,0:T(8,128)S(1)} %collective-permute-done.1.b1), channel_id=1, source_target_pairs={{0,3},{1,0},{2,1},{3,2},{4,7},{5,4},{6,5},{7,6},{8,11},{9,8},{10,9... | collective-permute-start | bytes 1671176 | tf_op jit(solution)/shard_map/ppermute | solution.py:218
  87.3 1.1 copy-start.8
  89.5 1.1 copy-start.12
  93.9 7.2 %copy-start = (bf16[4,512,512]{2,1,0:T(8,128)(2,1)}, bf16[4,512,512]{2,1,0:T(8,128)(2,1)S(1)}, u32[]{:S(2)}) copy-start(bf16[4,512,512]{2,1,0:T(8,128)(2,1)S(1)} %get-tuple-element.23.nl) | copy-start | bytes 6291460
  93.9 7.3 %collective-permute-start.6 = (f32[32,512]{1,0:T(8,128)S(1)}, f32[32,512]{1,0:T(8,128)S(1)}, u32[]{:S(2)}, u32[]{:S(2)}) collective-permute-start(f32[32,512]{1,0:T(8,128)S(1)} %get-tuple-element.21.base), channel_id=1, source_target_pairs={{0,4},{1,5},{2,6},{3,7},{4,8},{5,9},{6,10},{7,11},{8,12},{9,13},{1... | collective-permute-start | bytes 196616 | tf_op jit(solution)/shard_map/ppermute | solution.py:228
  101.2 13.7 %copy-start.3 = (f32[1,1,256,512]{3,2,1,0:T(8,128)S(1)}, f32[1,1,256,512]{3,2,1,0:T(8,128)}, u32[]{:S(2)}) copy-start(f32[1,1,256,512]{3,2,1,0:T(8,128)} %param.11) | copy-start | bytes 1572868
  101.2 13.7 %copy-start.14 = (s32[1,1,256]{2,1,0:T(1,128)S(1)}, s32[1,1,256]{2,1,0:T(1,128)}, u32[]{:S(2)}) copy-start(s32[1,1,256]{2,1,0:T(1,128)} %param.12) | copy-start | bytes 3076
  101.6 61.8 %copy-start.13 = (f32[32,1024]{1,0:T(8,128)S(1)}, f32[32,1024]{1,0:T(8,128)}, u32[]{:S(2)}) copy-start(f32[32,1024]{1,0:T(8,128)} %top_right.1) | copy-start | bytes 393220
  101.6 6.3 %collective-permute-start.7 = (f32[32,512]{1,0:T(8,128)S(1)}, f32[32,512]{1,0:T(8,128)S(1)}, u32[]{:S(2)}, u32[]{:S(2)}) collective-permute-start(f32[32,512]{1,0:T(8,128)S(1)} %shard_map.98), channel_id=1, source_target_pairs={{0,4},{1,5},{2,6},{3,7},{4,8},{5,9},{6,10},{7,11},{8,12},{9,13},{1... | collective-permute-start | bytes 196616 | tf_op jit(solution)/shard_map/ppermute | solution.py:228
  108.3 6.5 %collective-permute-start.8 = (f32[32,512]{1,0:T(8,128)S(1)}, f32[32,512]{1,0:T(8,128)S(1)}, u32[]{:S(2)}, u32[]{:S(2)}) collective-permute-start(f32[32,512]{1,0:T(8,128)S(1)} %shard_map.99), channel_id=1, source_target_pairs={{0,4},{1,5},{2,6},{3,7},{4,8},{5,9},{6,10},{7,11},{8,12},{9,13},{1... | collective-permute-start | bytes 196616 | tf_op jit(solution)/shard_map/ppermute | solution.py:228
  163.4 2.2 %copy-start.2 = (f32[64,8,8,256]{3,2,1,0:T(8,128)S(1)}, f32[64,8,8,256]{3,2,1,0:T(8,128)}, u32[]{:S(2)}) copy-start(f32[64,8,8,256]{3,2,1,0:T(8,128)} %all-gather.5.cloned.1.call-done) | copy-start | bytes 12582916
  166.7 12.1 %copy-start.1 = (bf16[4,512,512]{2,1,0:T(8,128)(2,1)S(1)}, bf16[4,512,512]{2,1,0:T(8,128)(2,1)}, u32[]{:S(2)}) copy-start(bf16[4,512,512]{2,1,0:T(8,128)(2,1)} %copy-done) | copy-start | bytes 6291460
  179.9 19.2 %copy-start.6 = (f32[1,1,512,512]{3,2,1,0:T(8,128)S(1)}, f32[1,1,512,512]{3,2,1,0:T(8,128)}, u32[]{:S(2)}) copy-start(f32[1,1,512,512]{3,2,1,0:T(8,128)} %param.9) | copy-start | bytes 3145732
  179.9 6.3 %collective-permute-start.9 = (f32[32,512]{1,0:T(8,128)S(1)}, f32[32,512]{1,0:T(8,128)S(1)}, u32[]{:S(2)}, u32[]{:S(2)}) collective-permute-start(f32[32,512]{1,0:T(8,128)S(1)} %get-tuple-element.32.base), channel_id=1, source_target_pairs={{4,0},{5,1},{6,2},{7,3},{8,4},{9,5},{10,6},{11,7},{12,8},{13,9},{1... | collective-permute-start | bytes 196616 | tf_op jit(solution)/shard_map/ppermute | solution.py:228
  186.5 6.2 %collective-permute-start.10 = (f32[32,512]{1,0:T(8,128)S(1)}, f32[32,512]{1,0:T(8,128)S(1)}, u32[]{:S(2)}, u32[]{:S(2)}) collective-permute-start(f32[32,512]{1,0:T(8,128)S(1)} %shard_map.105), channel_id=1, source_target_pairs={{4,0},{5,1},{6,2},{7,3},{8,4},{9,5},{10,6},{11,7},{12,8},{13,9},{1... | collective-permute-start | bytes 196616 | tf_op jit(solution)/shard_map/ppermute | solution.py:228
  192.9 6.2 %collective-permute-start.11 = (f32[32,512]{1,0:T(8,128)S(1)}, f32[32,512]{1,0:T(8,128)S(1)}, u32[]{:S(2)}, u32[]{:S(2)}) collective-permute-start(f32[32,512]{1,0:T(8,128)S(1)} %shard_map.106), channel_id=1, source_target_pairs={{4,0},{5,1},{6,2},{7,3},{8,4},{9,5},{10,6},{11,7},{12,8},{13,9},{1... | collective-permute-start | bytes 196616 | tf_op jit(solution)/shard_map/ppermute | solution.py:228
  (6 other events, 5.4 us)
Sparse Core Ops, SparseCore 0:
  48.2 47.3 all-gather.4

commit v2 on v1

--- a/solution.py
+++ b/solution.py
@@ -11,6 +11,7 @@
 NT = (((1,), (1,)), ((), ()))
 VMEM = pl.BlockSpec(memory_space=pltpu.VMEM)
 SMEM = pl.BlockSpec(memory_space=pltpu.SMEM)
+HBM = pl.BlockSpec(memory_space=pltpu.HBM)
 F32 = jnp.float32
 BF16 = jnp.bfloat16
 
@@ -30,7 +31,7 @@
     return both[:rows] + both[rows:] + bdot(left[0], right[1], dims)
 
 
-def kernel_call(body, outs, ins, scratch=(), flops=0, nbytes=0, limit=40):
+def kernel_call(body, outs, ins, scratch=(), flops=0, nbytes=0, limit=16):
     return pl.pallas_call(
         body,
         out_shape=outs,
@@ -46,18 +47,33 @@
     return jax.ShapeDtypeStruct(dims, kind)
 
 
-def prepare(live, right, inverse, coupling, upper, lower):
+def prepare(live, right_hbm, inverse_hbm, coupling_hbm, upper, lower, right, inverse, coupling, sems):
     width = inverse.shape[0]
     half = width // 2
     rhs = right.shape[0]
+    halves = (pl.ds(0, half), pl.ds(half, half))
+    moves = [
+        pltpu.make_async_copy(inverse_hbm, inverse, sems.at[0]),
+        pltpu.make_async_copy(coupling_hbm.at[halves[0]], coupling.at[halves[0]], sems.at[1]),
+        pltpu.make_async_copy(coupling_hbm.at[halves[1]], coupling.at[halves[1]], sems.at[2]),
+        pltpu.make_async_copy(right_hbm, right, sems.at[3]),
+    ]
+    for move in moves:
+        move.start()
     count = live[0, 0]
+    row = lax.broadcasted_iota(jnp.int32, (half, width), 0)
+    moves[0].wait()
     dh, dl = split(inverse[...])
-    ch, cl = split(coupling[...])
-    row = lax.broadcasted_iota(jnp.int32, (half, width), 0)
-    top = dot3((dh[:half, :half], dl[:half, :half]), (ch[:half], cl[:half]), NN)
+    moves[1].wait()
+    ch, cl = split(coupling[:half])
+    top = dot3((dh[:half, :half], dl[:half, :half]), (ch, cl), NN)
     upper[:half] = jnp.where(row < count, -top, 0.0)
-    bottom = dot3((dh[half:], dl[half:]), (ch, cl), NN)
+    bottom = dot3((dh[half:, :half], dl[half:, :half]), (ch, cl), NN)
+    moves[2].wait()
+    ch, cl = split(coupling[half:])
+    bottom = bottom + dot3((dh[half:, half:], dl[half:, half:]), (ch, cl), NN)
     lower[:half] = jnp.where(row + half < count, -bottom, 0.0)
+    moves[3].wait()
     own = dot3(split(right[...]), (dh, dl), NT)
     col = lax.broadcasted_iota(jnp.int32, (rhs, width), 1)
     own = jnp.where(col < count, own, 0.0)
@@ -65,20 +81,40 @@
     lower[half:] = own[rhs // 2 :]
 
 
-def assemble(place, a0, b0, a1, b1, a2, b2, a3, b3, nh, nl, group, last):
+def pack_lower(blocks, out):
+    start = 0
+    for y in range(blocks.shape[0]):
+        wide = (y + 1) * blocks.shape[2] // blocks.shape[0]
+        out[:, start : start + wide] = blocks[y, :, :wide]
+        start += wide
+
+
+def place_block(a, b, slot, nh, nl, group):
     half = nh.shape[1] // 2
     rhs = group.shape[1]
+    high, low = split(a[:half])
+    nh[slot, :half] = high
+    nl[slot, :half] = low
+    high, low = split(b[:half])
+    nh[slot, half:] = high
+    nl[slot, half:] = low
+    group[slot, : rhs // 2] = a[half:]
+    group[slot, rhs // 2 :] = b[half:]
+
+
+def stage(a0, b0, a1, b1, a3, b3, nh, nl, group):
+    for slot, (a, b) in enumerate(((a0, b0), (a1, b1), (a3, b3))):
+        place_block(a, b, slot, nh, nl, group)
+
+
+def assemble(place, sh, sl, sgroup, a2, b2, nh, nl, group, last):
     here = place[0]
-    for offset, (a, b) in enumerate(((a0, b0), (a1, b1), (a2, b2), (a3, b3))):
+    for at, offset in enumerate((0, 1, 3)):
         slot = lax.rem(here + offset, ROW)
-        high, low = split(a[:half])
-        nh[slot, :half] = high
-        nl[slot, :half] = low
-        high, low = split(b[:half])
-        nh[slot, half:] = high
-        nl[slot, half:] = low
-        group[slot, : rhs // 2] = a[half:]
-        group[slot, rhs // 2 :] = b[half:]
+        nh[slot] = sh[at]
+        nl[slot] = sl[at]
+        group[slot] = sgroup[at]
+    place_block(a2, b2, lax.rem(here + 2, ROW), nh, nl, group)
     value = group[0]
     for j in range(1, ROW):
         value = group[j] + dot3(split(value), (nh[j], nl[j]), NT)
@@ -124,45 +160,79 @@
     value = group[here] + dot3(split(coming[...]), (qh[...], ql[...]), NT)
     solved[...] = value
     pushed = dot3(split(value), split(across[...]), NT)
-    count, top_rows_, lanes = tiles.shape
-    col_blocks = count // (value.shape[0] // top_rows_)
-    onehot = onehot_of(rows, col_blocks * lanes)
+    count, depth, lanes = tiles.shape
+    col_blocks = count * depth // value.shape[0]
     high, low = split(pushed)
-    both = bdot(jnp.concatenate((high, low), 0), onehot, NT)
+    both = bdot(jnp.concatenate((high, low), 0), onehot_of(rows, col_blocks * lanes), NT)
     total = both[: value.shape[0]] + both[value.shape[0] :]
-    for piece in range(count):
-        r, c = piece // col_blocks, piece % col_blocks
-        tiles[piece] = total[r * top_rows_ : (r + 1) * top_rows_, c * lanes : (c + 1) * lanes]
-
-
-def total_of(tiles, out):
-    value = tiles[0]
-    for piece in range(1, tiles.shape[0]):
-        value = value + tiles[piece]
+    for tile in range(count):
+        r, c = tile // col_blocks, tile % col_blocks
+        tiles[tile] = total[r * depth : (r + 1) * depth, c * lanes : (c + 1) * lanes]
+
+
+def total_of(pieces, out):
+    value = pieces[0]
+    for piece in range(1, pieces.shape[0]):
+        value = value + pieces[piece]
     for piece in range(out.shape[0]):
         out[piece] = value
 
 
-def solve_top(tiles, top_right, weights, rows, solved, across, top_out, reduced):
-    count, tile_rows, lanes = tiles.shape
+def solve_top(
+    tiles, top_right, packed_hbm, across_hbm, rows, solved, top_out, reduced, packed, across, wh, wl, sems
+):
+    count, depth, lanes = tiles.shape
     rhs, top = top_right.shape
     col_blocks = top // lanes
+    steps = packed.shape[1] * packed.shape[0]
+    moves = []
+    start = 0
+    for step in range(top // steps):
+        wide = (step + 1) * steps
+        part = (slice(None), slice(None), pl.ds(start, wide))
+        moves.append(
+            pltpu.make_async_copy(packed_hbm.at[part], packed.at[part], sems.at[step])
+        )
+        start += wide
+    moves.append(pltpu.make_async_copy(across_hbm, across, sems.at[top // steps]))
+    for move in moves:
+        move.start()
     lines = []
-    for r in range(rhs // tile_rows):
+    for r in range(rhs // depth):
         lines.append(jnp.concatenate([tiles[r * col_blocks + c] for c in range(col_blocks)], 1))
-    rest = top_right[...] - jnp.concatenate(lines, 0)
-    blocks, _, block_cols = weights.shape
-    pairs = [split(weights[j]) for j in range(blocks)]
-    mid = jnp.zeros((rhs, top), F32)
-    for j in range(blocks):
-        mid = mid + dot3(split(rest[:, j * block_cols : (j + 1) * block_cols]), pairs[j], NT)
-    mid = split(mid)
-    answer = jnp.concatenate([dot3(mid, pairs[j], NN) for j in range(blocks)], 1)
+    rest = split(top_right[...] - jnp.concatenate(lines, 0))
+    block = 2 * steps
+    mid = []
+    start = 0
+    for step in range(top // steps):
+        wide = (step + 1) * steps
+        moves[step].wait()
+        high, low = split(packed[:, :, start : start + wide].reshape(steps, wide))
+        at = slice(step * steps, (step + 1) * steps)
+        wh[at, :wide] = high
+        wl[at, :wide] = low
+        start += wide
+        if step % 2 == 0:
+            wh[at, wide : wide + steps] = jnp.zeros((steps, steps), BF16)
+            wl[at, wide : wide + steps] = jnp.zeros((steps, steps), BF16)
+        else:
+            at = slice(wide - block, wide)
+            mid.append(
+                dot3((rest[0][:, :wide], rest[1][:, :wide]), (wh[at, :wide], wl[at, :wide]), NT)
+            )
+    mid = split(jnp.concatenate(mid, 1))
+    answer = []
+    for j in range(0, top, block):
+        end = j + block
+        answer.append(
+            dot3((mid[0][:, j:], mid[1][:, j:]), (wh[j:, j:end], wl[j:, j:end]), NN)
+        )
+    answer = jnp.concatenate(answer, 1)
     top_out[...] = answer
-    onehot = onehot_of(rows, top)
     high, low = split(answer)
-    both = bdot(jnp.concatenate((high, low), 0), onehot, NN)
+    both = bdot(jnp.concatenate((high, low), 0), onehot_of(rows, top), NN)
     lifted = both[:rhs] + both[rhs:]
+    moves[-1].wait()
     value = solved[...] - dot3(split(lifted), split(across[...]), NN)
     for piece in range(reduced.shape[0]):
         reduced[piece] = value
@@ -230,24 +300,21 @@
     def pair(*dims):
         return (shape(*dims, kind=BF16), shape(*dims, kind=BF16))
 
-    level = lax.axis_index("gz")
-    tile = 8
-    wide = top // (gz // (top_inverse.shape[0] // tile))
-    ways = top_inverse.shape[0] // tile
-    piece = lax.dynamic_slice(
-        top_inverse, (level % ways * tile, level // ways * wide), (tile, wide)
-    )
-    piece = lax.all_gather(piece, "ga", axis_index_groups=y_groups)
-    piece = lax.all_gather(piece, "ga", axis_index_groups=x_groups)
-    weights = lax.all_gather(piece, "gz").reshape(gz // ways, top, wide)
-
+    blocks = lax.all_gather(top_inverse, "ga", axis_index_groups=y_groups)
     half = width // 2 + rhs // 2
     a0, b0 = kernel_call(
         prepare,
         (shape(half, width), shape(half, width)),
-        [SMEM, VMEM, VMEM, VMEM],
+        [SMEM, HBM, HBM, HBM],
+        scratch=[
+            pltpu.VMEM((rhs, width), F32),
+            pltpu.VMEM((width, width), F32),
+            pltpu.VMEM((width, width), F32),
+            pltpu.SemaphoreType.DMA((4,)),
+        ],
         flops=6 * width**3,
         nbytes=16 * width**2,
+        limit=60,
     )(live_cols, right, inverse, coupling)
     a3 = ring(a0, 1)
     b1 = ring(b0, -1)
@@ -256,13 +323,19 @@
     a2 = ring(a3, 1)
     b2 = ring(b1, -1)
 
+    staged = kernel_call(
+        stage,
+        pair(ROW - 1, width, width) + (shape(ROW - 1, rhs, width),),
+        [VMEM] * 6,
+        nbytes=32 * width**2,
+    )(a0, b0, a1, b1, a3, b3)
     nh, nl, group, last = kernel_call(
         assemble,
         pair(ROW, width, width) + (shape(ROW, rhs, width), shape(rhs, width)),
-        [SMEM] + [VMEM] * 8,
+        [SMEM] + [VMEM] * 5,
         flops=24 * rhs * width**2,
         nbytes=32 * width**2,
-    )(place, a0, b0, a1, b1, a2, b2, a3, b3)
+    )(place, *staged, a2, b2)
     coming = hop(last, 1)
     qh, ql, ph, plow = kernel_call(
         multiply_up,
@@ -271,14 +344,22 @@
         flops=18 * width**3,
         nbytes=24 * width**2,
     )(place, nh, nl)
-    for _ in range(chain_rows - 2):
+    for step in range(chain_rows - 2):
         moved = kernel_call(
             hop_forward, shape(rhs, width), [VMEM] * 4, flops=6 * rhs * width**2
         )(last, coming, ph, plow)
+        if step == 0:
+            blocks, moved = lax.optimization_barrier((blocks, moved))
         coming = hop(moved, 1)
-
-    pieces = ga
-    tiles = (pieces, rhs * top // pieces // 128, 128)
+    packed = kernel_call(
+        pack_lower,
+        shape(top_inverse.shape[0], top * (ga // ROW + 1) // 2),
+        [VMEM],
+        nbytes=2 * top**2,
+    )(blocks)
+    packed = lax.all_gather(packed, "ga", axis_index_groups=x_groups)
+
+    tiles = (ga, rhs * top // ga // 128, 128)
     solved, partial = kernel_call(
         contribute,
         (shape(rhs, width), shape(*tiles)),
@@ -290,12 +371,21 @@
     partial = lax.all_to_all(partial, "gz", 0, 0)
     partial = kernel_call(total_of, shape(*tiles), [VMEM])(partial)
     partial = lax.all_to_all(partial, "ga", 0, 0)
+    partial, packed = lax.optimization_barrier((partial, packed))
     top_solution, reduced = kernel_call(
         solve_top,
         (shape(rhs, top), shape(ROW, rhs, width)),
-        [VMEM] * 6,
+        [VMEM, VMEM, HBM, HBM, VMEM, VMEM],
+        scratch=[
+            pltpu.VMEM(packed.shape, F32),
+            pltpu.VMEM(across.shape, F32),
+            pltpu.VMEM((top, top), BF16),
+            pltpu.VMEM((top, top), BF16),
+            pltpu.SemaphoreType.DMA((ga // ROW + 1,)),
+        ],
         flops=12 * rhs * top**2,
-    )(partial, top_right, weights, rows, solved, across)
+        limit=24,
+    )(partial, top_right, packed, across, rows, solved)
 
     reduced = lax.all_to_all(reduced, "ga", 0, 0, axis_index_groups=x_groups)
     own, sent = kernel_call(

time: 209 us -> 183 us (0.88)
  blocking collectives: 96.6 us -> 59.4 us
  waiting for transfers between devices: 28.1 us -> 35.1 us
  Pallas kernels: 16.1 us -> 19.3 us
    all_gather x2 -> x0, blocking collectives: 40.1 us -> none  [the longest x1 27.1 us: shards(): piece = lax.all_gather(piece, 'ga', axis_index_groups=y_groups)]
    ppermute x6, waiting for transfers between devices: 11.9 us -> 19.7 us  [ring(): lax.ppermute(value, 'ga', [(i, i // ROW * ROW + (i + step) % ROW) for i i...]
    pallas_call x2 -> x4, Pallas kernels: 4.04 us -> 9.17 us  [the longest x1 3.81 us: shards(): kernel_call(solve_top, (shape(rhs, top), shape(ROW, rhs, width)), [VMEM,...]
    all_to_all x1, blocking collectives: 15.8 us -> 18.2 us  [shards(): partial = lax.all_to_all(partial, 'gz', 0, 0)]
    unnamed x34 -> x36, local copies, waits for them, and re-layouts: 12.1 us -> 13.5 us
  transfers between devices with their start and end apart: 13 -> 14, of which waited for: 8 -> 9; matrix products, arithmetic and copies ran while one was open for 0% -> 0% of each run, Pallas kernels for 5% -> 7%
where the time goes in v2:
time: 183 us; the launch traced here: 182 us
  blocking collectives  59.4 us (32%)
  starting transfers between devices  39.7 us (22%)
  waiting for transfers between devices  35.1 us (19%)
  Pallas kernels  19.3 us (11%)
  between operations  14.9 us (8%)
  local copies, waits for them, and re-layouts  13.5 us (7%)
    all_to_all x2, blocking collectives, shards(): partial = lax.all_to_all(partial, 'ga', 0, 0)  32.1 us
    ppermute x6, starting transfers between devices, ring(): lax.ppermute(value, 'ga', [(i, i // ROW * ROW + (i + step) % ROW) for i i...  19.9 us
    ppermute x6, waiting for transfers between devices, ring(): lax.ppermute(value, 'ga', [(i, i // ROW * ROW + (i + step) % ROW) for i i...  19.7 us
    ppermute x6, starting transfers between devices, hop(): return lax.ppermute(value, 'ga', route)  19.7 us
    all_to_all x1, blocking collectives, shards(): partial = lax.all_to_all(partial, 'gz', 0, 0)  18.2 us
    ppermute x6, waiting for transfers between devices, hop(): return lax.ppermute(value, 'ga', route)  14.7 us
    unnamed x36, local copies, waits for them, and re-layouts  13.5 us
    all_to_all x1, blocking collectives, shards(): reduced = lax.all_to_all(reduced, 'ga', 0, 0, axis_index_groups=x_groups)  9.07 us
  transfers between devices with their start and end apart: 14, of which 9 were waited for; matrix products, arithmetic and copies ran while one was open for 0% of the time, Pallas kernels for 7%

profile of v2, /device:TPU:8, one launch (start us, length us, event | category | flops | bytes accessed | tf_op | source)
XLA Modules:
  0.0 182.0 jit_solution(12435272503436552744)
XLA Ops:
  8.6 3.7 %shard_map.95 = (f32[272,512]{1,0:T(8,128)}, f32[272,512]{1,0:T(8,128)}) custom-call(s32[1,1]{1,0:T(1,128)S(6)} %copy.10.live, f32[32,512]{1,0:T(8,128)} %bitcast.19, f32[512,512]{1,0:T(8,128)} %bitcast.13, f32[512,512]{1,0:T(8,128)} %bitcast.18), custom_call_target="tpu_custom_call" | custom-call | flops 805306368 | bytes 4194304 | tf_op jit(solution)/shard_map/pallas_call | solution.py:305
  12.3 3.4 %collective-permute-start.2 = (f32[272,512]{1,0:T(8,128)}, f32[272,512]{1,0:T(8,128)S(1)}, u32[]{:S(2)}, u32[]{:S(2)}) collective-permute-start(f32[272,512]{1,0:T(8,128)} %get-tuple-element.25.a0), channel_id=1, source_target_pairs={{0,1},{1,2},{2,3},{3,0},{4,5},{5,6},{6,7},{7,4},{8,9},{9,10},{10,1... | collective-permute-start | bytes 1671176 | tf_op jit(solution)/shard_map/ppermute | solution.py:288
  15.7 3.7 %collective-permute-start.1 = (f32[272,512]{1,0:T(8,128)}, f32[272,512]{1,0:T(8,128)S(1)}, u32[]{:S(2)}, u32[]{:S(2)}) collective-permute-start(f32[272,512]{1,0:T(8,128)} %get-tuple-element.26.b0), channel_id=1, source_target_pairs={{0,3},{1,0},{2,1},{3,2},{4,7},{5,4},{6,5},{7,6},{8,11},{9,8},{10,9... | collective-permute-start | bytes 1671176 | tf_op jit(solution)/shard_map/ppermute | solution.py:288
  19.4 3.5 %collective-permute-start = (f32[272,512]{1,0:T(8,128)}, f32[272,512]{1,0:T(8,128)S(1)}, u32[]{:S(2)}, u32[]{:S(2)}) collective-permute-start(f32[272,512]{1,0:T(8,128)} %get-tuple-element.25.a0), channel_id=1, source_target_pairs={{0,3},{1,0},{2,1},{3,2},{4,7},{5,4},{6,5},{7,6},{8,11},{9,8},{10,9... | collective-permute-start | bytes 1671176 | tf_op jit(solution)/shard_map/ppermute | solution.py:288
  25.2 5.9 %collective-permute-done.2.a3 = f32[272,512]{1,0:T(8,128)S(1)} collective-permute-done((f32[272,512]{1,0:T(8,128)}, f32[272,512]{1,0:T(8,128)S(1)}, u32[]{:S(2)}, u32[]{:S(2)}) %collective-permute-start.2) | collective-permute-done | bytes 557088 | tf_op jit(solution)/shard_map/ppermute | solution.py:288
  33.4 4.9 %collective-permute-start.5 = (f32[272,512]{1,0:T(8,128)S(1)}, f32[272,512]{1,0:T(8,128)S(1)}, u32[]{:S(2)}, u32[]{:S(2)}) collective-permute-start(f32[272,512]{1,0:T(8,128)S(1)} %collective-permute-done.1.b1), channel_id=1, source_target_pairs={{0,3},{1,0},{2,1},{3,2},{4,7},{5,4},{6,5},{7,6},{8,11},{9,8},{10,9... | collective-permute-start | bytes 1671176 | tf_op jit(solution)/shard_map/ppermute | solution.py:288
  38.2 7.1 %collective-permute-done.a1 = f32[272,512]{1,0:T(8,128)S(1)} collective-permute-done((f32[272,512]{1,0:T(8,128)}, f32[272,512]{1,0:T(8,128)S(1)}, u32[]{:S(2)}, u32[]{:S(2)}) %collective-permute-start) | collective-permute-done | bytes 557088 | tf_op jit(solution)/shard_map/ppermute | solution.py:288
  49.0 4.8 %collective-permute-done.4.a2 = f32[272,512]{1,0:T(8,128)S(1)} collective-permute-done((f32[272,512]{1,0:T(8,128)S(1)}, f32[272,512]{1,0:T(8,128)S(1)}, u32[]{:S(2)}, u32[]{:S(2)}) %collective-permute-start.4) | collective-permute-done | bytes 557088 | tf_op jit(solution)/shard_map/ppermute | solution.py:288
  57.3 3.5 %collective-permute-start.6 = (f32[32,512]{1,0:T(8,128)S(1)}, f32[32,512]{1,0:T(8,128)S(1)}, u32[]{:S(2)}, u32[]{:S(2)}) collective-permute-start(f32[32,512]{1,0:T(8,128)S(1)} %get-tuple-element.31.base), channel_id=1, source_target_pairs={{0,4},{1,5},{2,6},{3,7},{4,8},{5,9},{6,10},{7,11},{8,12},{9,13},{1... | collective-permute-start | bytes 196616 | tf_op jit(solution)/shard_map/ppermute | solution.py:298
  60.8 3.2 %shard_map.98 = (bf16[512,512]{1,0:T(8,128)(2,1)S(1)}, bf16[512,512]{1,0:T(8,128)(2,1)S(1)}, bf16[512,512]{1,0:T(8,128)(2,1)S(1)}, bf16[512,512]{1,0:T(8,128)(2,1)S(1)}) custom-call(s32[1]{0:T(128)} %bitcast.place, bf16[4,512,512]{2,1,0:T(8,128)(2,1)S(1)} %get-tuple-element.32.nh, bf16[4,512,512]{2,1,0:T(8,128)(2,1)S(1)} %get-tuple-element.33.nl), custom_call_target="tpu_custom_call" | custom-call | flops 2415919104 | bytes 6291456 | tf_op jit(solution)/shard_map/pallas_call | solution.py:340
  68.2 3.5 %collective-permute-start.7 = (f32[32,512]{1,0:T(8,128)S(1)}, f32[32,512]{1,0:T(8,128)S(1)}, u32[]{:S(2)}, u32[]{:S(2)}) collective-permute-start(f32[32,512]{1,0:T(8,128)S(1)} %shard_map.99), channel_id=1, source_target_pairs={{0,4},{1,5},{2,6},{3,7},{4,8},{5,9},{6,10},{7,11},{8,12},{9,13},{1... | collective-permute-start | bytes 196616 | tf_op jit(solution)/shard_map/ppermute | solution.py:298
  71.7 2.7 %collective-permute-done.7.coming = f32[32,512]{1,0:T(8,128)S(1)} collective-permute-done((f32[32,512]{1,0:T(8,128)S(1)}, f32[32,512]{1,0:T(8,128)S(1)}, u32[]{:S(2)}, u32[]{:S(2)}) %collective-permute-start.7) | collective-permute-done | bytes 65568 | tf_op jit(solution)/shard_map/ppermute | solution.py:298
  74.8 3.5 %collective-permute-start.8 = (f32[32,512]{1,0:T(8,128)S(1)}, f32[32,512]{1,0:T(8,128)S(1)}, u32[]{:S(2)}, u32[]{:S(2)}) collective-permute-start(f32[32,512]{1,0:T(8,128)S(1)} %shard_map.100), channel_id=1, source_target_pairs={{0,4},{1,5},{2,6},{3,7},{4,8},{5,9},{6,10},{7,11},{8,12},{9,13},{1... | collective-permute-start | bytes 196616 | tf_op jit(solution)/shard_map/ppermute | solution.py:298
  85.1 17.9 %all_to_all.20.pieces = f32[32,8,128]{2,1,0:T(8,128)S(1)} all-to-all(f32[32,8,128]{2,1,0:T(8,128)S(1)} %get-tuple-element.39), channel_id=1, replica_groups=mesh['gz'=16,'ga'=32] {'ga'}, dimensions={0} | all-to-all | bytes 262144 | tf_op jit(solution)/shard_map/all_to_all | solution.py:369
  103.0 18.2 %all_to_all.21.pieces = f32[16,8,128]{2,1,0:T(8,128)S(1)} all-to-all(f32[16,8,128]{2,1,0:T(8,128)S(1)} %shard_map.102), channel_id=1, replica_groups=mesh['gz'=16,'ga'=32] {'gz'}, dimensions={0} | all-to-all | bytes 131072 | tf_op jit(solution)/shard_map/all_to_all | solution.py:371
  121.3 14.3 %all_to_all.22.tiles = f32[32,8,128]{2,1,0:T(8,128)S(1)} all-to-all(f32[32,8,128]{2,1,0:T(8,128)S(1)} %shard_map.103), channel_id=1, replica_groups=mesh['gz'=16,'ga'=32] {'ga'}, dimensions={0} | all-to-all | bytes 262144 | tf_op jit(solution)/shard_map/all_to_all | solution.py:373
  140.2 3.8 %shard_map.105 = (f32[32,1024]{1,0:T(8,128)}, f32[4,32,512]{2,1,0:T(8,128)S(1)}) custom-call(f32[32,8,128]{2,1,0:T(8,128)S(1)} %all_to_all.22.tiles, f32[32,1024]{1,0:T(8,128)S(1)} %copy-done.14, f32[4,32,4608]{2,1,0:T(8,128)S(1)} %bitcast.9, f32[256,512]{1,0:T(8,128)S(1)} %bitcast.11, s32[1,256]{1,0:T(1,128)S(1)} %bitcast.16, f32[32,512]{1,0:T(8,128)S(1)} %copy-done.16), custom_call_target="tpu_custom_call" | custom-call | flops 402653184 | tf_op jit(solution)/shard_map/pallas_call | solution.py:375
  144.0 9.1 %all_to_all.23.reduced = f32[4,32,512]{2,1,0:T(8,128)S(1)} all-to-all(f32[4,32,512]{2,1,0:T(8,128)S(1)} %get-tuple-element.44), channel_id=1, replica_groups={{0,1,2,3},{4,5,6,7},{8,9,10,11},{12,13,14,15},{16,17,18,19},{20,21,22,2..., dimensions={0} | all-to-all | bytes 524288 | tf_op jit(solution)/shard_map/all_to_all | solution.py:390
  154.2 3.2 %collective-permute-start.9 = (f32[32,512]{1,0:T(8,128)S(1)}, f32[32,512]{1,0:T(8,128)S(1)}, u32[]{:S(2)}, u32[]{:S(2)}) collective-permute-start(f32[32,512]{1,0:T(8,128)S(1)} %get-tuple-element.46.base), channel_id=1, source_target_pairs={{4,0},{5,1},{6,2},{7,3},{8,4},{9,5},{10,6},{11,7},{12,8},{13,9},{1... | collective-permute-start | bytes 196616 | tf_op jit(solution)/shard_map/ppermute | solution.py:298
  157.4 3.1 %collective-permute-done.9.coming = f32[32,512]{1,0:T(8,128)S(1)} collective-permute-done((f32[32,512]{1,0:T(8,128)S(1)}, f32[32,512]{1,0:T(8,128)S(1)}, u32[]{:S(2)}, u32[]{:S(2)}) %collective-permute-start.9) | collective-permute-done | bytes 65568 | tf_op jit(solution)/shard_map/ppermute | solution.py:298
  160.8 3.0 %collective-permute-start.10 = (f32[32,512]{1,0:T(8,128)S(1)}, f32[32,512]{1,0:T(8,128)S(1)}, u32[]{:S(2)}, u32[]{:S(2)}) collective-permute-start(f32[32,512]{1,0:T(8,128)S(1)} %shard_map.107), channel_id=1, source_target_pairs={{4,0},{5,1},{6,2},{7,3},{8,4},{9,5},{10,6},{11,7},{12,8},{13,9},{1... | collective-permute-start | bytes 196616 | tf_op jit(solution)/shard_map/ppermute | solution.py:298
  163.8 3.1 %collective-permute-done.10.coming = f32[32,512]{1,0:T(8,128)S(1)} collective-permute-done((f32[32,512]{1,0:T(8,128)S(1)}, f32[32,512]{1,0:T(8,128)S(1)}, u32[]{:S(2)}, u32[]{:S(2)}) %collective-permute-start.10) | collective-permute-done | bytes 65568 | tf_op jit(solution)/shard_map/ppermute | solution.py:298
  167.2 3.0 %collective-permute-start.11 = (f32[32,512]{1,0:T(8,128)S(1)}, f32[32,512]{1,0:T(8,128)S(1)}, u32[]{:S(2)}, u32[]{:S(2)}) collective-permute-start(f32[32,512]{1,0:T(8,128)S(1)} %shard_map.108), channel_id=1, source_target_pairs={{4,0},{5,1},{6,2},{7,3},{8,4},{9,5},{10,6},{11,7},{12,8},{13,9},{1... | collective-permute-start | bytes 196616 | tf_op jit(solution)/shard_map/ppermute | solution.py:298
  170.3 3.1 %collective-permute-done.11.coming = f32[32,512]{1,0:T(8,128)S(1)} collective-permute-done((f32[32,512]{1,0:T(8,128)S(1)}, f32[32,512]{1,0:T(8,128)S(1)}, u32[]{:S(2)}, u32[]{:S(2)}) %collective-permute-start.11) | collective-permute-done | bytes 65568 | tf_op jit(solution)/shard_map/ppermute | solution.py:298
  (61 shorter events, 32.1 us)
Async XLA Ops:
  7.2 58.9 %all-gather.5.cloned.1.call-start = ((), (), s32[]{:S(2)}) async-start(), calls=%async_computation.4 | async-start | bytes 1179648 | tf_op jit(solution)/shard_map/all_gather | solution.py:303
  7.9 127.7 %all-gather.7.cloned.1.call-start = ((), (), s32[]{:S(2)}) async-start(), calls=%async_computation.5 | async-start | bytes 2949120 | tf_op jit(solution)/shard_map/all_gather | solution.py:360
  12.3 18.8 %collective-permute-start.2 = (f32[272,512]{1,0:T(8,128)}, f32[272,512]{1,0:T(8,128)S(1)}, u32[]{:S(2)}, u32[]{:S(2)}) collective-permute-start(f32[272,512]{1,0:T(8,128)} %get-tuple-element.25.a0), channel_id=1, source_target_pairs={{0,1},{1,2},{2,3},{3,0},{4,5},{5,6},{6,7},{7,4},{8,9},{9,10},{10,1... | collective-permute-start | bytes 1671176 | tf_op jit(solution)/shard_map/ppermute | solution.py:288
  15.7 17.7 %collective-permute-start.1 = (f32[272,512]{1,0:T(8,128)}, f32[272,512]{1,0:T(8,128)S(1)}, u32[]{:S(2)}, u32[]{:S(2)}) collective-permute-start(f32[272,512]{1,0:T(8,128)} %get-tuple-element.26.b0), channel_id=1, source_target_pairs={{0,3},{1,0},{2,1},{3,2},{4,7},{5,4},{6,5},{7,6},{8,11},{9,8},{10,9... | collective-permute-start | bytes 1671176 | tf_op jit(solution)/shard_map/ppermute | solution.py:288
  19.4 25.9 %collective-permute-start = (f32[272,512]{1,0:T(8,128)}, f32[272,512]{1,0:T(8,128)S(1)}, u32[]{:S(2)}, u32[]{:S(2)}) collective-permute-start(f32[272,512]{1,0:T(8,128)} %get-tuple-element.25.a0), channel_id=1, source_target_pairs={{0,3},{1,0},{2,1},{3,2},{4,7},{5,4},{6,5},{7,6},{8,11},{9,8},{10,9... | collective-permute-start | bytes 1671176 | tf_op jit(solution)/shard_map/ppermute | solution.py:288
  22.8 22.5 %collective-permute-start.3 = (f32[272,512]{1,0:T(8,128)}, f32[272,512]{1,0:T(8,128)}, u32[]{:S(2)}, u32[]{:S(2)}) collective-permute-start(f32[272,512]{1,0:T(8,128)} %get-tuple-element.26.b0), channel_id=1, source_target_pairs={{0,1},{1,2},{2,3},{3,0},{4,5},{5,6},{6,7},{7,4},{8,9},{9,10},{10,1... | collective-permute-start | bytes 1671176 | tf_op jit(solution)/shard_map/ppermute | solution.py:288
  31.1 22.7 %collective-permute-start.4 = (f32[272,512]{1,0:T(8,128)S(1)}, f32[272,512]{1,0:T(8,128)S(1)}, u32[]{:S(2)}, u32[]{:S(2)}) collective-permute-start(f32[272,512]{1,0:T(8,128)S(1)} %collective-permute-done.2.a3), channel_id=1, source_target_pairs={{0,1},{1,2},{2,3},{3,0},{4,5},{5,6},{6,7},{7,4},{8,9},{9,10},{10,1... | collective-permute-start | bytes 1671176 | tf_op jit(solution)/shard_map/ppermute | solution.py:288
  33.4 22.4 %collective-permute-start.5 = (f32[272,512]{1,0:T(8,128)S(1)}, f32[272,512]{1,0:T(8,128)S(1)}, u32[]{:S(2)}, u32[]{:S(2)}) collective-permute-start(f32[272,512]{1,0:T(8,128)S(1)} %collective-permute-done.1.b1), channel_id=1, source_target_pairs={{0,3},{1,0},{2,1},{3,2},{4,7},{5,4},{6,5},{7,6},{8,11},{9,8},{10,9... | collective-permute-start | bytes 1671176 | tf_op jit(solution)/shard_map/ppermute | solution.py:288
  45.3 1.1 copy-start.8
  46.4 1.1 copy-start.9
  57.3 6.7 %copy-start = (bf16[4,512,512]{2,1,0:T(8,128)(2,1)}, bf16[4,512,512]{2,1,0:T(8,128)(2,1)S(1)}, u32[]{:S(2)}) copy-start(bf16[4,512,512]{2,1,0:T(8,128)(2,1)S(1)} %get-tuple-element.33.nl) | copy-start | bytes 6291460
  57.3 8.3 %collective-permute-start.6 = (f32[32,512]{1,0:T(8,128)S(1)}, f32[32,512]{1,0:T(8,128)S(1)}, u32[]{:S(2)}, u32[]{:S(2)}) collective-permute-start(f32[32,512]{1,0:T(8,128)S(1)} %get-tuple-element.31.base), channel_id=1, source_target_pairs={{0,4},{1,5},{2,6},{3,7},{4,8},{5,9},{6,10},{7,11},{8,12},{9,13},{1... | collective-permute-start | bytes 196616 | tf_op jit(solution)/shard_map/ppermute | solution.py:298
  65.6 15.3 %copy-start.17 = (s32[1,1,256]{2,1,0:T(1,128)S(1)}, s32[1,1,256]{2,1,0:T(1,128)}, u32[]{:S(2)}) copy-start(s32[1,1,256]{2,1,0:T(1,128)} %param.12) | copy-start | bytes 3076
  66.1 1.2 copy-start.6
  68.2 6.2 %collective-permute-start.7 = (f32[32,512]{1,0:T(8,128)S(1)}, f32[32,512]{1,0:T(8,128)S(1)}, u32[]{:S(2)}, u32[]{:S(2)}) collective-permute-start(f32[32,512]{1,0:T(8,128)S(1)} %shard_map.99), channel_id=1, source_target_pairs={{0,4},{1,5},{2,6},{3,7},{4,8},{5,9},{6,10},{7,11},{8,12},{9,13},{1... | collective-permute-start | bytes 196616 | tf_op jit(solution)/shard_map/ppermute | solution.py:298
  74.8 6.2 %collective-permute-start.8 = (f32[32,512]{1,0:T(8,128)S(1)}, f32[32,512]{1,0:T(8,128)S(1)}, u32[]{:S(2)}, u32[]{:S(2)}) collective-permute-start(f32[32,512]{1,0:T(8,128)S(1)} %shard_map.100), channel_id=1, source_target_pairs={{0,4},{1,5},{2,6},{3,7},{4,8},{5,9},{6,10},{7,11},{8,12},{9,13},{1... | collective-permute-start | bytes 196616 | tf_op jit(solution)/shard_map/ppermute | solution.py:298
  80.9 1.0 copy-start.4
  85.1 36.1 %copy-start.15 = (f32[32,512]{1,0:T(8,128)}, f32[32,512]{1,0:T(8,128)S(1)}, u32[]{:S(2)}) copy-start(f32[32,512]{1,0:T(8,128)S(1)} %get-tuple-element.43.solved) | copy-start | bytes 196612
  135.6 17.5 %copy-start.1 = (bf16[4,512,512]{2,1,0:T(8,128)(2,1)S(1)}, bf16[4,512,512]{2,1,0:T(8,128)(2,1)}, u32[]{:S(2)}) copy-start(bf16[4,512,512]{2,1,0:T(8,128)(2,1)} %copy-done) | copy-start | bytes 6291460
  135.6 1.8 copy-start.3
  154.2 19.2 %copy-start.7 = (f32[1,1,512,512]{3,2,1,0:T(8,128)S(1)}, f32[1,1,512,512]{3,2,1,0:T(8,128)}, u32[]{:S(2)}) copy-start(f32[1,1,512,512]{3,2,1,0:T(8,128)} %param.9) | copy-start | bytes 3145732
  154.2 6.3 %collective-permute-start.9 = (f32[32,512]{1,0:T(8,128)S(1)}, f32[32,512]{1,0:T(8,128)S(1)}, u32[]{:S(2)}, u32[]{:S(2)}) collective-permute-start(f32[32,512]{1,0:T(8,128)S(1)} %get-tuple-element.46.base), channel_id=1, source_target_pairs={{4,0},{5,1},{6,2},{7,3},{8,4},{9,5},{10,6},{11,7},{12,8},{13,9},{1... | collective-permute-start | bytes 196616 | tf_op jit(solution)/shard_map/ppermute | solution.py:298
  160.8 6.2 %collective-permute-start.10 = (f32[32,512]{1,0:T(8,128)S(1)}, f32[32,512]{1,0:T(8,128)S(1)}, u32[]{:S(2)}, u32[]{:S(2)}) collective-permute-start(f32[32,512]{1,0:T(8,128)S(1)} %shard_map.107), channel_id=1, source_target_pairs={{4,0},{5,1},{6,2},{7,3},{8,4},{9,5},{10,6},{11,7},{12,8},{13,9},{1... | collective-permute-start | bytes 196616 | tf_op jit(solution)/shard_map/ppermute | solution.py:298
  167.2 6.2 %collective-permute-start.11 = (f32[32,512]{1,0:T(8,128)S(1)}, f32[32,512]{1,0:T(8,128)S(1)}, u32[]{:S(2)}, u32[]{:S(2)}) collective-permute-start(f32[32,512]{1,0:T(8,128)S(1)} %shard_map.108), channel_id=1, source_target_pairs={{4,0},{5,1},{6,2},{7,3},{8,4},{9,5},{10,6},{11,7},{12,8},{13,9},{1... | collective-permute-start | bytes 196616 | tf_op jit(solution)/shard_map/ppermute | solution.py:298
  (8 other events, 7.3 us)
Sparse Core Ops, SparseCore 0:
  10.1 45.2 all-gather.4
  68.3 43.3 all-gather.6

commit v3 on v2

--- a/solution.py
+++ b/solution.py
@@ -29,6 +29,10 @@
     rows = left[0].shape[0]
     both = bdot(jnp.concatenate(left, 0), right[0], dims)
     return both[:rows] + both[rows:] + bdot(left[0], right[1], dims)
+
+
+def place_in_row():
+    return lax.rem(lax.axis_index("ga"), ROW)
 
 
 def kernel_call(body, outs, ins, scratch=(), flops=0, nbytes=0, limit=16):
@@ -107,8 +111,8 @@
         place_block(a, b, slot, nh, nl, group)
 
 
-def assemble(place, sh, sl, sgroup, a2, b2, nh, nl, group, last):
-    here = place[0]
+def assemble(sh, sl, sgroup, a2, b2, nh, nl, group, last):
+    here = place_in_row()
     for at, offset in enumerate((0, 1, 3)):
         slot = lax.rem(here + offset, ROW)
         nh[slot] = sh[at]
@@ -122,8 +126,8 @@
     last[...] = value
 
 
-def multiply_up(place, nh, nl, qh, ql, ph, plow):
-    here = place[0]
+def multiply_up(nh, nl, qh, ql, ph, plow):
+    here = place_in_row()
     high, low = nh[0], nl[0]
 
     @pl.when(here == 0)
@@ -155,8 +159,8 @@
     return (lax.broadcasted_iota(jnp.int32, (top, rows.shape[1]), 0) == rows[...]).astype(F32).astype(BF16)
 
 
-def contribute(place, group, coming, qh, ql, across, rows, solved, tiles):
-    here = place[0]
+def contribute(group, coming, qh, ql, across, rows, top_right, solved, tiles):
+    here = place_in_row()
     value = group[here] + dot3(split(coming[...]), (qh[...], ql[...]), NT)
     solved[...] = value
     pushed = dot3(split(value), split(across[...]), NT)
@@ -165,6 +169,8 @@
     high, low = split(pushed)
     both = bdot(jnp.concatenate((high, low), 0), onehot_of(rows, col_blocks * lanes), NT)
     total = both[: value.shape[0]] + both[value.shape[0] :]
+    first = (lax.axis_index("gz") == 0) & (lax.axis_index("ga") == 0)
+    total = jnp.where(first, top_right[...] - total, -total)
     for tile in range(count):
         r, c = tile // col_blocks, tile % col_blocks
         tiles[tile] = total[r * depth : (r + 1) * depth, c * lanes : (c + 1) * lanes]
@@ -178,35 +184,20 @@
         out[piece] = value
 
 
-def solve_top(
-    tiles, top_right, packed_hbm, across_hbm, rows, solved, top_out, reduced, packed, across, wh, wl, sems
-):
+def solve_top(tiles, packed, top_out, wh, wl):
     count, depth, lanes = tiles.shape
-    rhs, top = top_right.shape
+    rhs, top = top_out.shape
     col_blocks = top // lanes
     steps = packed.shape[1] * packed.shape[0]
-    moves = []
-    start = 0
-    for step in range(top // steps):
-        wide = (step + 1) * steps
-        part = (slice(None), slice(None), pl.ds(start, wide))
-        moves.append(
-            pltpu.make_async_copy(packed_hbm.at[part], packed.at[part], sems.at[step])
-        )
-        start += wide
-    moves.append(pltpu.make_async_copy(across_hbm, across, sems.at[top // steps]))
-    for move in moves:
-        move.start()
     lines = []
     for r in range(rhs // depth):
         lines.append(jnp.concatenate([tiles[r * col_blocks + c] for c in range(col_blocks)], 1))
-    rest = split(top_right[...] - jnp.concatenate(lines, 0))
+    rest = split(jnp.concatenate(lines, 0))
     block = 2 * steps
     mid = []
     start = 0
     for step in range(top // steps):
         wide = (step + 1) * steps
-        moves[step].wait()
         high, low = split(packed[:, :, start : start + wide].reshape(steps, wide))
         at = slice(step * steps, (step + 1) * steps)
         wh[at, :wide] = high
@@ -227,19 +218,21 @@
         answer.append(
             dot3((mid[0][:, j:], mid[1][:, j:]), (wh[j:, j:end], wl[j:, j:end]), NN)
         )
-    answer = jnp.concatenate(answer, 1)
-    top_out[...] = answer
-    high, low = split(answer)
+    top_out[...] = jnp.concatenate(answer, 1)
+
+
+def lift(top_out, across, rows, solved, reduced):
+    rhs, top = top_out.shape
+    high, low = split(top_out[...])
     both = bdot(jnp.concatenate((high, low), 0), onehot_of(rows, top), NN)
     lifted = both[:rhs] + both[rhs:]
-    moves[-1].wait()
     value = solved[...] - dot3(split(lifted), split(across[...]), NN)
     for piece in range(reduced.shape[0]):
         reduced[piece] = value
 
 
-def row_backward(place, reduced, nh, nl, own, sent):
-    here = place[0]
+def row_backward(reduced, nh, nl, own, sent):
+    here = place_in_row()
     value = reduced[ROW - 1]
     for j in range(ROW - 1, -1, -1):
         if j < ROW - 1:
@@ -253,8 +246,8 @@
     sent[...] = value
 
 
-def finish(place, live, own, coming, nh, nl, inverse, out, term):
-    here = place[0]
+def finish(live, own, coming, nh, nl, inverse, out, term):
+    here = place_in_row()
     term[...] = coming[...]
     for j in range(ROW - 1, 0, -1):
 
@@ -274,8 +267,6 @@
     ga, gz = lax.axis_size("ga"), lax.axis_size("gz")
     chain_len = ga // BRANCHES
     chain_rows = chain_len // ROW
-    index = lax.axis_index("ga")
-    place = (index % ROW).astype(jnp.int32)[None]
     right, inverse = right_sides[0, 0], diag_inverse[0, 0]
     coupling, across = chain_block[0, 0], top_block[0, 0]
     rows = top_rows[0]
@@ -300,7 +291,6 @@
     def pair(*dims):
         return (shape(*dims, kind=BF16), shape(*dims, kind=BF16))
 
-    blocks = lax.all_gather(top_inverse, "ga", axis_index_groups=y_groups)
     half = width // 2 + rhs // 2
     a0, b0 = kernel_call(
         prepare,
@@ -316,6 +306,8 @@
         nbytes=16 * width**2,
         limit=60,
     )(live_cols, right, inverse, coupling)
+    top_inverse, a0 = lax.optimization_barrier((top_inverse, a0))
+    blocks = lax.all_gather(top_inverse, "ga", axis_index_groups=y_groups)
     a3 = ring(a0, 1)
     b1 = ring(b0, -1)
     b3 = ring(b0, 1)
@@ -332,68 +324,64 @@
     nh, nl, group, last = kernel_call(
         assemble,
         pair(ROW, width, width) + (shape(ROW, rhs, width), shape(rhs, width)),
-        [SMEM] + [VMEM] * 5,
+        [VMEM] * 5,
         flops=24 * rhs * width**2,
         nbytes=32 * width**2,
-    )(place, *staged, a2, b2)
+    )(*staged, a2, b2)
     coming = hop(last, 1)
     qh, ql, ph, plow = kernel_call(
         multiply_up,
         pair(width, width) * 2,
-        [SMEM, VMEM, VMEM],
+        [VMEM, VMEM],
         flops=18 * width**3,
         nbytes=24 * width**2,
-    )(place, nh, nl)
-    for step in range(chain_rows - 2):
-        moved = kernel_call(
-            hop_forward, shape(rhs, width), [VMEM] * 4, flops=6 * rhs * width**2
-        )(last, coming, ph, plow)
-        if step == 0:
-            blocks, moved = lax.optimization_barrier((blocks, moved))
-        coming = hop(moved, 1)
+    )(nh, nl)
+    blocks, coming, plow = lax.optimization_barrier((blocks, coming, plow))
     packed = kernel_call(
         pack_lower,
         shape(top_inverse.shape[0], top * (ga // ROW + 1) // 2),
         [VMEM],
         nbytes=2 * top**2,
     )(blocks)
+    packed, coming = lax.optimization_barrier((packed, coming))
     packed = lax.all_gather(packed, "ga", axis_index_groups=x_groups)
+    for _ in range(chain_rows - 2):
+        moved = kernel_call(
+            hop_forward, shape(rhs, width), [VMEM] * 4, flops=6 * rhs * width**2
+        )(last, coming, ph, plow)
+        coming = hop(moved, 1)
 
     tiles = (ga, rhs * top // ga // 128, 128)
     solved, partial = kernel_call(
         contribute,
         (shape(rhs, width), shape(*tiles)),
-        [SMEM] + [VMEM] * 6,
+        [VMEM] * 7,
         flops=12 * rhs * width**2,
-    )(place, group, coming, qh, ql, across, rows)
+    )(group, coming, qh, ql, across, rows, top_right)
     partial = lax.all_to_all(partial, "ga", 0, 0)
     partial = kernel_call(total_of, shape(gz, *tiles[1:]), [VMEM])(partial)
     partial = lax.all_to_all(partial, "gz", 0, 0)
     partial = kernel_call(total_of, shape(*tiles), [VMEM])(partial)
     partial = lax.all_to_all(partial, "ga", 0, 0)
     partial, packed = lax.optimization_barrier((partial, packed))
-    top_solution, reduced = kernel_call(
+    top_solution = kernel_call(
         solve_top,
-        (shape(rhs, top), shape(ROW, rhs, width)),
-        [VMEM, VMEM, HBM, HBM, VMEM, VMEM],
-        scratch=[
-            pltpu.VMEM(packed.shape, F32),
-            pltpu.VMEM(across.shape, F32),
-            pltpu.VMEM((top, top), BF16),
-            pltpu.VMEM((top, top), BF16),
-            pltpu.SemaphoreType.DMA((ga // ROW + 1,)),
-        ],
+        shape(rhs, top),
+        [VMEM] * 2,
+        scratch=[pltpu.VMEM((top, top), BF16), pltpu.VMEM((top, top), BF16)],
         flops=12 * rhs * top**2,
-        limit=24,
-    )(partial, top_right, packed, across, rows, solved)
+    )(partial, packed)
+    reduced = kernel_call(
+        lift, shape(ROW, rhs, width), [VMEM] * 4, flops=6 * rhs * top * width
+    )(top_solution, across, rows, solved)
 
     reduced = lax.all_to_all(reduced, "ga", 0, 0, axis_index_groups=x_groups)
     own, sent = kernel_call(
         row_backward,
         (shape(rhs, width), shape(rhs, width)),
-        [SMEM] + [VMEM] * 3,
+        [VMEM] * 3,
         flops=24 * rhs * width**2,
-    )(place, reduced, nh, nl)
+    )(reduced, nh, nl)
     coming = hop(sent, -1)
     for _ in range(chain_rows - 2):
         moved = kernel_call(
@@ -403,10 +391,10 @@
     result = kernel_call(
         finish,
         shape(rhs, width),
-        [SMEM, SMEM] + [VMEM] * 5,
+        [SMEM] + [VMEM] * 5,
         scratch=[pltpu.VMEM((rhs, width), F32)],
         flops=24 * rhs * width**2,
-    )(place, live_cols, own, coming, nh, nl, inverse)
+    )(live_cols, own, coming, nh, nl, inverse)
     return (result[None, None], top_solution)
 
 

time: 183 us -> 176 us (0.962)
  local copies, waits for them, and re-layouts: 13.5 us -> 8.53 us
  Pallas kernels: 19.3 us -> 17.2 us
    unnamed x36 -> x34, local copies, waits for them, and re-layouts: 13.5 us -> 8.53 us
    pallas_call x5 -> x6, Pallas kernels: 11.1 us -> 10 us  [the longest x1 3.21 us: shards(): kernel_call(multiply_up, pair(width, width) * 2, [VMEM, VMEM], flops=18 *...]
  transfers between devices with their start and end apart: 14 -> 14, of which waited for: 9 -> 9; matrix products, arithmetic and copies ran while one was open for 0% -> 0% of each run, Pallas kernels for 7% -> 4%
where the time goes in v3:
time: 176 us; the launch traced here: 175 us
  blocking collectives  59.3 us (34%)
  starting transfers between devices  39.9 us (23%)
  waiting for transfers between devices  35.5 us (20%)
  Pallas kernels  17.2 us (10%)
  between operations  14.9 us (8%)
  local copies, waits for them, and re-layouts  8.53 us (5%)
    all_to_all x2, blocking collectives, shards(): partial = lax.all_to_all(partial, 'ga', 0, 0)  32.2 us
    ppermute x6, waiting for transfers between devices, ring(): lax.ppermute(value, 'ga', [(i, i // ROW * ROW + (i + step) % ROW) for i i...  20.8 us
    ppermute x6, starting transfers between devices, ring(): lax.ppermute(value, 'ga', [(i, i // ROW * ROW + (i + step) % ROW) for i i...  19.9 us
    ppermute x6, starting transfers between devices, hop(): return lax.ppermute(value, 'ga', route)  19.9 us
    all_to_all x1, blocking collectives, shards(): partial = lax.all_to_all(partial, 'gz', 0, 0)  18.1 us
    ppermute x6, waiting for transfers between devices, hop(): return lax.ppermute(value, 'ga', route)  14.7 us
    all_to_all x1, blocking collectives, shards(): reduced = lax.all_to_all(reduced, 'ga', 0, 0, axis_index_groups=x_groups)  9.07 us
    unnamed x34, local copies, waits for them, and re-layouts  8.53 us
  transfers between devices with their start and end apart: 14, of which 9 were waited for; matrix products, arithmetic and copies ran while one was open for 0% of the time, Pallas kernels for 4%

profile of v3, /device:TPU:8, one launch (start us, length us, event | category | flops | bytes accessed | tf_op | source)
XLA Modules:
  0.0 175.4 jit_solution(6154195583083463525)
XLA Ops:
  7.9 3.7 %shard_map.95 = (f32[272,512]{1,0:T(8,128)}, f32[272,512]{1,0:T(8,128)}) custom-call(s32[1,1]{1,0:T(1,128)S(6)} %copy.10.live, f32[32,512]{1,0:T(8,128)} %bitcast.18, f32[512,512]{1,0:T(8,128)} %bitcast.12, f32[512,512]{1,0:T(8,128)} %bitcast.17), custom_call_target="tpu_custom_call" | custom-call | flops 805306368 | bytes 4194304 | tf_op jit(solution)/shard_map/pallas_call | solution.py:295
  11.6 3.4 %collective-permute-start.2 = (f32[272,512]{1,0:T(8,128)}, f32[272,512]{1,0:T(8,128)S(1)}, u32[]{:S(2)}, u32[]{:S(2)}) collective-permute-start(f32[272,512]{1,0:T(8,128)} %get-tuple-element.29.a0), channel_id=1, source_target_pairs={{0,1},{1,2},{2,3},{3,0},{4,5},{5,6},{6,7},{7,4},{8,9},{9,10},{10,1... | collective-permute-start | bytes 1671176 | tf_op jit(solution)/shard_map/ppermute | solution.py:279
  15.0 3.7 %collective-permute-start.1 = (f32[272,512]{1,0:T(8,128)}, f32[272,512]{1,0:T(8,128)S(1)}, u32[]{:S(2)}, u32[]{:S(2)}) collective-permute-start(f32[272,512]{1,0:T(8,128)} %get-tuple-element.30.b0), channel_id=1, source_target_pairs={{0,3},{1,0},{2,1},{3,2},{4,7},{5,4},{6,5},{7,6},{8,11},{9,8},{10,9... | collective-permute-start | bytes 1671176 | tf_op jit(solution)/shard_map/ppermute | solution.py:279
  18.7 3.5 %collective-permute-start = (f32[272,512]{1,0:T(8,128)}, f32[272,512]{1,0:T(8,128)S(1)}, u32[]{:S(2)}, u32[]{:S(2)}) collective-permute-start(f32[272,512]{1,0:T(8,128)} %get-tuple-element.29.a0), channel_id=1, source_target_pairs={{0,3},{1,0},{2,1},{3,2},{4,7},{5,4},{6,5},{7,6},{8,11},{9,8},{10,9... | collective-permute-start | bytes 1671176 | tf_op jit(solution)/shard_map/ppermute | solution.py:279
  24.6 5.9 %collective-permute-done.2.a3 = f32[272,512]{1,0:T(8,128)S(1)} collective-permute-done((f32[272,512]{1,0:T(8,128)}, f32[272,512]{1,0:T(8,128)S(1)}, u32[]{:S(2)}, u32[]{:S(2)}) %collective-permute-start.2) | collective-permute-done | bytes 557088 | tf_op jit(solution)/shard_map/ppermute | solution.py:279
  32.7 4.9 %collective-permute-start.5 = (f32[272,512]{1,0:T(8,128)S(1)}, f32[272,512]{1,0:T(8,128)S(1)}, u32[]{:S(2)}, u32[]{:S(2)}) collective-permute-start(f32[272,512]{1,0:T(8,128)S(1)} %collective-permute-done.1.b1), channel_id=1, source_target_pairs={{0,3},{1,0},{2,1},{3,2},{4,7},{5,4},{6,5},{7,6},{8,11},{9,8},{10,9... | collective-permute-start | bytes 1671176 | tf_op jit(solution)/shard_map/ppermute | solution.py:279
  37.6 7.1 %collective-permute-done.a1 = f32[272,512]{1,0:T(8,128)S(1)} collective-permute-done((f32[272,512]{1,0:T(8,128)}, f32[272,512]{1,0:T(8,128)S(1)}, u32[]{:S(2)}, u32[]{:S(2)}) %collective-permute-start) | collective-permute-done | bytes 557088 | tf_op jit(solution)/shard_map/ppermute | solution.py:279
  47.3 5.9 %collective-permute-done.4.a2 = f32[272,512]{1,0:T(8,128)S(1)} collective-permute-done((f32[272,512]{1,0:T(8,128)S(1)}, f32[272,512]{1,0:T(8,128)S(1)}, u32[]{:S(2)}, u32[]{:S(2)}) %collective-permute-start.4) | collective-permute-done | bytes 557088 | tf_op jit(solution)/shard_map/ppermute | solution.py:279
  56.6 3.5 %collective-permute-start.6 = (f32[32,512]{1,0:T(8,128)S(1)}, f32[32,512]{1,0:T(8,128)S(1)}, u32[]{:S(2)}, u32[]{:S(2)}) collective-permute-start(f32[32,512]{1,0:T(8,128)S(1)} %get-tuple-element.35.base), channel_id=1, source_target_pairs={{0,4},{1,5},{2,6},{3,7},{4,8},{5,9},{6,10},{7,11},{8,12},{9,13},{1... | collective-permute-start | bytes 196616 | tf_op jit(solution)/shard_map/ppermute | solution.py:289
  60.1 3.2 %shard_map.98 = (bf16[512,512]{1,0:T(8,128)(2,1)S(1)}, bf16[512,512]{1,0:T(8,128)(2,1)S(1)}, bf16[512,512]{1,0:T(8,128)(2,1)S(1)}, bf16[512,512]{1,0:T(8,128)(2,1)S(1)}) custom-call(bf16[4,512,512]{2,1,0:T(8,128)(2,1)S(1)} %get-tuple-element.37.nh, bf16[4,512,512]{2,1,0:T(8,128)(2,1)S(1)} %get-tuple-element.38.nl), custom_call_target="tpu_custom_call" | custom-call | flops 2415919104 | bytes 6291456 | tf_op jit(solution)/shard_map/pallas_call | solution.py:332
  67.5 3.6 %collective-permute-start.7 = (f32[32,512]{1,0:T(8,128)S(1)}, f32[32,512]{1,0:T(8,128)S(1)}, u32[]{:S(2)}, u32[]{:S(2)}) collective-permute-start(f32[32,512]{1,0:T(8,128)S(1)} %shard_map.100), channel_id=1, source_target_pairs={{0,4},{1,5},{2,6},{3,7},{4,8},{5,9},{6,10},{7,11},{8,12},{9,13},{1... | collective-permute-start | bytes 196616 | tf_op jit(solution)/shard_map/ppermute | solution.py:289
  71.2 2.7 %collective-permute-done.7.coming = f32[32,512]{1,0:T(8,128)S(1)} collective-permute-done((f32[32,512]{1,0:T(8,128)S(1)}, f32[32,512]{1,0:T(8,128)S(1)}, u32[]{:S(2)}, u32[]{:S(2)}) %collective-permute-start.7) | collective-permute-done | bytes 65568 | tf_op jit(solution)/shard_map/ppermute | solution.py:289
  74.2 3.5 %collective-permute-start.8 = (f32[32,512]{1,0:T(8,128)S(1)}, f32[32,512]{1,0:T(8,128)S(1)}, u32[]{:S(2)}, u32[]{:S(2)}) collective-permute-start(f32[32,512]{1,0:T(8,128)S(1)} %shard_map.101), channel_id=1, source_target_pairs={{0,4},{1,5},{2,6},{3,7},{4,8},{5,9},{6,10},{7,11},{8,12},{9,13},{1... | collective-permute-start | bytes 196616 | tf_op jit(solution)/shard_map/ppermute | solution.py:289
  77.7 2.7 %collective-permute-done.8.coming = f32[32,512]{1,0:T(8,128)S(1)} collective-permute-done((f32[32,512]{1,0:T(8,128)S(1)}, f32[32,512]{1,0:T(8,128)S(1)}, u32[]{:S(2)}, u32[]{:S(2)}) %collective-permute-start.8) | collective-permute-done | bytes 65568 | tf_op jit(solution)/shard_map/ppermute | solution.py:289
  81.5 17.9 %all_to_all.20.pieces = f32[32,8,128]{2,1,0:T(8,128)S(1)} all-to-all(f32[32,8,128]{2,1,0:T(8,128)S(1)} %get-tuple-element.47), channel_id=1, replica_groups=mesh['gz'=16,'ga'=32] {'ga'}, dimensions={0} | all-to-all | bytes 262144 | tf_op jit(solution)/shard_map/all_to_all | solution.py:361
  99.4 18.1 %all_to_all.21.pieces = f32[16,8,128]{2,1,0:T(8,128)S(1)} all-to-all(f32[16,8,128]{2,1,0:T(8,128)S(1)} %shard_map.103), channel_id=1, replica_groups=mesh['gz'=16,'ga'=32] {'gz'}, dimensions={0} | all-to-all | bytes 131072 | tf_op jit(solution)/shard_map/all_to_all | solution.py:363
  117.6 14.3 %all_to_all.22.tiles = f32[32,8,128]{2,1,0:T(8,128)S(1)} all-to-all(f32[32,8,128]{2,1,0:T(8,128)S(1)} %shard_map.104), channel_id=1, replica_groups=mesh['gz'=16,'ga'=32] {'ga'}, dimensions={0} | all-to-all | bytes 262144 | tf_op jit(solution)/shard_map/all_to_all | solution.py:365
  137.4 9.1 %all_to_all.23.reduced = f32[4,32,512]{2,1,0:T(8,128)S(1)} all-to-all(f32[4,32,512]{2,1,0:T(8,128)S(1)} %shard_map.106), channel_id=1, replica_groups={{0,1,2,3},{4,5,6,7},{8,9,10,11},{12,13,14,15},{16,17,18,19},{20,21,22,2..., dimensions={0} | all-to-all | bytes 524288 | tf_op jit(solution)/shard_map/all_to_all | solution.py:378
  147.6 3.2 %collective-permute-start.9 = (f32[32,512]{1,0:T(8,128)S(1)}, f32[32,512]{1,0:T(8,128)S(1)}, u32[]{:S(2)}, u32[]{:S(2)}) collective-permute-start(f32[32,512]{1,0:T(8,128)S(1)} %get-tuple-element.53.base), channel_id=1, source_target_pairs={{4,0},{5,1},{6,2},{7,3},{8,4},{9,5},{10,6},{11,7},{12,8},{13,9},{1... | collective-permute-start | bytes 196616 | tf_op jit(solution)/shard_map/ppermute | solution.py:289
  150.8 3.1 %collective-permute-done.9.coming = f32[32,512]{1,0:T(8,128)S(1)} collective-permute-done((f32[32,512]{1,0:T(8,128)S(1)}, f32[32,512]{1,0:T(8,128)S(1)}, u32[]{:S(2)}, u32[]{:S(2)}) %collective-permute-start.9) | collective-permute-done | bytes 65568 | tf_op jit(solution)/shard_map/ppermute | solution.py:289
  154.1 3.0 %collective-permute-start.10 = (f32[32,512]{1,0:T(8,128)S(1)}, f32[32,512]{1,0:T(8,128)S(1)}, u32[]{:S(2)}, u32[]{:S(2)}) collective-permute-start(f32[32,512]{1,0:T(8,128)S(1)} %shard_map.108), channel_id=1, source_target_pairs={{4,0},{5,1},{6,2},{7,3},{8,4},{9,5},{10,6},{11,7},{12,8},{13,9},{1... | collective-permute-start | bytes 196616 | tf_op jit(solution)/shard_map/ppermute | solution.py:289
  157.2 3.1 %collective-permute-done.10.coming = f32[32,512]{1,0:T(8,128)S(1)} collective-permute-done((f32[32,512]{1,0:T(8,128)S(1)}, f32[32,512]{1,0:T(8,128)S(1)}, u32[]{:S(2)}, u32[]{:S(2)}) %collective-permute-start.10) | collective-permute-done | bytes 65568 | tf_op jit(solution)/shard_map/ppermute | solution.py:289
  160.6 3.0 %collective-permute-start.11 = (f32[32,512]{1,0:T(8,128)S(1)}, f32[32,512]{1,0:T(8,128)S(1)}, u32[]{:S(2)}, u32[]{:S(2)}) collective-permute-start(f32[32,512]{1,0:T(8,128)S(1)} %shard_map.109), channel_id=1, source_target_pairs={{4,0},{5,1},{6,2},{7,3},{8,4},{9,5},{10,6},{11,7},{12,8},{13,9},{1... | collective-permute-start | bytes 196616 | tf_op jit(solution)/shard_map/ppermute | solution.py:289
  163.6 3.1 %collective-permute-done.11.coming = f32[32,512]{1,0:T(8,128)S(1)} collective-permute-done((f32[32,512]{1,0:T(8,128)S(1)}, f32[32,512]{1,0:T(8,128)S(1)}, u32[]{:S(2)}, u32[]{:S(2)}) %collective-permute-start.11) | collective-permute-done | bytes 65568 | tf_op jit(solution)/shard_map/ppermute | solution.py:289
  (60 shorter events, 25.5 us)
Async XLA Ops:
  7.2 57.8 %all-gather.5.cloned.1.call-start = ((), (), s32[]{:S(2)}) async-start(), calls=%async_computation.4 | async-start | bytes 1179648 | tf_op jit(solution)/shard_map/all_gather | solution.py:310
  11.6 120.2 %all-gather.7.cloned.1.call-start = ((), (), s32[]{:S(2)}) async-start(), calls=%async_computation.5 | async-start | bytes 2949120 | tf_op jit(solution)/shard_map/all_gather | solution.py:347
  11.6 18.8 %collective-permute-start.2 = (f32[272,512]{1,0:T(8,128)}, f32[272,512]{1,0:T(8,128)S(1)}, u32[]{:S(2)}, u32[]{:S(2)}) collective-permute-start(f32[272,512]{1,0:T(8,128)} %get-tuple-element.29.a0), channel_id=1, source_target_pairs={{0,1},{1,2},{2,3},{3,0},{4,5},{5,6},{6,7},{7,4},{8,9},{9,10},{10,1... | collective-permute-start | bytes 1671176 | tf_op jit(solution)/shard_map/ppermute | solution.py:279
  15.0 17.7 %collective-permute-start.1 = (f32[272,512]{1,0:T(8,128)}, f32[272,512]{1,0:T(8,128)S(1)}, u32[]{:S(2)}, u32[]{:S(2)}) collective-permute-start(f32[272,512]{1,0:T(8,128)} %get-tuple-element.30.b0), channel_id=1, source_target_pairs={{0,3},{1,0},{2,1},{3,2},{4,7},{5,4},{6,5},{7,6},{8,11},{9,8},{10,9... | collective-permute-start | bytes 1671176 | tf_op jit(solution)/shard_map/ppermute | solution.py:279
  18.7 25.9 %collective-permute-start = (f32[272,512]{1,0:T(8,128)}, f32[272,512]{1,0:T(8,128)S(1)}, u32[]{:S(2)}, u32[]{:S(2)}) collective-permute-start(f32[272,512]{1,0:T(8,128)} %get-tuple-element.29.a0), channel_id=1, source_target_pairs={{0,3},{1,0},{2,1},{3,2},{4,7},{5,4},{6,5},{7,6},{8,11},{9,8},{10,9... | collective-permute-start | bytes 1671176 | tf_op jit(solution)/shard_map/ppermute | solution.py:279
  22.2 22.5 %collective-permute-start.3 = (f32[272,512]{1,0:T(8,128)}, f32[272,512]{1,0:T(8,128)S(1)}, u32[]{:S(2)}, u32[]{:S(2)}) collective-permute-start(f32[272,512]{1,0:T(8,128)} %get-tuple-element.30.b0), channel_id=1, source_target_pairs={{0,1},{1,2},{2,3},{3,0},{4,5},{5,6},{6,7},{7,4},{8,9},{9,10},{10,1... | collective-permute-start | bytes 1671176 | tf_op jit(solution)/shard_map/ppermute | solution.py:279
  30.5 22.7 %collective-permute-start.4 = (f32[272,512]{1,0:T(8,128)S(1)}, f32[272,512]{1,0:T(8,128)S(1)}, u32[]{:S(2)}, u32[]{:S(2)}) collective-permute-start(f32[272,512]{1,0:T(8,128)S(1)} %collective-permute-done.2.a3), channel_id=1, source_target_pairs={{0,1},{1,2},{2,3},{3,0},{4,5},{5,6},{6,7},{7,4},{8,9},{9,10},{10,1... | collective-permute-start | bytes 1671176 | tf_op jit(solution)/shard_map/ppermute | solution.py:279
  32.7 22.4 %collective-permute-start.5 = (f32[272,512]{1,0:T(8,128)S(1)}, f32[272,512]{1,0:T(8,128)S(1)}, u32[]{:S(2)}, u32[]{:S(2)}) collective-permute-start(f32[272,512]{1,0:T(8,128)S(1)} %collective-permute-done.1.b1), channel_id=1, source_target_pairs={{0,3},{1,0},{2,1},{3,2},{4,7},{5,4},{6,5},{7,6},{8,11},{9,8},{10,9... | collective-permute-start | bytes 1671176 | tf_op jit(solution)/shard_map/ppermute | solution.py:279
  56.6 6.7 %copy-start = (bf16[4,512,512]{2,1,0:T(8,128)(2,1)}, bf16[4,512,512]{2,1,0:T(8,128)(2,1)S(1)}, u32[]{:S(2)}) copy-start(bf16[4,512,512]{2,1,0:T(8,128)(2,1)S(1)} %get-tuple-element.38.nl) | copy-start | bytes 6291460
  56.6 8.4 %collective-permute-start.6 = (f32[32,512]{1,0:T(8,128)S(1)}, f32[32,512]{1,0:T(8,128)S(1)}, u32[]{:S(2)}, u32[]{:S(2)}) collective-permute-start(f32[32,512]{1,0:T(8,128)S(1)} %get-tuple-element.35.base), channel_id=1, source_target_pairs={{0,4},{1,5},{2,6},{3,7},{4,8},{5,9},{6,10},{7,11},{8,12},{9,13},{1... | collective-permute-start | bytes 196616 | tf_op jit(solution)/shard_map/ppermute | solution.py:289
  66.2 14.2 %copy-start.16 = (s32[1,1,256]{2,1,0:T(1,128)S(1)}, s32[1,1,256]{2,1,0:T(1,128)}, u32[]{:S(2)}) copy-start(s32[1,1,256]{2,1,0:T(1,128)} %param.12) | copy-start | bytes 3076
  67.1 13.3 %copy-start.4 = (f32[1,1,256,512]{3,2,1,0:T(8,128)S(1)}, f32[1,1,256,512]{3,2,1,0:T(8,128)}, u32[]{:S(2)}) copy-start(f32[1,1,256,512]{3,2,1,0:T(8,128)} %param.11) | copy-start | bytes 1572868
  67.1 13.3 %copy-start.11 = (bf16[512,512]{1,0:T(8,128)(2,1)S(1)}, bf16[512,512]{1,0:T(8,128)(2,1)}, u32[]{:S(2)}) copy-start(bf16[512,512]{1,0:T(8,128)(2,1)} %copy-done.10) | copy-start | bytes 1572868
  67.1 13.3 %copy-start.13 = (bf16[512,512]{1,0:T(8,128)(2,1)S(1)}, bf16[512,512]{1,0:T(8,128)(2,1)}, u32[]{:S(2)}) copy-start(bf16[512,512]{1,0:T(8,128)(2,1)} %copy-done.12) | copy-start | bytes 1572868
  67.1 13.3 %copy-start.15 = (f32[32,1024]{1,0:T(8,128)S(1)}, f32[32,1024]{1,0:T(8,128)}, u32[]{:S(2)}) copy-start(f32[32,1024]{1,0:T(8,128)} %top_right.1) | copy-start | bytes 393220
  67.5 6.3 %collective-permute-start.7 = (f32[32,512]{1,0:T(8,128)S(1)}, f32[32,512]{1,0:T(8,128)S(1)}, u32[]{:S(2)}, u32[]{:S(2)}) collective-permute-start(f32[32,512]{1,0:T(8,128)S(1)} %shard_map.100), channel_id=1, source_target_pairs={{0,4},{1,5},{2,6},{3,7},{4,8},{5,9},{6,10},{7,11},{8,12},{9,13},{1... | collective-permute-start | bytes 196616 | tf_op jit(solution)/shard_map/ppermute | solution.py:289
  74.2 6.2 %collective-permute-start.8 = (f32[32,512]{1,0:T(8,128)S(1)}, f32[32,512]{1,0:T(8,128)S(1)}, u32[]{:S(2)}, u32[]{:S(2)}) collective-permute-start(f32[32,512]{1,0:T(8,128)S(1)} %shard_map.101), channel_id=1, source_target_pairs={{0,4},{1,5},{2,6},{3,7},{4,8},{5,9},{6,10},{7,11},{8,12},{9,13},{1... | collective-permute-start | bytes 196616 | tf_op jit(solution)/shard_map/ppermute | solution.py:289
  131.8 14.6 %copy-start.1 = (bf16[4,512,512]{2,1,0:T(8,128)(2,1)S(1)}, bf16[4,512,512]{2,1,0:T(8,128)(2,1)}, u32[]{:S(2)}) copy-start(bf16[4,512,512]{2,1,0:T(8,128)(2,1)} %copy-done) | copy-start | bytes 6291460
  131.8 1.8 %copy-start.3 = (f32[128,4608]{1,0:T(8,128)S(1)}, f32[128,4608]{1,0:T(8,128)}, u32[]{:S(2)}) copy-start(f32[128,4608]{1,0:T(8,128)} %all-gather.7.cloned.1.call-done) | copy-start | bytes 7077892
  133.7 2.3 %copy-start.5 = (f32[1,1,256,512]{3,2,1,0:T(8,128)S(1)}, f32[1,1,256,512]{3,2,1,0:T(8,128)}, u32[]{:S(2)}) copy-start(f32[1,1,256,512]{3,2,1,0:T(8,128)} %param.11) | copy-start | bytes 1572868
  147.6 19.2 %copy-start.7 = (f32[1,1,512,512]{3,2,1,0:T(8,128)S(1)}, f32[1,1,512,512]{3,2,1,0:T(8,128)}, u32[]{:S(2)}) copy-start(f32[1,1,512,512]{3,2,1,0:T(8,128)} %param.9) | copy-start | bytes 3145732
  147.6 6.3 %collective-permute-start.9 = (f32[32,512]{1,0:T(8,128)S(1)}, f32[32,512]{1,0:T(8,128)S(1)}, u32[]{:S(2)}, u32[]{:S(2)}) collective-permute-start(f32[32,512]{1,0:T(8,128)S(1)} %get-tuple-element.53.base), channel_id=1, source_target_pairs={{4,0},{5,1},{6,2},{7,3},{8,4},{9,5},{10,6},{11,7},{12,8},{13,9},{1... | collective-permute-start | bytes 196616 | tf_op jit(solution)/shard_map/ppermute | solution.py:289
  154.1 6.2 %collective-permute-start.10 = (f32[32,512]{1,0:T(8,128)S(1)}, f32[32,512]{1,0:T(8,128)S(1)}, u32[]{:S(2)}, u32[]{:S(2)}) collective-permute-start(f32[32,512]{1,0:T(8,128)S(1)} %shard_map.108), channel_id=1, source_target_pairs={{4,0},{5,1},{6,2},{7,3},{8,4},{9,5},{10,6},{11,7},{12,8},{13,9},{1... | collective-permute-start | bytes 196616 | tf_op jit(solution)/shard_map/ppermute | solution.py:289
  160.6 6.2 %collective-permute-start.11 = (f32[32,512]{1,0:T(8,128)S(1)}, f32[32,512]{1,0:T(8,128)S(1)}, u32[]{:S(2)}, u32[]{:S(2)}) collective-permute-start(f32[32,512]{1,0:T(8,128)S(1)} %shard_map.109), channel_id=1, source_target_pairs={{4,0},{5,1},{6,2},{7,3},{8,4},{9,5},{10,6},{11,7},{12,8},{13,9},{1... | collective-permute-start | bytes 196616 | tf_op jit(solution)/shard_map/ppermute | solution.py:289
  (7 other events, 6.7 us)
Sparse Core Ops, SparseCore 0:
  11.7 45.3 all-gather.4
  67.2 43.1 all-gather.6

commit v4 on v3

--- a/solution.py
+++ b/solution.py
@@ -7,6 +7,7 @@
 
 BRANCHES = 2
 ROW = 4
+STORE = 128
 NN = (((1,), (0,)), ((), ()))
 NT = (((1,), (1,)), ((), ()))
 VMEM = pl.BlockSpec(memory_space=pltpu.VMEM)
@@ -35,12 +36,12 @@
     return lax.rem(lax.axis_index("ga"), ROW)
 
 
-def kernel_call(body, outs, ins, scratch=(), flops=0, nbytes=0, limit=16):
+def kernel_call(body, outs, ins, scratch=(), flops=0, nbytes=0, limit=16, out_specs=None):
     return pl.pallas_call(
         body,
         out_shape=outs,
         in_specs=ins,
-        out_specs=jax.tree.map(lambda _: VMEM, outs),
+        out_specs=out_specs or jax.tree.map(lambda _: VMEM, outs),
         scratch_shapes=list(scratch),
         compiler_params=pltpu.CompilerParams(vmem_limit_bytes=limit * 2**20),
         cost_estimate=pl.CostEstimate(flops=flops, bytes_accessed=nbytes, transcendentals=0),
@@ -51,38 +52,61 @@
     return jax.ShapeDtypeStruct(dims, kind)
 
 
-def prepare(live, right_hbm, inverse_hbm, coupling_hbm, upper, lower, right, inverse, coupling, sems):
+def prepare(
+    live, right_hbm, inverse_hbm, coupling_hbm, upper_hbm, lower_hbm, right, inverse, coupling, upper, lower, sems
+):
     width = inverse.shape[0]
     half = width // 2
     rhs = right.shape[0]
-    halves = (pl.ds(0, half), pl.ds(half, half))
+    first, second = pl.ds(0, half), pl.ds(half, half)
+    corner = (first, first)
     moves = [
-        pltpu.make_async_copy(inverse_hbm, inverse, sems.at[0]),
-        pltpu.make_async_copy(coupling_hbm.at[halves[0]], coupling.at[halves[0]], sems.at[1]),
-        pltpu.make_async_copy(coupling_hbm.at[halves[1]], coupling.at[halves[1]], sems.at[2]),
-        pltpu.make_async_copy(right_hbm, right, sems.at[3]),
+        pltpu.make_async_copy(inverse_hbm.at[corner], inverse.at[corner], sems.at[0]),
+        pltpu.make_async_copy(coupling_hbm.at[first], coupling.at[first], sems.at[1]),
+        pltpu.make_async_copy(inverse_hbm.at[second], inverse.at[second], sems.at[2]),
+        pltpu.make_async_copy(coupling_hbm.at[second], coupling.at[second], sems.at[3]),
+        pltpu.make_async_copy(right_hbm, right, sems.at[4]),
     ]
     for move in moves:
         move.start()
+    results = [
+        pltpu.make_async_copy(upper.at[first], upper_hbm.at[first], sems.at[5]),
+        pltpu.make_async_copy(lower.at[first], lower_hbm.at[first], sems.at[6]),
+        pltpu.make_async_copy(
+            upper.at[pl.ds(half, rhs // 2)], upper_hbm.at[pl.ds(half, rhs // 2)], sems.at[7]
+        ),
+        pltpu.make_async_copy(
+            lower.at[pl.ds(half, rhs // 2)], lower_hbm.at[pl.ds(half, rhs // 2)], sems.at[8]
+        ),
+    ]
     count = live[0, 0]
     row = lax.broadcasted_iota(jnp.int32, (half, width), 0)
     moves[0].wait()
-    dh, dl = split(inverse[...])
+    corner = split(inverse[:half, :half])
     moves[1].wait()
     ch, cl = split(coupling[:half])
-    top = dot3((dh[:half, :half], dl[:half, :half]), (ch, cl), NN)
-    upper[:half] = jnp.where(row < count, -top, 0.0)
-    bottom = dot3((dh[half:, :half], dl[half:, :half]), (ch, cl), NN)
+    upper[:half] = jnp.where(row < count, -dot3(corner, (ch, cl), NN), 0.0)
+    results[0].start()
     moves[2].wait()
-    ch, cl = split(coupling[half:])
-    bottom = bottom + dot3((dh[half:, half:], dl[half:, half:]), (ch, cl), NN)
+    left = split(inverse[half:, :half])
+    bottom = dot3(left, (ch, cl), NN)
+    full = split(inverse[half:, half:])
+    moves[3].wait()
+    bottom = bottom + dot3(full, split(coupling[half:]), NN)
     lower[:half] = jnp.where(row + half < count, -bottom, 0.0)
-    moves[3].wait()
-    own = dot3(split(right[...]), (dh, dl), NT)
+    results[1].start()
+    moves[4].wait()
+    sides = split(right[...])
+    head, rest = ((sides[0][:, :half], sides[1][:, :half]), (sides[0][:, half:], sides[1][:, half:]))
+    own = jnp.concatenate((dot3(head, corner, NT), dot3(head, left, NT) + dot3(rest, full, NT)), 1)
     col = lax.broadcasted_iota(jnp.int32, (rhs, width), 1)
     own = jnp.where(col < count, own, 0.0)
     upper[half:] = own[: rhs // 2]
     lower[half:] = own[rhs // 2 :]
+    results[2].start()
+    results[3].start()
+    for result in results:
+        result.wait()
 
 
 def pack_lower(blocks, out):
@@ -126,42 +150,50 @@
     last[...] = value
 
 
-def multiply_up(nh, nl, qh, ql, ph, plow):
+def multiply_up(nh, nl, products, store, sems):
+    moves = [
+        pltpu.make_async_copy(block, store.at[pl.ds(at * ROW, ROW)], sems.at[at])
+        for at, block in enumerate((nh, nl))
+    ]
+    for move in moves:
+        move.start()
     here = place_in_row()
     high, low = nh[0], nl[0]
 
     @pl.when(here == 0)
     def _():
-        qh[...] = high
-        ql[...] = low
+        products[0] = high
+        products[1] = low
 
     for j in range(1, ROW):
         high, low = split(dot3((nh[j], nl[j]), (high, low), NN))
 
         @pl.when(here == j)
         def _():
-            qh[...] = high
-            ql[...] = low
-
-    ph[...] = high
-    plow[...] = low
-
-
-def hop_forward(base, coming, ph, plow, out):
-    out[...] = base[...] + dot3(split(coming[...]), (ph[...], plow[...]), NT)
-
-
-def hop_backward(base, coming, ph, plow, out):
-    out[...] = base[...] + dot3(split(coming[...]), (ph[...], plow[...]), NN)
+            products[0] = high
+            products[1] = low
+
+    products[2] = high
+    products[3] = low
+    for move in moves:
+        move.wait()
+
+
+def hop_forward(base, coming, products, out):
+    out[...] = base[...] + dot3(split(coming[...]), (products[2], products[3]), NT)
+
+
+def hop_backward(base, coming, products, out):
+    out[...] = base[...] + dot3(split(coming[...]), (products[2], products[3]), NN)
 
 
 def onehot_of(rows, top):
     return (lax.broadcasted_iota(jnp.int32, (top, rows.shape[1]), 0) == rows[...]).astype(F32).astype(BF16)
 
 
-def contribute(group, coming, qh, ql, across, rows, top_right, solved, tiles):
+def contribute(group, coming, products, across, rows, top_right, solved, tiles):
     here = place_in_row()
-    value = group[here] + dot3(split(coming[...]), (qh[...], ql[...]), NT)
+    value = group[here] + dot3(split(coming[...]), (products[0], products[1]), NT)
     solved[...] = value
     pushed = dot3(split(value), split(across[...]), NT)
     count, depth, lanes = tiles.shape
@@ -231,8 +263,18 @@
         reduced[piece] = value
 
 
-def row_backward(reduced, nh, nl, own, sent):
+def row_backward(reduced, store, own, sent, nh, nl, sems):
     here = place_in_row()
+    moves = [
+        [
+            pltpu.make_async_copy(store.at[at * ROW + j], block.at[j], sems.at[at, j])
+            for at, block in enumerate((nh, nl))
+        ]
+        for j in range(ROW)
+    ]
+    for pair_of in reversed(moves):
+        for move in pair_of:
+            move.start()
     value = reduced[ROW - 1]
     for j in range(ROW - 1, -1, -1):
         if j < ROW - 1:
@@ -242,23 +284,30 @@
         def _():
             own[...] = value
 
+        for move in moves[j]:
+            move.wait()
         value = dot3(split(value), (nh[j], nl[j]), NN)
     sent[...] = value
 
 
-def finish(live, own, coming, nh, nl, inverse, out, term):
+def tail(live, own, nh, nl, inverse, settled, zh, zl):
     here = place_in_row()
-    term[...] = coming[...]
-    for j in range(ROW - 1, 0, -1):
+    row = lax.broadcasted_iota(jnp.int32, inverse.shape, 0)
+    high, low = split(jnp.where(row < live[0, 0], inverse[...], 0.0))
+    settled[...] = dot3(split(own[...]), (high, low), NN)
+    zh[...] = high
+    zl[...] = low
+    for j in range(1, ROW):
 
         @pl.when(here < j)
         def _():
-            term[...] = dot3(split(term[...]), (nh[j], nl[j]), NN)
-
-    value = own[...] + term[...]
-    col = lax.broadcasted_iota(jnp.int32, value.shape, 1)
-    value = jnp.where(col < live[0, 0], value, 0.0)
-    out[...] = dot3(split(value), split(inverse[...]), NN)
+            high, low = split(dot3((nh[j], nl[j]), (zh[...], zl[...]), NN))
+            zh[...] = high
+            zl[...] = low
+
+
+def finish(settled, coming, zh, zl, out):
+    out[...] = settled[...] + dot3(split(coming[...]), (zh[...], zl[...]), NN)
 
 
 def shards(
@@ -300,8 +349,11 @@
             pltpu.VMEM((rhs, width), F32),
             pltpu.VMEM((width, width), F32),
             pltpu.VMEM((width, width), F32),
-            pltpu.SemaphoreType.DMA((4,)),
+            pltpu.VMEM((half, width), F32),
+            pltpu.VMEM((half, width), F32),
+            pltpu.SemaphoreType.DMA((9,)),
         ],
+        out_specs=(HBM, HBM),
         flops=6 * width**3,
         nbytes=16 * width**2,
         limit=60,
@@ -329,35 +381,38 @@
         nbytes=32 * width**2,
     )(*staged, a2, b2)
     coming = hop(last, 1)
-    qh, ql, ph, plow = kernel_call(
+    products, store = kernel_call(
         multiply_up,
-        pair(width, width) * 2,
+        (shape(4, width, width, kind=BF16), shape(STORE, width, width, kind=BF16)),
         [VMEM, VMEM],
+        scratch=[pltpu.SemaphoreType.DMA((2,))],
+        out_specs=(VMEM, HBM),
         flops=18 * width**3,
         nbytes=24 * width**2,
     )(nh, nl)
-    blocks, coming, plow = lax.optimization_barrier((blocks, coming, plow))
+    blocks, coming, products = lax.optimization_barrier((blocks, coming, products))
     packed = kernel_call(
         pack_lower,
         shape(top_inverse.shape[0], top * (ga // ROW + 1) // 2),
         [VMEM],
         nbytes=2 * top**2,
     )(blocks)
-    packed, coming = lax.optimization_barrier((packed, coming))
+    for step in range(chain_rows - 2):
+        moved = kernel_call(
+            hop_forward, shape(rhs, width), [VMEM] * 3, flops=6 * rhs * width**2
+        )(last, coming, products)
+        coming = hop(moved, 1)
+        if step == 0:
+            packed, coming = lax.optimization_barrier((packed, coming))
     packed = lax.all_gather(packed, "ga", axis_index_groups=x_groups)
-    for _ in range(chain_rows - 2):
-        moved = kernel_call(
-            hop_forward, shape(rhs, width), [VMEM] * 4, flops=6 * rhs * width**2
-        )(last, coming, ph, plow)
-        coming = hop(moved, 1)
 
     tiles = (ga, rhs * top // ga // 128, 128)
     solved, partial = kernel_call(
         contribute,
         (shape(rhs, width), shape(*tiles)),
-        [VMEM] * 7,
+        [VMEM] * 6,
         flops=12 * rhs * width**2,
-    )(group, coming, qh, ql, across, rows, top_right)
+    )(group, coming, products, across, rows, top_right)
     partial = lax.all_to_all(partial, "ga", 0, 0)
     partial = kernel_call(total_of, shape(gz, *tiles[1:]), [VMEM])(partial)
     partial = lax.all_to_all(partial, "gz", 0, 0)
@@ -376,25 +431,29 @@
     )(top_solution, across, rows, solved)
 
     reduced = lax.all_to_all(reduced, "ga", 0, 0, axis_index_groups=x_groups)
-    own, sent = kernel_call(
+    own, sent, nh, nl = kernel_call(
         row_backward,
-        (shape(rhs, width), shape(rhs, width)),
-        [VMEM] * 3,
+        (shape(rhs, width), shape(rhs, width)) + pair(ROW, width, width),
+        [VMEM, HBM],
+        scratch=[pltpu.SemaphoreType.DMA((2, ROW))],
         flops=24 * rhs * width**2,
-    )(reduced, nh, nl)
+    )(reduced, store)
     coming = hop(sent, -1)
+    settled, zh, zl = kernel_call(
+        tail,
+        (shape(rhs, width),) + pair(width, width),
+        [SMEM] + [VMEM] * 4,
+        flops=18 * width**3,
+        nbytes=24 * width**2,
+    )(live_cols, own, nh, nl, inverse)
     for _ in range(chain_rows - 2):
         moved = kernel_call(
-            hop_backward, shape(rhs, width), [VMEM] * 4, flops=6 * rhs * width**2
-        )(sent, coming, ph, plow)
+            hop_backward, shape(rhs, width), [VMEM] * 3, flops=6 * rhs * width**2
+        )(sent, coming, products)
         coming = hop(moved, -1)
     result = kernel_call(
-        finish,
-        shape(rhs, width),
-        [SMEM] + [VMEM] * 5,
-        scratch=[pltpu.VMEM((rhs, width), F32)],
-        flops=24 * rhs * width**2,
-    )(live_cols, own, coming, nh, nl, inverse)
+        finish, shape(rhs, width), [VMEM] * 4, flops=6 * rhs * width**2
+    )(settled, coming, zh, zl)
     return (result[None, None], top_solution)
 
 

time: 176 us -> 173 us (0.983)
  Pallas kernels: 17.2 us -> 21.4 us
  waiting for transfers between devices: 35.5 us -> 31.5 us
  local copies, waits for them, and re-layouts: 8.53 us -> 4.72 us
    ppermute x6, waiting for transfers between devices: 14.7 us -> 10.7 us  [hop(): return lax.ppermute(value, 'ga', route)]
    unnamed x34 -> x18, local copies, waits for them, and re-layouts: 8.53 us -> 4.72 us
    pallas_call x8 -> x9, Pallas kernels: 8.57 us -> 12.4 us  [the longest x1 3.28 us: shards(): kernel_call(tail, (shape(rhs, width),) + pair(width, width), [SMEM] + [VM...]
  transfers between devices with their start and end apart: 14 -> 14, of which waited for: 9 -> 8; matrix products, arithmetic and copies ran while one was open for 0% -> 0% of each run, Pallas kernels for 4% -> 6%
where the time goes in v4:
time: 173 us; the launch traced here: 172 us
  blocking collectives  59.6 us (34%)
  starting transfers between devices  39.9 us (23%)
  waiting for transfers between devices  31.5 us (18%)
  Pallas kernels  21.4 us (12%)
  between operations  14.9 us (9%)
  local copies, waits for them, and re-layouts  4.72 us (3%)
    all_to_all x2, blocking collectives, shards(): partial = lax.all_to_all(partial, 'ga', 0, 0)  32.4 us
    ppermute x6, waiting for transfers between devices, ring(): lax.ppermute(value, 'ga', [(i, i // ROW * ROW + (i + step) % ROW) for i i...  20.8 us
    ppermute x6, starting transfers between devices, ring(): lax.ppermute(value, 'ga', [(i, i // ROW * ROW + (i + step) % ROW) for i i...  19.9 us
    ppermute x6, starting transfers between devices, hop(): return lax.ppermute(value, 'ga', route)  19.9 us
    all_to_all x1, blocking collectives, shards(): partial = lax.all_to_all(partial, 'gz', 0, 0)  18.1 us
    ppermute x6, waiting for transfers between devices, hop(): return lax.ppermute(value, 'ga', route)  10.7 us
    all_to_all x1, blocking collectives, shards(): reduced = lax.all_to_all(reduced, 'ga', 0, 0, axis_index_groups=x_groups)  9.07 us
    unnamed x18, local copies, waits for them, and re-layouts  4.72 us
  transfers between devices with their start and end apart: 14, of which 8 were waited for; matrix products, arithmetic and copies ran while one was open for 0% of the time, Pallas kernels for 6%

profile of v4, /device:TPU:8, one launch (start us, length us, event | category | flops | bytes accessed | tf_op | source)
XLA Modules:
  0.0 172.1 jit_solution(1443376559942643747)
XLA Ops:
  7.9 3.3 %shard_map.95 = (f32[272,512]{1,0:T(8,128)}, f32[272,512]{1,0:T(8,128)}) custom-call(s32[1,1]{1,0:T(1,128)S(6)} %copy.10.live, f32[32,512]{1,0:T(8,128)} %bitcast.18, f32[512,512]{1,0:T(8,128)} %bitcast.14, f32[512,512]{1,0:T(8,128)} %bitcast.17), custom_call_target="tpu_custom_call" | custom-call | flops 805306368 | bytes 4194304 | tf_op jit(solution)/shard_map/pallas_call | solution.py:344
  11.2 3.4 %collective-permute-start.2 = (f32[272,512]{1,0:T(8,128)}, f32[272,512]{1,0:T(8,128)S(1)}, u32[]{:S(2)}, u32[]{:S(2)}) collective-permute-start(f32[272,512]{1,0:T(8,128)} %get-tuple-element.32.a0), channel_id=1, source_target_pairs={{0,1},{1,2},{2,3},{3,0},{4,5},{5,6},{6,7},{7,4},{8,9},{9,10},{10,1... | collective-permute-start | bytes 1671176 | tf_op jit(solution)/shard_map/ppermute | solution.py:328
  14.7 3.7 %collective-permute-start.1 = (f32[272,512]{1,0:T(8,128)}, f32[272,512]{1,0:T(8,128)S(1)}, u32[]{:S(2)}, u32[]{:S(2)}) collective-permute-start(f32[272,512]{1,0:T(8,128)} %get-tuple-element.33.b0), channel_id=1, source_target_pairs={{0,3},{1,0},{2,1},{3,2},{4,7},{5,4},{6,5},{7,6},{8,11},{9,8},{10,9... | collective-permute-start | bytes 1671176 | tf_op jit(solution)/shard_map/ppermute | solution.py:328
  18.3 3.5 %collective-permute-start = (f32[272,512]{1,0:T(8,128)}, f32[272,512]{1,0:T(8,128)S(1)}, u32[]{:S(2)}, u32[]{:S(2)}) collective-permute-start(f32[272,512]{1,0:T(8,128)} %get-tuple-element.32.a0), channel_id=1, source_target_pairs={{0,3},{1,0},{2,1},{3,2},{4,7},{5,4},{6,5},{7,6},{8,11},{9,8},{10,9... | collective-permute-start | bytes 1671176 | tf_op jit(solution)/shard_map/ppermute | solution.py:328
  24.2 5.9 %collective-permute-done.2.a3 = f32[272,512]{1,0:T(8,128)S(1)} collective-permute-done((f32[272,512]{1,0:T(8,128)}, f32[272,512]{1,0:T(8,128)S(1)}, u32[]{:S(2)}, u32[]{:S(2)}) %collective-permute-start.2) | collective-permute-done | bytes 557088 | tf_op jit(solution)/shard_map/ppermute | solution.py:328
  32.3 4.8 %collective-permute-start.5 = (f32[272,512]{1,0:T(8,128)S(1)}, f32[272,512]{1,0:T(8,128)S(1)}, u32[]{:S(2)}, u32[]{:S(2)}) collective-permute-start(f32[272,512]{1,0:T(8,128)S(1)} %collective-permute-done.1.b1), channel_id=1, source_target_pairs={{0,3},{1,0},{2,1},{3,2},{4,7},{5,4},{6,5},{7,6},{8,11},{9,8},{10,9... | collective-permute-start | bytes 1671176 | tf_op jit(solution)/shard_map/ppermute | solution.py:328
  37.2 7.1 %collective-permute-done.a1 = f32[272,512]{1,0:T(8,128)S(1)} collective-permute-done((f32[272,512]{1,0:T(8,128)}, f32[272,512]{1,0:T(8,128)S(1)}, u32[]{:S(2)}, u32[]{:S(2)}) %collective-permute-start) | collective-permute-done | bytes 557088 | tf_op jit(solution)/shard_map/ppermute | solution.py:328
  46.9 5.9 %collective-permute-done.4.a2 = f32[272,512]{1,0:T(8,128)S(1)} collective-permute-done((f32[272,512]{1,0:T(8,128)S(1)}, f32[272,512]{1,0:T(8,128)S(1)}, u32[]{:S(2)}, u32[]{:S(2)}) %collective-permute-start.4) | collective-permute-done | bytes 557088 | tf_op jit(solution)/shard_map/ppermute | solution.py:328
  56.2 3.5 %collective-permute-start.6 = (f32[32,512]{1,0:T(8,128)S(1)}, f32[32,512]{1,0:T(8,128)S(1)}, u32[]{:S(2)}, u32[]{:S(2)}) collective-permute-start(f32[32,512]{1,0:T(8,128)S(1)} %get-tuple-element.38.base), channel_id=1, source_target_pairs={{0,4},{1,5},{2,6},{3,7},{4,8},{5,9},{6,10},{7,11},{8,12},{9,13},{1... | collective-permute-start | bytes 196616 | tf_op jit(solution)/shard_map/ppermute | solution.py:338
  59.7 3.2 %shard_map.98 = (bf16[4,512,512]{2,1,0:T(8,128)(2,1)S(1)}, bf16[128,512,512]{2,1,0:T(8,128)(2,1)}) custom-call(bf16[4,512,512]{2,1,0:T(8,128)(2,1)S(1)} %get-tuple-element.40.nh, bf16[4,512,512]{2,1,0:T(8,128)(2,1)S(1)} %get-tuple-element.41.nl), custom_call_target="tpu_custom_call" | custom-call | flops 2415919104 | bytes 6291456 | tf_op jit(solution)/shard_map/pallas_call | solution.py:384
  63.4 3.6 %collective-permute-start.7 = (f32[32,512]{1,0:T(8,128)S(1)}, f32[32,512]{1,0:T(8,128)S(1)}, u32[]{:S(2)}, u32[]{:S(2)}) collective-permute-start(f32[32,512]{1,0:T(8,128)S(1)} %shard_map.100), channel_id=1, source_target_pairs={{0,4},{1,5},{2,6},{3,7},{4,8},{5,9},{6,10},{7,11},{8,12},{9,13},{1... | collective-permute-start | bytes 196616 | tf_op jit(solution)/shard_map/ppermute | solution.py:338
  70.2 3.5 %collective-permute-start.8 = (f32[32,512]{1,0:T(8,128)S(1)}, f32[32,512]{1,0:T(8,128)S(1)}, u32[]{:S(2)}, u32[]{:S(2)}) collective-permute-start(f32[32,512]{1,0:T(8,128)S(1)} %shard_map.101), channel_id=1, source_target_pairs={{0,4},{1,5},{2,6},{3,7},{4,8},{5,9},{6,10},{7,11},{8,12},{9,13},{1... | collective-permute-start | bytes 196616 | tf_op jit(solution)/shard_map/ppermute | solution.py:338
  73.7 2.7 %collective-permute-done.8.coming = f32[32,512]{1,0:T(8,128)S(1)} collective-permute-done((f32[32,512]{1,0:T(8,128)S(1)}, f32[32,512]{1,0:T(8,128)S(1)}, u32[]{:S(2)}, u32[]{:S(2)}) %collective-permute-start.8) | collective-permute-done | bytes 65568 | tf_op jit(solution)/shard_map/ppermute | solution.py:338
  77.4 18.1 %all_to_all.20.pieces = f32[32,8,128]{2,1,0:T(8,128)S(1)} all-to-all(f32[32,8,128]{2,1,0:T(8,128)S(1)} %get-tuple-element.47), channel_id=1, replica_groups=mesh['gz'=16,'ga'=32] {'ga'}, dimensions={0} | all-to-all | bytes 262144 | tf_op jit(solution)/shard_map/all_to_all | solution.py:416
  95.6 18.1 %all_to_all.21.pieces = f32[16,8,128]{2,1,0:T(8,128)S(1)} all-to-all(f32[16,8,128]{2,1,0:T(8,128)S(1)} %shard_map.103), channel_id=1, replica_groups=mesh['gz'=16,'ga'=32] {'gz'}, dimensions={0} | all-to-all | bytes 131072 | tf_op jit(solution)/shard_map/all_to_all | solution.py:418
  113.7 14.3 %all_to_all.22.tiles = f32[32,8,128]{2,1,0:T(8,128)S(1)} all-to-all(f32[32,8,128]{2,1,0:T(8,128)S(1)} %shard_map.104), channel_id=1, replica_groups=mesh['gz'=16,'ga'=32] {'ga'}, dimensions={0} | all-to-all | bytes 262144 | tf_op jit(solution)/shard_map/all_to_all | solution.py:420
  133.4 9.1 %all_to_all.23.reduced = f32[4,32,512]{2,1,0:T(8,128)S(1)} all-to-all(f32[4,32,512]{2,1,0:T(8,128)S(1)} %shard_map.106), channel_id=1, replica_groups={{0,1,2,3},{4,5,6,7},{8,9,10,11},{12,13,14,15},{16,17,18,19},{20,21,22,2..., dimensions={0} | all-to-all | bytes 524288 | tf_op jit(solution)/shard_map/all_to_all | solution.py:433
  142.4 2.5 %shard_map.107 = (f32[32,512]{1,0:T(8,128)S(1)}, f32[32,512]{1,0:T(8,128)S(1)}, bf16[4,512,512]{2,1,0:T(8,128)(2,1)S(1)}, bf16[4,512,512]{2,1,0:T(8,128)(2,1)S(1)}) custom-call(f32[4,32,512]{2,1,0:T(8,128)S(1)} %all_to_all.23.reduced, bf16[128,512,512]{2,1,0:T(8,128)(2,1)} %get-tuple-element.52.store), custom_call_target="tpu_custom_call" | custom-call | flops 201326592 | tf_op jit(solution)/shard_map/pallas_call | solution.py:434
  144.9 3.2 %collective-permute-start.9 = (f32[32,512]{1,0:T(8,128)S(1)}, f32[32,512]{1,0:T(8,128)S(1)}, u32[]{:S(2)}, u32[]{:S(2)}) collective-permute-start(f32[32,512]{1,0:T(8,128)S(1)} %get-tuple-element.57.base), channel_id=1, source_target_pairs={{4,0},{5,1},{6,2},{7,3},{8,4},{9,5},{10,6},{11,7},{12,8},{13,9},{1... | collective-permute-start | bytes 196616 | tf_op jit(solution)/shard_map/ppermute | solution.py:338
  148.1 3.1 %collective-permute-done.9.coming = f32[32,512]{1,0:T(8,128)S(1)} collective-permute-done((f32[32,512]{1,0:T(8,128)S(1)}, f32[32,512]{1,0:T(8,128)S(1)}, u32[]{:S(2)}, u32[]{:S(2)}) %collective-permute-start.9) | collective-permute-done | bytes 65568 | tf_op jit(solution)/shard_map/ppermute | solution.py:338
  151.5 3.1 %collective-permute-start.10 = (f32[32,512]{1,0:T(8,128)S(1)}, f32[32,512]{1,0:T(8,128)S(1)}, u32[]{:S(2)}, u32[]{:S(2)}) collective-permute-start(f32[32,512]{1,0:T(8,128)S(1)} %shard_map.109), channel_id=1, source_target_pairs={{4,0},{5,1},{6,2},{7,3},{8,4},{9,5},{10,6},{11,7},{12,8},{13,9},{1... | collective-permute-start | bytes 196616 | tf_op jit(solution)/shard_map/ppermute | solution.py:338
  154.6 3.1 %collective-permute-done.10.coming = f32[32,512]{1,0:T(8,128)S(1)} collective-permute-done((f32[32,512]{1,0:T(8,128)S(1)}, f32[32,512]{1,0:T(8,128)S(1)}, u32[]{:S(2)}, u32[]{:S(2)}) %collective-permute-start.10) | collective-permute-done | bytes 65568 | tf_op jit(solution)/shard_map/ppermute | solution.py:338
  157.9 3.1 %collective-permute-start.11 = (f32[32,512]{1,0:T(8,128)S(1)}, f32[32,512]{1,0:T(8,128)S(1)}, u32[]{:S(2)}, u32[]{:S(2)}) collective-permute-start(f32[32,512]{1,0:T(8,128)S(1)} %shard_map.110), channel_id=1, source_target_pairs={{4,0},{5,1},{6,2},{7,3},{8,4},{9,5},{10,6},{11,7},{12,8},{13,9},{1... | collective-permute-start | bytes 196616 | tf_op jit(solution)/shard_map/ppermute | solution.py:338
  161.0 3.3 %shard_map.108 = (f32[32,512]{1,0:T(8,128)S(1)}, bf16[512,512]{1,0:T(8,128)(2,1)S(1)}, bf16[512,512]{1,0:T(8,128)(2,1)S(1)}) custom-call(s32[1,1]{1,0:T(1,128)S(6)} %copy.10.live, f32[32,512]{1,0:T(8,128)S(1)} %get-tuple-element.53.own, bf16[4,512,512]{2,1,0:T(8,128)(2,1)S(1)} %get-tuple-element.54.nh, bf16[4,512,512]{2,1,0:T(8,128)(2,1)S(1)} %get-tuple-element.55.nl, ...), custom_call_target="tpu_custom_call" | custom-call | flops 2415919104 | bytes 6291456 | tf_op jit(solution)/shard_map/pallas_call | solution.py:442
  (45 shorter events, 22.3 us)
Async XLA Ops:
  7.2 55.8 %all-gather.5.cloned.1.call-start = ((), (), s32[]{:S(2)}) async-start(), calls=%async_computation.4 | async-start | bytes 1179648 | tf_op jit(solution)/shard_map/all_gather | solution.py:362
  11.2 116.8 %all-gather.7.cloned.1.call-start = ((), (), s32[]{:S(2)}) async-start(), calls=%async_computation.5 | async-start | bytes 2949120 | tf_op jit(solution)/shard_map/all_gather | solution.py:407
  11.2 18.8 %collective-permute-start.2 = (f32[272,512]{1,0:T(8,128)}, f32[272,512]{1,0:T(8,128)S(1)}, u32[]{:S(2)}, u32[]{:S(2)}) collective-permute-start(f32[272,512]{1,0:T(8,128)} %get-tuple-element.32.a0), channel_id=1, source_target_pairs={{0,1},{1,2},{2,3},{3,0},{4,5},{5,6},{6,7},{7,4},{8,9},{9,10},{10,1... | collective-permute-start | bytes 1671176 | tf_op jit(solution)/shard_map/ppermute | solution.py:328
  14.7 17.7 %collective-permute-start.1 = (f32[272,512]{1,0:T(8,128)}, f32[272,512]{1,0:T(8,128)S(1)}, u32[]{:S(2)}, u32[]{:S(2)}) collective-permute-start(f32[272,512]{1,0:T(8,128)} %get-tuple-element.33.b0), channel_id=1, source_target_pairs={{0,3},{1,0},{2,1},{3,2},{4,7},{5,4},{6,5},{7,6},{8,11},{9,8},{10,9... | collective-permute-start | bytes 1671176 | tf_op jit(solution)/shard_map/ppermute | solution.py:328
  18.3 25.9 %collective-permute-start = (f32[272,512]{1,0:T(8,128)}, f32[272,512]{1,0:T(8,128)S(1)}, u32[]{:S(2)}, u32[]{:S(2)}) collective-permute-start(f32[272,512]{1,0:T(8,128)} %get-tuple-element.32.a0), channel_id=1, source_target_pairs={{0,3},{1,0},{2,1},{3,2},{4,7},{5,4},{6,5},{7,6},{8,11},{9,8},{10,9... | collective-permute-start | bytes 1671176 | tf_op jit(solution)/shard_map/ppermute | solution.py:328
  21.8 22.5 %collective-permute-start.3 = (f32[272,512]{1,0:T(8,128)}, f32[272,512]{1,0:T(8,128)S(1)}, u32[]{:S(2)}, u32[]{:S(2)}) collective-permute-start(f32[272,512]{1,0:T(8,128)} %get-tuple-element.33.b0), channel_id=1, source_target_pairs={{0,1},{1,2},{2,3},{3,0},{4,5},{5,6},{6,7},{7,4},{8,9},{9,10},{10,1... | collective-permute-start | bytes 1671176 | tf_op jit(solution)/shard_map/ppermute | solution.py:328
  30.1 22.7 %collective-permute-start.4 = (f32[272,512]{1,0:T(8,128)S(1)}, f32[272,512]{1,0:T(8,128)S(1)}, u32[]{:S(2)}, u32[]{:S(2)}) collective-permute-start(f32[272,512]{1,0:T(8,128)S(1)} %collective-permute-done.2.a3), channel_id=1, source_target_pairs={{0,1},{1,2},{2,3},{3,0},{4,5},{5,6},{6,7},{7,4},{8,9},{9,10},{10,1... | collective-permute-start | bytes 1671176 | tf_op jit(solution)/shard_map/ppermute | solution.py:328
  32.3 22.4 %collective-permute-start.5 = (f32[272,512]{1,0:T(8,128)S(1)}, f32[272,512]{1,0:T(8,128)S(1)}, u32[]{:S(2)}, u32[]{:S(2)}) collective-permute-start(f32[272,512]{1,0:T(8,128)S(1)} %collective-permute-done.1.b1), channel_id=1, source_target_pairs={{0,3},{1,0},{2,1},{3,2},{4,7},{5,4},{6,5},{7,6},{8,11},{9,8},{10,9... | collective-permute-start | bytes 1671176 | tf_op jit(solution)/shard_map/ppermute | solution.py:328
  44.3 1.1 copy-start.3
  45.3 1.1 copy-start.4
  56.2 6.7 %collective-permute-start.6 = (f32[32,512]{1,0:T(8,128)S(1)}, f32[32,512]{1,0:T(8,128)S(1)}, u32[]{:S(2)}, u32[]{:S(2)}) collective-permute-start(f32[32,512]{1,0:T(8,128)S(1)} %get-tuple-element.38.base), channel_id=1, source_target_pairs={{0,4},{1,5},{2,6},{3,7},{4,8},{5,9},{6,10},{7,11},{8,12},{9,13},{1... | collective-permute-start | bytes 196616 | tf_op jit(solution)/shard_map/ppermute | solution.py:338
  63.0 4.1 %copy-start.2 = (f32[256,1024]{1,0:T(8,128)S(1)}, f32[256,1024]{1,0:T(8,128)}, u32[]{:S(2)}) copy-start(f32[256,1024]{1,0:T(8,128)} %all-gather.5.cloned.1.call-done) | copy-start | bytes 3145732
  63.4 12.9 %copy-start.1 = (f32[1,1,256,512]{3,2,1,0:T(8,128)S(1)}, f32[1,1,256,512]{3,2,1,0:T(8,128)}, u32[]{:S(2)}) copy-start(f32[1,1,256,512]{3,2,1,0:T(8,128)} %param.11) | copy-start | bytes 1572868
  63.4 12.9 %copy-start.6 = (f32[32,1024]{1,0:T(8,128)S(1)}, f32[32,1024]{1,0:T(8,128)}, u32[]{:S(2)}) copy-start(f32[32,1024]{1,0:T(8,128)} %top_right.1) | copy-start | bytes 393220
  63.4 12.9 %copy-start.7 = (s32[1,1,256]{2,1,0:T(1,128)S(1)}, s32[1,1,256]{2,1,0:T(1,128)}, u32[]{:S(2)}) copy-start(s32[1,1,256]{2,1,0:T(1,128)} %param.12) | copy-start | bytes 3076
  63.4 6.3 %collective-permute-start.7 = (f32[32,512]{1,0:T(8,128)S(1)}, f32[32,512]{1,0:T(8,128)S(1)}, u32[]{:S(2)}, u32[]{:S(2)}) collective-permute-start(f32[32,512]{1,0:T(8,128)S(1)} %shard_map.100), channel_id=1, source_target_pairs={{0,4},{1,5},{2,6},{3,7},{4,8},{5,9},{6,10},{7,11},{8,12},{9,13},{1... | collective-permute-start | bytes 196616 | tf_op jit(solution)/shard_map/ppermute | solution.py:338
  70.2 6.2 %collective-permute-start.8 = (f32[32,512]{1,0:T(8,128)S(1)}, f32[32,512]{1,0:T(8,128)S(1)}, u32[]{:S(2)}, u32[]{:S(2)}) collective-permute-start(f32[32,512]{1,0:T(8,128)S(1)} %shard_map.101), channel_id=1, source_target_pairs={{0,4},{1,5},{2,6},{3,7},{4,8},{5,9},{6,10},{7,11},{8,12},{9,13},{1... | collective-permute-start | bytes 196616 | tf_op jit(solution)/shard_map/ppermute | solution.py:338
  128.0 1.7 copy-start
  131.9 0.9 copy-start.5
  144.9 16.1 %copy-start.8 = (f32[1,1,512,512]{3,2,1,0:T(8,128)S(1)}, f32[1,1,512,512]{3,2,1,0:T(8,128)}, u32[]{:S(2)}) copy-start(f32[1,1,512,512]{3,2,1,0:T(8,128)} %param.9) | copy-start | bytes 3145732
  144.9 6.3 %collective-permute-start.9 = (f32[32,512]{1,0:T(8,128)S(1)}, f32[32,512]{1,0:T(8,128)S(1)}, u32[]{:S(2)}, u32[]{:S(2)}) collective-permute-start(f32[32,512]{1,0:T(8,128)S(1)} %get-tuple-element.57.base), channel_id=1, source_target_pairs={{4,0},{5,1},{6,2},{7,3},{8,4},{9,5},{10,6},{11,7},{12,8},{13,9},{1... | collective-permute-start | bytes 196616 | tf_op jit(solution)/shard_map/ppermute | solution.py:338
  151.5 6.2 %collective-permute-start.10 = (f32[32,512]{1,0:T(8,128)S(1)}, f32[32,512]{1,0:T(8,128)S(1)}, u32[]{:S(2)}, u32[]{:S(2)}) collective-permute-start(f32[32,512]{1,0:T(8,128)S(1)} %shard_map.109), channel_id=1, source_target_pairs={{4,0},{5,1},{6,2},{7,3},{8,4},{9,5},{10,6},{11,7},{12,8},{13,9},{1... | collective-permute-start | bytes 196616 | tf_op jit(solution)/shard_map/ppermute | solution.py:338
  157.9 6.4 %collective-permute-start.11 = (f32[32,512]{1,0:T(8,128)S(1)}, f32[32,512]{1,0:T(8,128)S(1)}, u32[]{:S(2)}, u32[]{:S(2)}) collective-permute-start(f32[32,512]{1,0:T(8,128)S(1)} %shard_map.110), channel_id=1, source_target_pairs={{4,0},{5,1},{6,2},{7,3},{8,4},{9,5},{10,6},{11,7},{12,8},{13,9},{1... | collective-permute-start | bytes 196616 | tf_op jit(solution)/shard_map/ppermute | solution.py:338
Sparse Core Ops, SparseCore 0:
  11.3 45.3 all-gather.4
  69.9 41.8 all-gather.6

commit v5 on v4

--- a/solution.py
+++ b/solution.py
@@ -216,11 +216,17 @@
         out[piece] = value
 
 
-def solve_top(tiles, packed, top_out, wh, wl):
+def solve_top(tiles, packed, store, top_out, nh, nl, wh, wl, sems):
     count, depth, lanes = tiles.shape
     rhs, top = top_out.shape
     col_blocks = top // lanes
     steps = packed.shape[1] * packed.shape[0]
+    moves = [
+        pltpu.make_async_copy(store.at[pl.ds(at * ROW, ROW)], block, sems.at[at])
+        for at, block in enumerate((nh, nl))
+    ]
+    for move in moves:
+        move.start()
     lines = []
     for r in range(rhs // depth):
         lines.append(jnp.concatenate([tiles[r * col_blocks + c] for c in range(col_blocks)], 1))
@@ -251,6 +257,8 @@
             dot3((mid[0][:, j:], mid[1][:, j:]), (wh[j:, j:end], wl[j:, j:end]), NN)
         )
     top_out[...] = jnp.concatenate(answer, 1)
+    for move in moves:
+        move.wait()
 
 
 def lift(top_out, across, rows, solved, reduced):
@@ -263,18 +271,8 @@
         reduced[piece] = value
 
 
-def row_backward(reduced, store, own, sent, nh, nl, sems):
+def row_backward(reduced, nh, nl, own, sent):
     here = place_in_row()
-    moves = [
-        [
-            pltpu.make_async_copy(store.at[at * ROW + j], block.at[j], sems.at[at, j])
-            for at, block in enumerate((nh, nl))
-        ]
-        for j in range(ROW)
-    ]
-    for pair_of in reversed(moves):
-        for move in pair_of:
-            move.start()
     value = reduced[ROW - 1]
     for j in range(ROW - 1, -1, -1):
         if j < ROW - 1:
@@ -284,8 +282,6 @@
         def _():
             own[...] = value
 
-        for move in moves[j]:
-            move.wait()
         value = dot3(split(value), (nh[j], nl[j]), NN)
     sent[...] = value
 
@@ -419,25 +415,28 @@
     partial = kernel_call(total_of, shape(*tiles), [VMEM])(partial)
     partial = lax.all_to_all(partial, "ga", 0, 0)
     partial, packed = lax.optimization_barrier((partial, packed))
-    top_solution = kernel_call(
+    top_solution, nh, nl = kernel_call(
         solve_top,
-        shape(rhs, top),
-        [VMEM] * 2,
-        scratch=[pltpu.VMEM((top, top), BF16), pltpu.VMEM((top, top), BF16)],
+        (shape(rhs, top),) + pair(ROW, width, width),
+        [VMEM, VMEM, HBM],
+        scratch=[
+            pltpu.VMEM((top, top), BF16),
+            pltpu.VMEM((top, top), BF16),
+            pltpu.SemaphoreType.DMA((2,)),
+        ],
         flops=12 * rhs * top**2,
-    )(partial, packed)
+    )(partial, packed, store)
     reduced = kernel_call(
         lift, shape(ROW, rhs, width), [VMEM] * 4, flops=6 * rhs * top * width
     )(top_solution, across, rows, solved)
 
     reduced = lax.all_to_all(reduced, "ga", 0, 0, axis_index_groups=x_groups)
-    own, sent, nh, nl = kernel_call(
+    own, sent = kernel_call(
         row_backward,
-        (shape(rhs, width), shape(rhs, width)) + pair(ROW, width, width),
-        [VMEM, HBM],
-        scratch=[pltpu.SemaphoreType.DMA((2, ROW))],
+        (shape(rhs, width), shape(rhs, width)),
+        [VMEM] * 3,
         flops=24 * rhs * width**2,
-    )(reduced, store)
+    )(reduced, nh, nl)
     coming = hop(sent, -1)
     settled, zh, zl = kernel_call(
         tail,

time: 173 us -> 172 us (level)
  no operation moved by 1% of the time
where the time goes in v5:
time: 172 us; the launch traced here: 171 us
  blocking collectives  59.6 us (35%)
  starting transfers between devices  39.9 us (23%)
  waiting for transfers between devices  31.6 us (18%)
  Pallas kernels  20.8 us (12%)
  between operations  14.9 us (9%)
  local copies, waits for them, and re-layouts  4.72 us (3%)
    all_to_all x2, blocking collectives, shards(): partial = lax.all_to_all(partial, 'ga', 0, 0)  32.4 us
    ppermute x6, waiting for transfers between devices, ring(): lax.ppermute(value, 'ga', [(i, i // ROW * ROW + (i + step) % ROW) for i i...  20.8 us
    ppermute x6, starting transfers between devices, ring(): lax.ppermute(value, 'ga', [(i, i // ROW * ROW + (i + step) % ROW) for i i...  19.9 us
    ppermute x6, starting transfers between devices, hop(): return lax.ppermute(value, 'ga', route)  19.9 us
    all_to_all x1, blocking collectives, shards(): partial = lax.all_to_all(partial, 'gz', 0, 0)  18.1 us
    ppermute x6, waiting for transfers between devices, hop(): return lax.ppermute(value, 'ga', route)  10.7 us
    all_to_all x1, blocking collectives, shards(): reduced = lax.all_to_all(reduced, 'ga', 0, 0, axis_index_groups=x_groups)  9.07 us
    unnamed x18, local copies, waits for them, and re-layouts  4.72 us
  transfers between devices with their start and end apart: 14, of which 8 were waited for; matrix products, arithmetic and copies ran while one was open for 0% of the time, Pallas kernels for 6%

profile of v5, /device:TPU:8, one launch (start us, length us, event | category | flops | bytes accessed | tf_op | source)
XLA Modules:
  0.0 171.4 jit_solution(6044167223062615414)
XLA Ops:
  7.9 3.3 %shard_map.95 = (f32[272,512]{1,0:T(8,128)}, f32[272,512]{1,0:T(8,128)}) custom-call(s32[1,1]{1,0:T(1,128)S(6)} %copy.10.live, f32[32,512]{1,0:T(8,128)} %bitcast.18, f32[512,512]{1,0:T(8,128)} %bitcast.14, f32[512,512]{1,0:T(8,128)} %bitcast.17), custom_call_target="tpu_custom_call" | custom-call | flops 805306368 | bytes 4194304 | tf_op jit(solution)/shard_map/pallas_call | solution.py:340
  11.3 3.4 %collective-permute-start.2 = (f32[272,512]{1,0:T(8,128)}, f32[272,512]{1,0:T(8,128)S(1)}, u32[]{:S(2)}, u32[]{:S(2)}) collective-permute-start(f32[272,512]{1,0:T(8,128)} %get-tuple-element.33.a0), channel_id=1, source_target_pairs={{0,1},{1,2},{2,3},{3,0},{4,5},{5,6},{6,7},{7,4},{8,9},{9,10},{10,1... | collective-permute-start | bytes 1671176 | tf_op jit(solution)/shard_map/ppermute | solution.py:324
  14.7 3.7 %collective-permute-start.1 = (f32[272,512]{1,0:T(8,128)}, f32[272,512]{1,0:T(8,128)S(1)}, u32[]{:S(2)}, u32[]{:S(2)}) collective-permute-start(f32[272,512]{1,0:T(8,128)} %get-tuple-element.34.b0), channel_id=1, source_target_pairs={{0,3},{1,0},{2,1},{3,2},{4,7},{5,4},{6,5},{7,6},{8,11},{9,8},{10,9... | collective-permute-start | bytes 1671176 | tf_op jit(solution)/shard_map/ppermute | solution.py:324
  18.3 3.5 %collective-permute-start = (f32[272,512]{1,0:T(8,128)}, f32[272,512]{1,0:T(8,128)S(1)}, u32[]{:S(2)}, u32[]{:S(2)}) collective-permute-start(f32[272,512]{1,0:T(8,128)} %get-tuple-element.33.a0), channel_id=1, source_target_pairs={{0,3},{1,0},{2,1},{3,2},{4,7},{5,4},{6,5},{7,6},{8,11},{9,8},{10,9... | collective-permute-start | bytes 1671176 | tf_op jit(solution)/shard_map/ppermute | solution.py:324
  24.2 5.9 %collective-permute-done.2.a3 = f32[272,512]{1,0:T(8,128)S(1)} collective-permute-done((f32[272,512]{1,0:T(8,128)}, f32[272,512]{1,0:T(8,128)S(1)}, u32[]{:S(2)}, u32[]{:S(2)}) %collective-permute-start.2) | collective-permute-done | bytes 557088 | tf_op jit(solution)/shard_map/ppermute | solution.py:324
  32.3 4.8 %collective-permute-start.5 = (f32[272,512]{1,0:T(8,128)S(1)}, f32[272,512]{1,0:T(8,128)S(1)}, u32[]{:S(2)}, u32[]{:S(2)}) collective-permute-start(f32[272,512]{1,0:T(8,128)S(1)} %collective-permute-done.1.b1), channel_id=1, source_target_pairs={{0,3},{1,0},{2,1},{3,2},{4,7},{5,4},{6,5},{7,6},{8,11},{9,8},{10,9... | collective-permute-start | bytes 1671176 | tf_op jit(solution)/shard_map/ppermute | solution.py:324
  37.2 7.1 %collective-permute-done.a1 = f32[272,512]{1,0:T(8,128)S(1)} collective-permute-done((f32[272,512]{1,0:T(8,128)}, f32[272,512]{1,0:T(8,128)S(1)}, u32[]{:S(2)}, u32[]{:S(2)}) %collective-permute-start) | collective-permute-done | bytes 557088 | tf_op jit(solution)/shard_map/ppermute | solution.py:324
  47.0 5.9 %collective-permute-done.4.a2 = f32[272,512]{1,0:T(8,128)S(1)} collective-permute-done((f32[272,512]{1,0:T(8,128)S(1)}, f32[272,512]{1,0:T(8,128)S(1)}, u32[]{:S(2)}, u32[]{:S(2)}) %collective-permute-start.4) | collective-permute-done | bytes 557088 | tf_op jit(solution)/shard_map/ppermute | solution.py:324
  56.2 3.5 %collective-permute-start.6 = (f32[32,512]{1,0:T(8,128)S(1)}, f32[32,512]{1,0:T(8,128)S(1)}, u32[]{:S(2)}, u32[]{:S(2)}) collective-permute-start(f32[32,512]{1,0:T(8,128)S(1)} %get-tuple-element.39.base), channel_id=1, source_target_pairs={{0,4},{1,5},{2,6},{3,7},{4,8},{5,9},{6,10},{7,11},{8,12},{9,13},{1... | collective-permute-start | bytes 196616 | tf_op jit(solution)/shard_map/ppermute | solution.py:334
  59.7 3.2 %shard_map.98 = (bf16[4,512,512]{2,1,0:T(8,128)(2,1)S(1)}, bf16[128,512,512]{2,1,0:T(8,128)(2,1)}) custom-call(bf16[4,512,512]{2,1,0:T(8,128)(2,1)S(1)} %get-tuple-element.41.nh, bf16[4,512,512]{2,1,0:T(8,128)(2,1)S(1)} %get-tuple-element.42.nl), custom_call_target="tpu_custom_call" | custom-call | flops 2415919104 | bytes 6291456 | tf_op jit(solution)/shard_map/pallas_call | solution.py:380
  63.5 3.6 %collective-permute-start.7 = (f32[32,512]{1,0:T(8,128)S(1)}, f32[32,512]{1,0:T(8,128)S(1)}, u32[]{:S(2)}, u32[]{:S(2)}) collective-permute-start(f32[32,512]{1,0:T(8,128)S(1)} %shard_map.100), channel_id=1, source_target_pairs={{0,4},{1,5},{2,6},{3,7},{4,8},{5,9},{6,10},{7,11},{8,12},{9,13},{1... | collective-permute-start | bytes 196616 | tf_op jit(solution)/shard_map/ppermute | solution.py:334
  70.2 3.5 %collective-permute-start.8 = (f32[32,512]{1,0:T(8,128)S(1)}, f32[32,512]{1,0:T(8,128)S(1)}, u32[]{:S(2)}, u32[]{:S(2)}) collective-permute-start(f32[32,512]{1,0:T(8,128)S(1)} %shard_map.101), channel_id=1, source_target_pairs={{0,4},{1,5},{2,6},{3,7},{4,8},{5,9},{6,10},{7,11},{8,12},{9,13},{1... | collective-permute-start | bytes 196616 | tf_op jit(solution)/shard_map/ppermute | solution.py:334
  73.7 2.7 %collective-permute-done.8.coming = f32[32,512]{1,0:T(8,128)S(1)} collective-permute-done((f32[32,512]{1,0:T(8,128)S(1)}, f32[32,512]{1,0:T(8,128)S(1)}, u32[]{:S(2)}, u32[]{:S(2)}) %collective-permute-start.8) | collective-permute-done | bytes 65568 | tf_op jit(solution)/shard_map/ppermute | solution.py:334
  77.4 18.1 %all_to_all.20.pieces = f32[32,8,128]{2,1,0:T(8,128)S(1)} all-to-all(f32[32,8,128]{2,1,0:T(8,128)S(1)} %get-tuple-element.48), channel_id=1, replica_groups=mesh['gz'=16,'ga'=32] {'ga'}, dimensions={0} | all-to-all | bytes 262144 | tf_op jit(solution)/shard_map/all_to_all | solution.py:412
  95.6 18.1 %all_to_all.21.pieces = f32[16,8,128]{2,1,0:T(8,128)S(1)} all-to-all(f32[16,8,128]{2,1,0:T(8,128)S(1)} %shard_map.103), channel_id=1, replica_groups=mesh['gz'=16,'ga'=32] {'gz'}, dimensions={0} | all-to-all | bytes 131072 | tf_op jit(solution)/shard_map/all_to_all | solution.py:414
  113.7 14.3 %all_to_all.22.tiles = f32[32,8,128]{2,1,0:T(8,128)S(1)} all-to-all(f32[32,8,128]{2,1,0:T(8,128)S(1)} %shard_map.104), channel_id=1, replica_groups=mesh['gz'=16,'ga'=32] {'ga'}, dimensions={0} | all-to-all | bytes 262144 | tf_op jit(solution)/shard_map/all_to_all | solution.py:416
  129.7 3.0 %shard_map.105 = (f32[32,1024]{1,0:T(8,128)}, bf16[4,512,512]{2,1,0:T(8,128)(2,1)S(1)}, bf16[4,512,512]{2,1,0:T(8,128)(2,1)S(1)}) custom-call(f32[32,8,128]{2,1,0:T(8,128)S(1)} %all_to_all.22.tiles, f32[4,32,4608]{2,1,0:T(8,128)S(1)} %bitcast.8, bf16[128,512,512]{2,1,0:T(8,128)(2,1)} %get-tuple-element.52.store), custom_call_target="tpu_custom_call" | custom-call | flops 402653184 | tf_op jit(solution)/shard_map/pallas_call | solution.py:418
  134.1 9.1 %all_to_all.23.reduced = f32[4,32,512]{2,1,0:T(8,128)S(1)} all-to-all(f32[4,32,512]{2,1,0:T(8,128)S(1)} %shard_map.106), channel_id=1, replica_groups={{0,1,2,3},{4,5,6,7},{8,9,10,11},{12,13,14,15},{16,17,18,19},{20,21,22,2..., dimensions={0} | all-to-all | bytes 524288 | tf_op jit(solution)/shard_map/all_to_all | solution.py:433
  144.3 3.2 %collective-permute-start.9 = (f32[32,512]{1,0:T(8,128)S(1)}, f32[32,512]{1,0:T(8,128)S(1)}, u32[]{:S(2)}, u32[]{:S(2)}) collective-permute-start(f32[32,512]{1,0:T(8,128)S(1)} %get-tuple-element.59.base), channel_id=1, source_target_pairs={{4,0},{5,1},{6,2},{7,3},{8,4},{9,5},{10,6},{11,7},{12,8},{13,9},{1... | collective-permute-start | bytes 196616 | tf_op jit(solution)/shard_map/ppermute | solution.py:334
  147.5 3.1 %collective-permute-done.9.coming = f32[32,512]{1,0:T(8,128)S(1)} collective-permute-done((f32[32,512]{1,0:T(8,128)S(1)}, f32[32,512]{1,0:T(8,128)S(1)}, u32[]{:S(2)}, u32[]{:S(2)}) %collective-permute-start.9) | collective-permute-done | bytes 65568 | tf_op jit(solution)/shard_map/ppermute | solution.py:334
  150.9 3.1 %collective-permute-start.10 = (f32[32,512]{1,0:T(8,128)S(1)}, f32[32,512]{1,0:T(8,128)S(1)}, u32[]{:S(2)}, u32[]{:S(2)}) collective-permute-start(f32[32,512]{1,0:T(8,128)S(1)} %shard_map.109), channel_id=1, source_target_pairs={{4,0},{5,1},{6,2},{7,3},{8,4},{9,5},{10,6},{11,7},{12,8},{13,9},{1... | collective-permute-start | bytes 196616 | tf_op jit(solution)/shard_map/ppermute | solution.py:334
  153.9 3.1 %collective-permute-done.10.coming = f32[32,512]{1,0:T(8,128)S(1)} collective-permute-done((f32[32,512]{1,0:T(8,128)S(1)}, f32[32,512]{1,0:T(8,128)S(1)}, u32[]{:S(2)}, u32[]{:S(2)}) %collective-permute-start.10) | collective-permute-done | bytes 65568 | tf_op jit(solution)/shard_map/ppermute | solution.py:334
  157.3 3.1 %collective-permute-start.11 = (f32[32,512]{1,0:T(8,128)S(1)}, f32[32,512]{1,0:T(8,128)S(1)}, u32[]{:S(2)}, u32[]{:S(2)}) collective-permute-start(f32[32,512]{1,0:T(8,128)S(1)} %shard_map.110), channel_id=1, source_target_pairs={{4,0},{5,1},{6,2},{7,3},{8,4},{9,5},{10,6},{11,7},{12,8},{13,9},{1... | collective-permute-start | bytes 196616 | tf_op jit(solution)/shard_map/ppermute | solution.py:334
  160.4 3.3 %shard_map.108 = (f32[32,512]{1,0:T(8,128)S(1)}, bf16[512,512]{1,0:T(8,128)(2,1)S(1)}, bf16[512,512]{1,0:T(8,128)(2,1)S(1)}) custom-call(s32[1,1]{1,0:T(1,128)S(6)} %copy.10.live, f32[32,512]{1,0:T(8,128)S(1)} %get-tuple-element.57.own, bf16[4,512,512]{2,1,0:T(8,128)(2,1)S(1)} %get-tuple-element.55.nh, bf16[4,512,512]{2,1,0:T(8,128)(2,1)S(1)} %get-tuple-element.56.nl, ...), custom_call_target="tpu_custom_call" | custom-call | flops 2415919104 | bytes 6291456 | tf_op jit(solution)/shard_map/pallas_call | solution.py:441
  (45 shorter events, 21.1 us)
Async XLA Ops:
  7.2 55.8 %all-gather.5.cloned.1.call-start = ((), (), s32[]{:S(2)}) async-start(), calls=%async_computation.4 | async-start | bytes 1179648 | tf_op jit(solution)/shard_map/all_gather | solution.py:358
  11.2 116.8 %all-gather.7.cloned.1.call-start = ((), (), s32[]{:S(2)}) async-start(), calls=%async_computation.5 | async-start | bytes 2949120 | tf_op jit(solution)/shard_map/all_gather | solution.py:403
  11.3 18.8 %collective-permute-start.2 = (f32[272,512]{1,0:T(8,128)}, f32[272,512]{1,0:T(8,128)S(1)}, u32[]{:S(2)}, u32[]{:S(2)}) collective-permute-start(f32[272,512]{1,0:T(8,128)} %get-tuple-element.33.a0), channel_id=1, source_target_pairs={{0,1},{1,2},{2,3},{3,0},{4,5},{5,6},{6,7},{7,4},{8,9},{9,10},{10,1... | collective-permute-start | bytes 1671176 | tf_op jit(solution)/shard_map/ppermute | solution.py:324
  14.7 17.7 %collective-permute-start.1 = (f32[272,512]{1,0:T(8,128)}, f32[272,512]{1,0:T(8,128)S(1)}, u32[]{:S(2)}, u32[]{:S(2)}) collective-permute-start(f32[272,512]{1,0:T(8,128)} %get-tuple-element.34.b0), channel_id=1, source_target_pairs={{0,3},{1,0},{2,1},{3,2},{4,7},{5,4},{6,5},{7,6},{8,11},{9,8},{10,9... | collective-permute-start | bytes 1671176 | tf_op jit(solution)/shard_map/ppermute | solution.py:324
  18.3 25.9 %collective-permute-start = (f32[272,512]{1,0:T(8,128)}, f32[272,512]{1,0:T(8,128)S(1)}, u32[]{:S(2)}, u32[]{:S(2)}) collective-permute-start(f32[272,512]{1,0:T(8,128)} %get-tuple-element.33.a0), channel_id=1, source_target_pairs={{0,3},{1,0},{2,1},{3,2},{4,7},{5,4},{6,5},{7,6},{8,11},{9,8},{10,9... | collective-permute-start | bytes 1671176 | tf_op jit(solution)/shard_map/ppermute | solution.py:324
  21.8 22.5 %collective-permute-start.3 = (f32[272,512]{1,0:T(8,128)}, f32[272,512]{1,0:T(8,128)S(1)}, u32[]{:S(2)}, u32[]{:S(2)}) collective-permute-start(f32[272,512]{1,0:T(8,128)} %get-tuple-element.34.b0), channel_id=1, source_target_pairs={{0,1},{1,2},{2,3},{3,0},{4,5},{5,6},{6,7},{7,4},{8,9},{9,10},{10,1... | collective-permute-start | bytes 1671176 | tf_op jit(solution)/shard_map/ppermute | solution.py:324
  30.1 22.7 %collective-permute-start.4 = (f32[272,512]{1,0:T(8,128)S(1)}, f32[272,512]{1,0:T(8,128)S(1)}, u32[]{:S(2)}, u32[]{:S(2)}) collective-permute-start(f32[272,512]{1,0:T(8,128)S(1)} %collective-permute-done.2.a3), channel_id=1, source_target_pairs={{0,1},{1,2},{2,3},{3,0},{4,5},{5,6},{6,7},{7,4},{8,9},{9,10},{10,1... | collective-permute-start | bytes 1671176 | tf_op jit(solution)/shard_map/ppermute | solution.py:324
  32.3 22.4 %collective-permute-start.5 = (f32[272,512]{1,0:T(8,128)S(1)}, f32[272,512]{1,0:T(8,128)S(1)}, u32[]{:S(2)}, u32[]{:S(2)}) collective-permute-start(f32[272,512]{1,0:T(8,128)S(1)} %collective-permute-done.1.b1), channel_id=1, source_target_pairs={{0,3},{1,0},{2,1},{3,2},{4,7},{5,4},{6,5},{7,6},{8,11},{9,8},{10,9... | collective-permute-start | bytes 1671176 | tf_op jit(solution)/shard_map/ppermute | solution.py:324
  44.3 1.1 copy-start.3
  45.3 1.1 copy-start.4
  56.2 6.7 %collective-permute-start.6 = (f32[32,512]{1,0:T(8,128)S(1)}, f32[32,512]{1,0:T(8,128)S(1)}, u32[]{:S(2)}, u32[]{:S(2)}) collective-permute-start(f32[32,512]{1,0:T(8,128)S(1)} %get-tuple-element.39.base), channel_id=1, source_target_pairs={{0,4},{1,5},{2,6},{3,7},{4,8},{5,9},{6,10},{7,11},{8,12},{9,13},{1... | collective-permute-start | bytes 196616 | tf_op jit(solution)/shard_map/ppermute | solution.py:334
  63.0 4.1 %copy-start.2 = (f32[256,1024]{1,0:T(8,128)S(1)}, f32[256,1024]{1,0:T(8,128)}, u32[]{:S(2)}) copy-start(f32[256,1024]{1,0:T(8,128)} %all-gather.5.cloned.1.call-done) | copy-start | bytes 3145732
  63.4 12.9 %copy-start.1 = (f32[1,1,256,512]{3,2,1,0:T(8,128)S(1)}, f32[1,1,256,512]{3,2,1,0:T(8,128)}, u32[]{:S(2)}) copy-start(f32[1,1,256,512]{3,2,1,0:T(8,128)} %param.11) | copy-start | bytes 1572868
  63.4 12.9 %copy-start.5 = (f32[32,1024]{1,0:T(8,128)S(1)}, f32[32,1024]{1,0:T(8,128)}, u32[]{:S(2)}) copy-start(f32[32,1024]{1,0:T(8,128)} %top_right.1) | copy-start | bytes 393220
  63.4 12.9 %copy-start.7 = (s32[1,1,256]{2,1,0:T(1,128)S(1)}, s32[1,1,256]{2,1,0:T(1,128)}, u32[]{:S(2)}) copy-start(s32[1,1,256]{2,1,0:T(1,128)} %param.12) | copy-start | bytes 3076
  63.5 6.3 %collective-permute-start.7 = (f32[32,512]{1,0:T(8,128)S(1)}, f32[32,512]{1,0:T(8,128)S(1)}, u32[]{:S(2)}, u32[]{:S(2)}) collective-permute-start(f32[32,512]{1,0:T(8,128)S(1)} %shard_map.100), channel_id=1, source_target_pairs={{0,4},{1,5},{2,6},{3,7},{4,8},{5,9},{6,10},{7,11},{8,12},{9,13},{1... | collective-permute-start | bytes 196616 | tf_op jit(solution)/shard_map/ppermute | solution.py:334
  70.2 6.2 %collective-permute-start.8 = (f32[32,512]{1,0:T(8,128)S(1)}, f32[32,512]{1,0:T(8,128)S(1)}, u32[]{:S(2)}, u32[]{:S(2)}) collective-permute-start(f32[32,512]{1,0:T(8,128)S(1)} %shard_map.101), channel_id=1, source_target_pairs={{0,4},{1,5},{2,6},{3,7},{4,8},{5,9},{6,10},{7,11},{8,12},{9,13},{1... | collective-permute-start | bytes 196616 | tf_op jit(solution)/shard_map/ppermute | solution.py:334
  128.0 1.7 copy-start
  132.7 0.9 copy-start.6
  144.3 16.1 %copy-start.8 = (f32[1,1,512,512]{3,2,1,0:T(8,128)S(1)}, f32[1,1,512,512]{3,2,1,0:T(8,128)}, u32[]{:S(2)}) copy-start(f32[1,1,512,512]{3,2,1,0:T(8,128)} %param.9) | copy-start | bytes 3145732
  144.3 6.3 %collective-permute-start.9 = (f32[32,512]{1,0:T(8,128)S(1)}, f32[32,512]{1,0:T(8,128)S(1)}, u32[]{:S(2)}, u32[]{:S(2)}) collective-permute-start(f32[32,512]{1,0:T(8,128)S(1)} %get-tuple-element.59.base), channel_id=1, source_target_pairs={{4,0},{5,1},{6,2},{7,3},{8,4},{9,5},{10,6},{11,7},{12,8},{13,9},{1... | collective-permute-start | bytes 196616 | tf_op jit(solution)/shard_map/ppermute | solution.py:334
  150.9 6.2 %collective-permute-start.10 = (f32[32,512]{1,0:T(8,128)S(1)}, f32[32,512]{1,0:T(8,128)S(1)}, u32[]{:S(2)}, u32[]{:S(2)}) collective-permute-start(f32[32,512]{1,0:T(8,128)S(1)} %shard_map.109), channel_id=1, source_target_pairs={{4,0},{5,1},{6,2},{7,3},{8,4},{9,5},{10,6},{11,7},{12,8},{13,9},{1... | collective-permute-start | bytes 196616 | tf_op jit(solution)/shard_map/ppermute | solution.py:334
  157.3 6.4 %collective-permute-start.11 = (f32[32,512]{1,0:T(8,128)S(1)}, f32[32,512]{1,0:T(8,128)S(1)}, u32[]{:S(2)}, u32[]{:S(2)}) collective-permute-start(f32[32,512]{1,0:T(8,128)S(1)} %shard_map.110), channel_id=1, source_target_pairs={{4,0},{5,1},{6,2},{7,3},{8,4},{9,5},{10,6},{11,7},{12,8},{13,9},{1... | collective-permute-start | bytes 196616 | tf_op jit(solution)/shard_map/ppermute | solution.py:334
Sparse Core Ops, SparseCore 0:
  11.3 45.3 all-gather.4
  69.9 41.8 all-gather.6

commit v6 on v5

--- a/solution.py
+++ b/solution.py
@@ -191,9 +191,11 @@
     return (lax.broadcasted_iota(jnp.int32, (top, rows.shape[1]), 0) == rows[...]).astype(F32).astype(BF16)
 
 
-def contribute(group, coming, products, across, rows, top_right, solved, tiles):
+def contribute(group, products, across, rows, top_right, *others):
+    *came, solved, tiles = others
     here = place_in_row()
-    value = group[here] + dot3(split(coming[...]), (products[0], products[1]), NT)
+    coming = sum(block[...] for block in came)
+    value = group[here] + dot3(split(coming), (products[0], products[1]), NT)
     solved[...] = value
     pushed = dot3(split(value), split(across[...]), NT)
     count, depth, lanes = tiles.shape
@@ -302,8 +304,10 @@
             zl[...] = low
 
 
-def finish(settled, coming, zh, zl, out):
-    out[...] = settled[...] + dot3(split(coming[...]), (zh[...], zl[...]), NN)
+def finish(settled, zh, zl, *others):
+    *came, out = others
+    coming = sum(block[...] for block in came)
+    out[...] = settled[...] + dot3(split(coming), (zh[...], zl[...]), NN)
 
 
 def shards(
@@ -325,12 +329,8 @@
             value, "ga", [(i, i // ROW * ROW + (i + step) % ROW) for i in range(ga)]
         )
 
-    def hop(value, step):
-        route = [
-            (i, i + step * ROW)
-            for i in range(ga)
-            if 0 <= i // ROW % chain_rows + step < chain_rows
-        ]
+    def hop(value, row, step):
+        route = [(i, i + step * ROW) for i in range(ga) if i // ROW % chain_rows == row]
         return lax.ppermute(value, "ga", route)
 
     def pair(*dims):
@@ -376,7 +376,7 @@
         flops=24 * rhs * width**2,
         nbytes=32 * width**2,
     )(*staged, a2, b2)
-    coming = hop(last, 1)
+    came = [hop(last, 0, 1)]
     products, store = kernel_call(
         multiply_up,
         (shape(4, width, width, kind=BF16), shape(STORE, width, width, kind=BF16)),
@@ -386,29 +386,29 @@
         flops=18 * width**3,
         nbytes=24 * width**2,
     )(nh, nl)
-    blocks, coming, products = lax.optimization_barrier((blocks, coming, products))
+    blocks, came[0], products = lax.optimization_barrier((blocks, came[0], products))
     packed = kernel_call(
         pack_lower,
         shape(top_inverse.shape[0], top * (ga // ROW + 1) // 2),
         [VMEM],
         nbytes=2 * top**2,
     )(blocks)
-    for step in range(chain_rows - 2):
+    for row in range(1, chain_rows - 1):
         moved = kernel_call(
             hop_forward, shape(rhs, width), [VMEM] * 3, flops=6 * rhs * width**2
-        )(last, coming, products)
-        coming = hop(moved, 1)
-        if step == 0:
-            packed, coming = lax.optimization_barrier((packed, coming))
+        )(last, came[-1], products)
+        came.append(hop(moved, row, 1))
+        if row == 1:
+            packed, came[-1] = lax.optimization_barrier((packed, came[-1]))
     packed = lax.all_gather(packed, "ga", axis_index_groups=x_groups)
 
     tiles = (ga, rhs * top // ga // 128, 128)
     solved, partial = kernel_call(
         contribute,
         (shape(rhs, width), shape(*tiles)),
-        [VMEM] * 6,
+        [VMEM] * (5 + len(came)),
         flops=12 * rhs * width**2,
-    )(group, coming, products, across, rows, top_right)
+    )(group, products, across, rows, top_right, *came)
     partial = lax.all_to_all(partial, "ga", 0, 0)
     partial = kernel_call(total_of, shape(gz, *tiles[1:]), [VMEM])(partial)
     partial = lax.all_to_all(partial, "gz", 0, 0)
@@ -437,7 +437,7 @@
         [VMEM] * 3,
         flops=24 * rhs * width**2,
     )(reduced, nh, nl)
-    coming = hop(sent, -1)
+    came = [hop(sent, chain_rows - 1, -1)]
     settled, zh, zl = kernel_call(
         tail,
         (shape(rhs, width),) + pair(width, width),
@@ -445,14 +445,14 @@
         flops=18 * width**3,
         nbytes=24 * width**2,
     )(live_cols, own, nh, nl, inverse)
-    for _ in range(chain_rows - 2):
+    for row in range(chain_rows - 2, 0, -1):
         moved = kernel_call(
             hop_backward, shape(rhs, width), [VMEM] * 3, flops=6 * rhs * width**2
-        )(sent, coming, products)
-        coming = hop(moved, -1)
+        )(sent, came[-1], products)
+        came.append(hop(moved, row, -1))
     result = kernel_call(
-        finish, shape(rhs, width), [VMEM] * 4, flops=6 * rhs * width**2
-    )(settled, coming, zh, zl)
+        finish, shape(rhs, width), [VMEM] * (3 + len(came)), flops=6 * rhs * width**2
+    )(settled, zh, zl, *came)
     return (result[None, None], top_solution)
 
 

time: 172 us -> 164 us (0.953)
  starting transfers between devices: 39.9 us -> 26.8 us
  blocking collectives: 59.6 us -> 64.5 us
    ppermute x6, starting transfers between devices: 19.9 us -> 6.78 us  [hop(): return lax.ppermute(value, 'ga', route)]
    all_to_all x2, blocking collectives: 32.4 us -> 37.3 us  [shards(): partial = lax.all_to_all(partial, 'ga', 0, 0)]
  transfers between devices with their start and end apart: 14 -> 14, of which waited for: 8 -> 7; matrix products, arithmetic and copies ran while one was open for 0% -> 0% of each run, Pallas kernels for 6% -> 7%
where the time goes in v6:
time: 164 us; the launch traced here: 163 us
  blocking collectives  64.5 us (39%)
  waiting for transfers between devices  31.7 us (19%)
  starting transfers between devices  26.8 us (16%)
  Pallas kernels  20.8 us (13%)
  between operations  14.9 us (9%)
  local copies, waits for them, and re-layouts  4.72 us (3%)
    all_to_all x2, blocking collectives, shards(): partial = lax.all_to_all(partial, 'ga', 0, 0)  37.3 us
    ppermute x6, waiting for transfers between devices, ring(): lax.ppermute(value, 'ga', [(i, i // ROW * ROW + (i + step) % ROW) for i i...  20.8 us
    ppermute x6, starting transfers between devices, ring(): lax.ppermute(value, 'ga', [(i, i // ROW * ROW + (i + step) % ROW) for i i...  19.9 us
    all_to_all x1, blocking collectives, shards(): partial = lax.all_to_all(partial, 'gz', 0, 0)  18.1 us
    ppermute x6, waiting for transfers between devices, hop(): return lax.ppermute(value, 'ga', route)  10.9 us
    all_to_all x1, blocking collectives, shards(): reduced = lax.all_to_all(reduced, 'ga', 0, 0, axis_index_groups=x_groups)  9.07 us
    ppermute x6, starting transfers between devices, hop(): return lax.ppermute(value, 'ga', route)  6.78 us
    unnamed x18, local copies, waits for them, and re-layouts  4.72 us
  transfers between devices with their start and end apart: 14, of which 7 were waited for; matrix products, arithmetic and copies ran while one was open for 0% of the time, Pallas kernels for 7%

profile of v6, /device:TPU:8, one launch (start us, length us, event | category | flops | bytes accessed | tf_op | source)
XLA Modules:
  0.0 163.4 jit_solution(14914647283494624821)
XLA Ops:
  7.9 3.3 %shard_map.95 = (f32[272,512]{1,0:T(8,128)}, f32[272,512]{1,0:T(8,128)}) custom-call(s32[1,1]{1,0:T(1,128)S(6)} %copy.10.live, f32[32,512]{1,0:T(8,128)} %bitcast.18, f32[512,512]{1,0:T(8,128)} %bitcast.14, f32[512,512]{1,0:T(8,128)} %bitcast.17), custom_call_target="tpu_custom_call" | custom-call | flops 805306368 | bytes 4194304 | tf_op jit(solution)/shard_map/pallas_call | solution.py:340
  11.3 3.4 %collective-permute-start.2 = (f32[272,512]{1,0:T(8,128)}, f32[272,512]{1,0:T(8,128)S(1)}, u32[]{:S(2)}, u32[]{:S(2)}) collective-permute-start(f32[272,512]{1,0:T(8,128)} %get-tuple-element.33.a0), channel_id=1, source_target_pairs={{0,1},{1,2},{2,3},{3,0},{4,5},{5,6},{6,7},{7,4},{8,9},{9,10},{10,1... | collective-permute-start | bytes 1671176 | tf_op jit(solution)/shard_map/ppermute | solution.py:328
  14.7 3.7 %collective-permute-start.1 = (f32[272,512]{1,0:T(8,128)}, f32[272,512]{1,0:T(8,128)S(1)}, u32[]{:S(2)}, u32[]{:S(2)}) collective-permute-start(f32[272,512]{1,0:T(8,128)} %get-tuple-element.34.b0), channel_id=1, source_target_pairs={{0,3},{1,0},{2,1},{3,2},{4,7},{5,4},{6,5},{7,6},{8,11},{9,8},{10,9... | collective-permute-start | bytes 1671176 | tf_op jit(solution)/shard_map/ppermute | solution.py:328
  18.3 3.5 %collective-permute-start = (f32[272,512]{1,0:T(8,128)}, f32[272,512]{1,0:T(8,128)S(1)}, u32[]{:S(2)}, u32[]{:S(2)}) collective-permute-start(f32[272,512]{1,0:T(8,128)} %get-tuple-element.33.a0), channel_id=1, source_target_pairs={{0,3},{1,0},{2,1},{3,2},{4,7},{5,4},{6,5},{7,6},{8,11},{9,8},{10,9... | collective-permute-start | bytes 1671176 | tf_op jit(solution)/shard_map/ppermute | solution.py:328
  21.8 2.4 %collective-permute-start.3 = (f32[272,512]{1,0:T(8,128)}, f32[272,512]{1,0:T(8,128)S(1)}, u32[]{:S(2)}, u32[]{:S(2)}) collective-permute-start(f32[272,512]{1,0:T(8,128)} %get-tuple-element.34.b0), channel_id=1, source_target_pairs={{0,1},{1,2},{2,3},{3,0},{4,5},{5,6},{6,7},{7,4},{8,9},{9,10},{10,1... | collective-permute-start | bytes 1671176 | tf_op jit(solution)/shard_map/ppermute | solution.py:328
  24.2 5.9 %collective-permute-done.2.a3 = f32[272,512]{1,0:T(8,128)S(1)} collective-permute-done((f32[272,512]{1,0:T(8,128)}, f32[272,512]{1,0:T(8,128)S(1)}, u32[]{:S(2)}, u32[]{:S(2)}) %collective-permute-start.2) | collective-permute-done | bytes 557088 | tf_op jit(solution)/shard_map/ppermute | solution.py:328
  30.1 2.2 %collective-permute-start.4 = (f32[272,512]{1,0:T(8,128)S(1)}, f32[272,512]{1,0:T(8,128)S(1)}, u32[]{:S(2)}, u32[]{:S(2)}) collective-permute-start(f32[272,512]{1,0:T(8,128)S(1)} %collective-permute-done.2.a3), channel_id=1, source_target_pairs={{0,1},{1,2},{2,3},{3,0},{4,5},{5,6},{6,7},{7,4},{8,9},{9,10},{10,1... | collective-permute-start | bytes 1671176 | tf_op jit(solution)/shard_map/ppermute | solution.py:328
  32.3 4.8 %collective-permute-start.5 = (f32[272,512]{1,0:T(8,128)S(1)}, f32[272,512]{1,0:T(8,128)S(1)}, u32[]{:S(2)}, u32[]{:S(2)}) collective-permute-start(f32[272,512]{1,0:T(8,128)S(1)} %collective-permute-done.1.b1), channel_id=1, source_target_pairs={{0,3},{1,0},{2,1},{3,2},{4,7},{5,4},{6,5},{7,6},{8,11},{9,8},{10,9... | collective-permute-start | bytes 1671176 | tf_op jit(solution)/shard_map/ppermute | solution.py:328
  37.2 7.1 %collective-permute-done.a1 = f32[272,512]{1,0:T(8,128)S(1)} collective-permute-done((f32[272,512]{1,0:T(8,128)}, f32[272,512]{1,0:T(8,128)S(1)}, u32[]{:S(2)}, u32[]{:S(2)}) %collective-permute-start) | collective-permute-done | bytes 557088 | tf_op jit(solution)/shard_map/ppermute | solution.py:328
  47.0 5.9 %collective-permute-done.4.a2 = f32[272,512]{1,0:T(8,128)S(1)} collective-permute-done((f32[272,512]{1,0:T(8,128)S(1)}, f32[272,512]{1,0:T(8,128)S(1)}, u32[]{:S(2)}, u32[]{:S(2)}) %collective-permute-start.4) | collective-permute-done | bytes 557088 | tf_op jit(solution)/shard_map/ppermute | solution.py:328
  52.8 1.9 %collective-permute-done.5.b2 = f32[272,512]{1,0:T(8,128)S(1)} collective-permute-done((f32[272,512]{1,0:T(8,128)S(1)}, f32[272,512]{1,0:T(8,128)S(1)}, u32[]{:S(2)}, u32[]{:S(2)}) %collective-permute-start.5) | collective-permute-done | bytes 557088 | tf_op jit(solution)/shard_map/ppermute | solution.py:328
  54.7 1.5 shard_map.97
  57.5 3.2 %shard_map.98 = (bf16[4,512,512]{2,1,0:T(8,128)(2,1)S(1)}, bf16[128,512,512]{2,1,0:T(8,128)(2,1)}) custom-call(bf16[4,512,512]{2,1,0:T(8,128)(2,1)S(1)} %get-tuple-element.41.nh, bf16[4,512,512]{2,1,0:T(8,128)(2,1)S(1)} %get-tuple-element.42.nl), custom_call_target="tpu_custom_call" | custom-call | flops 2415919104 | bytes 6291456 | tf_op jit(solution)/shard_map/pallas_call | solution.py:380
  60.8 1.6 collective-permute-done.6.coming.others_0_
  62.8 1.4 collective-permute-start.7
  68.4 23.0 %all_to_all.20.pieces = f32[32,8,128]{2,1,0:T(8,128)S(1)} all-to-all(f32[32,8,128]{2,1,0:T(8,128)S(1)} %get-tuple-element.48), channel_id=1, replica_groups=mesh['gz'=16,'ga'=32] {'ga'}, dimensions={0} | all-to-all | bytes 262144 | tf_op jit(solution)/shard_map/all_to_all | solution.py:412
  91.4 18.1 %all_to_all.21.pieces = f32[16,8,128]{2,1,0:T(8,128)S(1)} all-to-all(f32[16,8,128]{2,1,0:T(8,128)S(1)} %shard_map.103), channel_id=1, replica_groups=mesh['gz'=16,'ga'=32] {'gz'}, dimensions={0} | all-to-all | bytes 131072 | tf_op jit(solution)/shard_map/all_to_all | solution.py:414
  109.6 14.3 %all_to_all.22.tiles = f32[32,8,128]{2,1,0:T(8,128)S(1)} all-to-all(f32[32,8,128]{2,1,0:T(8,128)S(1)} %shard_map.104), channel_id=1, replica_groups=mesh['gz'=16,'ga'=32] {'ga'}, dimensions={0} | all-to-all | bytes 262144 | tf_op jit(solution)/shard_map/all_to_all | solution.py:416
  123.8 1.7 %copy-done = f32[128,4608]{1,0:T(8,128)S(1)} copy-done((f32[128,4608]{1,0:T(8,128)S(1)}, f32[128,4608]{1,0:T(8,128)}, u32[]{:S(2)}) %copy-start) | copy-done | bytes 2359320
  125.5 3.0 %shard_map.105 = (f32[32,1024]{1,0:T(8,128)}, bf16[4,512,512]{2,1,0:T(8,128)(2,1)S(1)}, bf16[4,512,512]{2,1,0:T(8,128)(2,1)S(1)}) custom-call(f32[32,8,128]{2,1,0:T(8,128)S(1)} %all_to_all.22.tiles, f32[4,32,4608]{2,1,0:T(8,128)S(1)} %bitcast.8, bf16[128,512,512]{2,1,0:T(8,128)(2,1)} %get-tuple-element.52.store), custom_call_target="tpu_custom_call" | custom-call | flops 402653184 | tf_op jit(solution)/shard_map/pallas_call | solution.py:418
  129.9 9.1 %all_to_all.23.reduced = f32[4,32,512]{2,1,0:T(8,128)S(1)} all-to-all(f32[4,32,512]{2,1,0:T(8,128)S(1)} %shard_map.106), channel_id=1, replica_groups={{0,1,2,3},{4,5,6,7},{8,9,10,11},{12,13,14,15},{16,17,18,19},{20,21,22,2..., dimensions={0} | all-to-all | bytes 524288 | tf_op jit(solution)/shard_map/all_to_all | solution.py:433
  142.5 8.2 %collective-permute-done.10.coming.others_1_ = f32[32,512]{1,0:T(8,128)S(1)} collective-permute-done((f32[32,512]{1,0:T(8,128)S(1)}, f32[32,512]{1,0:T(8,128)S(1)}, u32[]{:S(2)}, u32[]{:S(2)}) %collective-permute-start.10) | collective-permute-done | bytes 65568 | tf_op jit(solution)/shard_map/ppermute | solution.py:334
  151.1 1.3 collective-permute-start.11
  152.4 3.3 %shard_map.108 = (f32[32,512]{1,0:T(8,128)S(1)}, bf16[512,512]{1,0:T(8,128)(2,1)S(1)}, bf16[512,512]{1,0:T(8,128)(2,1)S(1)}) custom-call(s32[1,1]{1,0:T(1,128)S(6)} %copy.10.live, f32[32,512]{1,0:T(8,128)S(1)} %get-tuple-element.57.own, bf16[4,512,512]{2,1,0:T(8,128)(2,1)S(1)} %get-tuple-element.55.nh, bf16[4,512,512]{2,1,0:T(8,128)(2,1)S(1)} %get-tuple-element.56.nl, ...), custom_call_target="tpu_custom_call" | custom-call | flops 2415919104 | bytes 6291456 | tf_op jit(solution)/shard_map/pallas_call | solution.py:441
  (45 shorter events, 14.8 us)
Async XLA Ops:
  7.2 55.2 %all-gather.5.cloned.1.call-start = ((), (), s32[]{:S(2)}) async-start(), calls=%async_computation.4 | async-start | bytes 1179648 | tf_op jit(solution)/shard_map/all_gather | solution.py:358
  11.2 112.6 %all-gather.7.cloned.1.call-start = ((), (), s32[]{:S(2)}) async-start(), calls=%async_computation.5 | async-start | bytes 2949120 | tf_op jit(solution)/shard_map/all_gather | solution.py:403
  11.3 18.8 %collective-permute-start.2 = (f32[272,512]{1,0:T(8,128)}, f32[272,512]{1,0:T(8,128)S(1)}, u32[]{:S(2)}, u32[]{:S(2)}) collective-permute-start(f32[272,512]{1,0:T(8,128)} %get-tuple-element.33.a0), channel_id=1, source_target_pairs={{0,1},{1,2},{2,3},{3,0},{4,5},{5,6},{6,7},{7,4},{8,9},{9,10},{10,1... | collective-permute-start | bytes 1671176 | tf_op jit(solution)/shard_map/ppermute | solution.py:328
  14.7 17.7 %collective-permute-start.1 = (f32[272,512]{1,0:T(8,128)}, f32[272,512]{1,0:T(8,128)S(1)}, u32[]{:S(2)}, u32[]{:S(2)}) collective-permute-start(f32[272,512]{1,0:T(8,128)} %get-tuple-element.34.b0), channel_id=1, source_target_pairs={{0,3},{1,0},{2,1},{3,2},{4,7},{5,4},{6,5},{7,6},{8,11},{9,8},{10,9... | collective-permute-start | bytes 1671176 | tf_op jit(solution)/shard_map/ppermute | solution.py:328
  18.3 25.9 %collective-permute-start = (f32[272,512]{1,0:T(8,128)}, f32[272,512]{1,0:T(8,128)S(1)}, u32[]{:S(2)}, u32[]{:S(2)}) collective-permute-start(f32[272,512]{1,0:T(8,128)} %get-tuple-element.33.a0), channel_id=1, source_target_pairs={{0,3},{1,0},{2,1},{3,2},{4,7},{5,4},{6,5},{7,6},{8,11},{9,8},{10,9... | collective-permute-start | bytes 1671176 | tf_op jit(solution)/shard_map/ppermute | solution.py:328
  21.8 22.5 %collective-permute-start.3 = (f32[272,512]{1,0:T(8,128)}, f32[272,512]{1,0:T(8,128)S(1)}, u32[]{:S(2)}, u32[]{:S(2)}) collective-permute-start(f32[272,512]{1,0:T(8,128)} %get-tuple-element.34.b0), channel_id=1, source_target_pairs={{0,1},{1,2},{2,3},{3,0},{4,5},{5,6},{6,7},{7,4},{8,9},{9,10},{10,1... | collective-permute-start | bytes 1671176 | tf_op jit(solution)/shard_map/ppermute | solution.py:328
  30.1 22.7 %collective-permute-start.4 = (f32[272,512]{1,0:T(8,128)S(1)}, f32[272,512]{1,0:T(8,128)S(1)}, u32[]{:S(2)}, u32[]{:S(2)}) collective-permute-start(f32[272,512]{1,0:T(8,128)S(1)} %collective-permute-done.2.a3), channel_id=1, source_target_pairs={{0,1},{1,2},{2,3},{3,0},{4,5},{5,6},{6,7},{7,4},{8,9},{9,10},{10,1... | collective-permute-start | bytes 1671176 | tf_op jit(solution)/shard_map/ppermute | solution.py:328
  32.3 22.4 %collective-permute-start.5 = (f32[272,512]{1,0:T(8,128)S(1)}, f32[272,512]{1,0:T(8,128)S(1)}, u32[]{:S(2)}, u32[]{:S(2)}) collective-permute-start(f32[272,512]{1,0:T(8,128)S(1)} %collective-permute-done.1.b1), channel_id=1, source_target_pairs={{0,3},{1,0},{2,1},{3,2},{4,7},{5,4},{6,5},{7,6},{8,11},{9,8},{10,9... | collective-permute-start | bytes 1671176 | tf_op jit(solution)/shard_map/ppermute | solution.py:328
  44.3 1.1 copy-start.3
  45.3 1.1 copy-start.4
  56.2 6.2 %collective-permute-start.6 = (f32[32,512]{1,0:T(8,128)S(1)}, f32[32,512]{1,0:T(8,128)S(1)}, u32[]{:S(2)}, u32[]{:S(2)}) collective-permute-start(f32[32,512]{1,0:T(8,128)S(1)} %get-tuple-element.40.base), channel_id=1, source_target_pairs={{0,4},{1,5},{2,6},{3,7},{16,20},{17,21},{18,22},{19,23},{32,36},{3... | collective-permute-start | bytes 196616 | tf_op jit(solution)/shard_map/ppermute | solution.py:334
  62.4 1.9 %copy-start.2 = (f32[256,1024]{1,0:T(8,128)S(1)}, f32[256,1024]{1,0:T(8,128)}, u32[]{:S(2)}) copy-start(f32[256,1024]{1,0:T(8,128)} %all-gather.5.cloned.1.call-done) | copy-start | bytes 3145732
  62.8 4.5 %copy-start.1 = (f32[1,1,256,512]{3,2,1,0:T(8,128)S(1)}, f32[1,1,256,512]{3,2,1,0:T(8,128)}, u32[]{:S(2)}) copy-start(f32[1,1,256,512]{3,2,1,0:T(8,128)} %param.11) | copy-start | bytes 1572868
  62.8 4.5 %copy-start.5 = (f32[32,1024]{1,0:T(8,128)S(1)}, f32[32,1024]{1,0:T(8,128)}, u32[]{:S(2)}) copy-start(f32[32,1024]{1,0:T(8,128)} %top_right.1) | copy-start | bytes 393220
  62.8 4.5 %copy-start.7 = (s32[1,1,256]{2,1,0:T(1,128)S(1)}, s32[1,1,256]{2,1,0:T(1,128)}, u32[]{:S(2)}) copy-start(s32[1,1,256]{2,1,0:T(1,128)} %param.12) | copy-start | bytes 3076
  62.8 3.3 %collective-permute-start.7 = (f32[32,512]{1,0:T(8,128)S(1)}, f32[32,512]{1,0:T(8,128)S(1)}, u32[]{:S(2)}, u32[]{:S(2)}) collective-permute-start(f32[32,512]{1,0:T(8,128)S(1)} %shard_map.100), channel_id=1, source_target_pairs={{4,8},{5,9},{6,10},{7,11},{20,24},{21,25},{22,26},{23,27},{36,40},... | collective-permute-start | bytes 196616 | tf_op jit(solution)/shard_map/ppermute | solution.py:334
  66.6 0.7 collective-permute-start.8
  123.8 1.7 %copy-start = (f32[128,4608]{1,0:T(8,128)S(1)}, f32[128,4608]{1,0:T(8,128)}, u32[]{:S(2)}) copy-start(f32[128,4608]{1,0:T(8,128)} %all-gather.7.cloned.1.call-done) | copy-start | bytes 7077892
  128.5 0.9 copy-start.6
  140.2 12.2 %copy-start.8 = (f32[1,1,512,512]{3,2,1,0:T(8,128)S(1)}, f32[1,1,512,512]{3,2,1,0:T(8,128)}, u32[]{:S(2)}) copy-start(f32[1,1,512,512]{3,2,1,0:T(8,128)} %param.9) | copy-start | bytes 3145732
  140.2 0.8 collective-permute-start.9
  141.2 9.5 %collective-permute-start.10 = (f32[32,512]{1,0:T(8,128)S(1)}, f32[32,512]{1,0:T(8,128)S(1)}, u32[]{:S(2)}, u32[]{:S(2)}) collective-permute-start(f32[32,512]{1,0:T(8,128)S(1)} %shard_map.109), channel_id=1, source_target_pairs={{8,4},{9,5},{10,6},{11,7},{24,20},{25,21},{26,22},{27,23},{40,36},... | collective-permute-start | bytes 196616 | tf_op jit(solution)/shard_map/ppermute | solution.py:334
  151.1 4.6 %collective-permute-start.11 = (f32[32,512]{1,0:T(8,128)S(1)}, f32[32,512]{1,0:T(8,128)S(1)}, u32[]{:S(2)}, u32[]{:S(2)}) collective-permute-start(f32[32,512]{1,0:T(8,128)S(1)} %shard_map.110), channel_id=1, source_target_pairs={{4,0},{5,1},{6,2},{7,3},{20,16},{21,17},{22,18},{23,19},{36,32},{3... | collective-permute-start | bytes 196616 | tf_op jit(solution)/shard_map/ppermute | solution.py:334
Sparse Core Ops, SparseCore 0:
  11.3 45.3 all-gather.4
  66.3 43.1 all-gather.6
